TPU v7x, 512 devices: a whole 4x8x8 slice. The times are simulated.
512 devices in a mesh: region: 32 (over x, z), line: 16 (over y, core).
Axes of the slice: x: 4, y: 8, z: 8, core: 2. Of those that a mesh axis runs over, the one named last changes fastest.
Arguments:
- modes_now: float32 [192, 1024, 1024], P('region', 'line'), may hold values from -50 to 50
- modes_prev: float32 [192, 1024, 1024], P('region', 'line'), may hold values from -50 to 50
- extents: int32 [192, 2], replicated, may hold values from 24 to 32, as said below
- partner: int32 [192], replicated, may hold values from 0 to 191, as said below
- offset: int32 [192], replicated, may hold values from -8 to 8
Outputs:
- modes_next: float32 [192, 1024, 1024], P('region', 'line')
Inputs may be any that keep to these rules, and one draw needn't show every extreme that they name: `extents`: each row holds the live cells of one rectangle along y, then along z; both are reached by some rectangle in every draw. Every rectangle is the upper partner of exactly one rectangle. Rectangle r is held at region index r // 6; its upper partner is held at the same index or at one next to it (cyclically), and in every draw some partner is held at another index.
All inputs are finite; a program needn't handle non-finite values.
Results may differ from a plain program's by a relative error of at most 0.0003.
Values sent between devices are 32-bit elements; how exact they have to be, the bound alone decides.
No kernel may reach another device: no remote copies, remote signals or barrier semaphores. Data moves between devices by JAX's collectives and lax.ppermute only.
A program may use at most 64 MiB of HBM per device.

v0:
```python
import math

import jax
import jax.numpy as jnp
from jax import lax
from jax.experimental import pallas as pl
from jax.experimental.pallas import tpu as pltpu
from jax.sharding import PartitionSpec as P

SIDE = 32
PAIRS = 3
OWN = 6
LANES = 128
A1, A2, A3 = 1.5, -0.15, 1.0 / 90.0
VMEM_LIMIT = 48 * 1024 * 1024

SERIES = [2.0 * (-1.0) ** k / math.factorial(2 * k + 2) for k in range(10)]


def series(u):
    total = jnp.full_like(u, SERIES[-1])
    for coefficient in SERIES[-2::-1]:
        total = total * u + coefficient
    return total


def cosine_entry(freq, cell, live):
    turn = 4.0 * live
    steps = freq * (2.0 * cell + 1.0)
    steps = steps - turn * jnp.floor((steps + 0.5) / turn)
    steps = jnp.minimum(steps, turn - steps)
    flip = steps > live
    steps = jnp.where(flip, 2.0 * live - steps, steps)
    angle = (0.5 * math.pi) * (steps / live)
    u = angle * angle
    value = 1.0 - 0.5 * u * series(u)
    value = jnp.where(flip, -value, value)
    weight = jnp.sqrt(jnp.where(freq == 0.0, 1.0, 2.0) / live)
    return jnp.where((freq < live) & (cell < live), weight * value, 0.0)


def z_table(live_z, to_cells):
    shape = (2 * SIDE, 6 * SIDE)
    row = lax.broadcasted_iota(jnp.int32, shape, 0)
    column = lax.broadcasted_iota(jnp.int32, shape, 1)
    same = (row // SIDE) == ((column // SIDE) % 2)
    row_f = (row % SIDE).astype(jnp.float32)
    column_f = (column % SIDE).astype(jnp.float32)
    freq, cell = (column_f, row_f) if to_cells else (row_f, column_f)
    table = jnp.where(same, cosine_entry(freq, cell, jnp.full(shape, live_z, jnp.float32)), 0.0)
    high = table.astype(jnp.bfloat16).astype(jnp.float32)
    return jnp.where(column < 4 * SIDE, high, table - high).astype(jnp.bfloat16)


def z_apply(table, values):
    high = values.astype(jnp.bfloat16)
    low = (values - high.astype(jnp.float32)).astype(jnp.bfloat16)
    stacked = jnp.concatenate([high, low, high], axis=0)
    return jnp.dot(table, stacked, preferred_element_type=jnp.float32)


def live(extents, rect, which):
    return extents[2 * rect + which].astype(jnp.float32)


def left_half(shape):
    return lax.broadcasted_iota(jnp.int32, shape, len(shape) - 1) < LANES // 2


def encode_kernel(extents, now, out):
    pair = pl.program_id(0)
    first = lax.axis_index("region") * OWN + pair
    left = left_half((2 * SIDE, LANES))
    tables = [z_table(live(extents, first + PAIRS * h, 1), True) for h in range(2)]
    for chunk in range(4):
        lanes = slice(chunk * 256, chunk * 256 + 256)
        one, two = (z_apply(tables[h], now[h, 0, :, lanes]) for h in range(2))
        for part in range(2):
            a = one[:, part * LANES : (part + 1) * LANES]
            b = two[:, part * LANES : (part + 1) * LANES]
            chip = 2 * chunk + part
            out[2 * chip, 0] = jnp.where(left, a, pltpu.roll(b, 64, 1))
            out[2 * chip + 1, 0] = jnp.where(left, pltpu.roll(a, 64, 1), b)


def rows_kernel(extents, modes, rows, tables):
    region = lax.axis_index("region")
    left = left_half((3 * SIDE, LANES))
    index = lax.broadcasted_iota(jnp.int32, (3 * SIDE, LANES), 0)
    freq = (index % SIDE).astype(jnp.float32)
    cell = (index // SIDE).astype(jnp.float32)
    for pair in range(PAIRS):
        first = region * OWN + pair
        live_y = jnp.where(left, live(extents, first, 0), live(extents, first + PAIRS, 0))
        tables[pair] = cosine_entry(freq, cell, live_y)
    for pair in range(PAIRS):
        even, odd = [None] * 3, [None] * 3
        for source in range(16):
            for which, total in ((0, even), (1, odd)):
                block = modes[source, pair, which * SIDE : (which + 1) * SIDE]
                for e in range(3):
                    at = e * SIDE + 2 * source + which
                    term = tables[pair, at : at + 1] * block
                    total[e] = term if total[e] is None else total[e] + term
        for e in range(3):
            rows[pair, e] = even[e] + odd[e]
            rows[pair, 3 + e] = even[e] - odd[e]


def spread(d):
    return [A1 * d[0] + A2 * d[1] + A3 * d[2], A2 * d[0] + A3 * d[1], A3 * d[0]]


def force_kernel(extents, partner, offset, own, up, down, tables, out, near):
    region = lax.axis_index("region")
    count = lax.axis_size("region")
    first = region * OWN
    total = count * OWN
    for pair in range(PAIRS):
        near[pair] = down[pair]
        near[PAIRS + pair] = own[pair]
        near[2 * PAIRS + pair] = up[pair]
    lower_of = [jnp.int32(0)] * OWN
    for w in range(3 * OWN):
        rect = lax.rem(first + total + w - OWN, total)
        target = partner[rect] - first
        for r in range(OWN):
            lower_of[r] = jnp.where(target == r, rect, lower_of[r])
    z = lax.broadcasted_iota(jnp.int32, (SIDE, LANES), 0)
    left = left_half((SIDE, LANES))
    left3 = left_half((3, SIDE, LANES))

    def fetch(rect, row, shift, half):
        place = lax.div(rect, OWN)
        slot = rect - place * OWN
        side = lax.div(slot, PAIRS)
        at = lax.rem(place - region + 1 + count, count) * PAIRS + slot - side * PAIRS
        cells = near[at, row : row + 3]
        cells = pltpu.roll(cells, lax.rem(shift + SIDE, SIDE), 1)
        return jnp.where(side == half, cells, pltpu.roll(cells, LANES // 2, 2))

    for pair in range(PAIRS):
        taken = {}
        for name in ("upper", "lower"):
            pieces, masks = [], []
            for half in range(2):
                r = pair + PAIRS * half
                rect = first + r
                if name == "upper":
                    other = partner[rect]
                    shift = offset[rect]
                    pieces.append(fetch(other, 0, shift, half))
                else:
                    other = lower_of[r]
                    shift = -offset[other]
                    pieces.append(fetch(other, 3, shift, half))
                source = z - shift
                masks.append(
                    jnp.where(
                        (source >= 0)
                        & (source < extents[2 * other + 1])
                        & (z < extents[2 * rect + 1]),
                        1.0,
                        0.0,
                    )
                )
            mask = jnp.where(left, masks[0], masks[1])
            both = jnp.where(left3, pieces[0], pieces[1])
            base = 3 if name == "upper" else 0
            taken[name] = spread([mask * (both[e] - own[pair, base + e]) for e in range(3)])
        even = [taken["lower"][e] + taken["upper"][e] for e in range(3)]
        odd = [taken["lower"][e] - taken["upper"][e] for e in range(3)]
        for source in range(16):
            for which, parts in ((0, even), (1, odd)):
                value = None
                for e in range(3):
                    at = e * SIDE + 2 * source + which
                    term = tables[pair, at : at + 1] * parts[e]
                    value = term if value is None else value + term
                out[source, pair, which * SIDE : (which + 1) * SIDE] = value


def update_kernel(extents, mixed, now, previous, out):
    pair = pl.program_id(0)
    first = lax.axis_index("region") * OWN + pair
    line = lax.axis_index("line")
    left = left_half((2 * SIDE, LANES))
    row = lax.broadcasted_iota(jnp.int32, (2 * SIDE, 256), 0)
    freq_y = (2 * line + row // SIDE).astype(jnp.float32)
    freq_z = (row % SIDE).astype(jnp.float32)
    column = lax.broadcasted_iota(jnp.int32, (1, 256), 1)
    quarter = (0.5 * math.pi) ** 2
    tables, bases, actives = [], [], []
    for h in range(2):
        live_y = live(extents, first + PAIRS * h, 0)
        live_z = live(extents, first + PAIRS * h, 1)
        tables.append(z_table(live_z, False))
        y = freq_y / live_y
        z = freq_z / live_z
        bases.append(quarter * (y * y + z * z))
        actives.append((freq_y < live_y) & (freq_z < live_z))
    for chunk in range(4):
        lanes = slice(chunk * 256, chunk * 256 + 256)
        ones, twos = [], []
        for part in range(2):
            chip = 2 * chunk + part
            a = mixed[2 * chip, 0]
            b = mixed[2 * chip + 1, 0]
            ones.append(jnp.where(left, a, pltpu.roll(b, 64, 1)))
            twos.append(jnp.where(left, pltpu.roll(a, 64, 1), b))
        x = (column + chunk * 256).astype(jnp.float32) * (1.0 / 1024.0)
        along = quarter * (x * x)
        for h, pieces in ((0, ones), (1, twos)):
            spectral = z_apply(tables[h], jnp.concatenate(pieces, axis=1))
            u = bases[h] + along
            s = series(u)
            current = now[h, 0, :, lanes]
            stepped = (2.0 - u * s) * current - previous[h, 0, :, lanes] + 0.25 * s * spectral
            out[h, 0, :, lanes] = jnp.where(actives[h], stepped, 0.0)


def smem():
    return pl.BlockSpec(memory_space=pltpu.SMEM)


def vmem():
    return pl.BlockSpec(memory_space=pltpu.VMEM)


def shards(modes_now, modes_prev, extents, partner, offset):
    f32 = jnp.float32
    extents = extents.reshape(-1)
    now = modes_now.reshape(2, PAIRS, 2 * SIDE, 1024)
    previous = modes_prev.reshape(2, PAIRS, 2 * SIDE, 1024)
    wide = pl.BlockSpec((2, 1, 2 * SIDE, 1024), lambda i: (0, i, 0, 0))
    packed = pl.BlockSpec((16, 1, 2 * SIDE, LANES), lambda i: (0, i, 0, 0))
    packed_shape = jax.ShapeDtypeStruct((16, PAIRS, 2 * SIDE, LANES), f32)
    rows_shape = jax.ShapeDtypeStruct((PAIRS, 6, SIDE, LANES), f32)
    params = pltpu.CompilerParams(vmem_limit_bytes=VMEM_LIMIT)

    with jax.named_scope("encode"):
        sent = pl.pallas_call(
            encode_kernel,
            grid=(PAIRS,),
            out_shape=packed_shape,
            in_specs=[smem(), wide],
            out_specs=packed,
            compiler_params=params,
        )(extents, now)
    held = lax.all_to_all(sent, "line", 0, 0, tiled=True)
    with jax.named_scope("rows"):
        rows, tables = pl.pallas_call(
            rows_kernel,
            out_shape=(rows_shape, jax.ShapeDtypeStruct((PAIRS, 3 * SIDE, LANES), f32)),
            in_specs=[smem(), vmem()],
            out_specs=(vmem(), vmem()),
            compiler_params=params,
        )(extents, held)
    count = lax.axis_size("region")
    up = lax.ppermute(rows, "region", [((i + 1) % count, i) for i in range(count)])
    down = lax.ppermute(rows, "region", [(i, (i + 1) % count) for i in range(count)])
    with jax.named_scope("force"):
        forced = pl.pallas_call(
            force_kernel,
            out_shape=packed_shape,
            in_specs=[smem(), smem(), smem()] + [vmem()] * 4,
            out_specs=vmem(),
            scratch_shapes=[pltpu.VMEM((3 * PAIRS, 6, SIDE, LANES), f32)],
            compiler_params=params,
        )(extents, partner, offset, rows, up, down, tables)
    mixed = lax.all_to_all(forced, "line", 0, 0, tiled=True)
    with jax.named_scope("update"):
        result = pl.pallas_call(
            update_kernel,
            grid=(PAIRS,),
            out_shape=jax.ShapeDtypeStruct(now.shape, f32),
            in_specs=[smem(), packed, wide, wide],
            out_specs=wide,
            compiler_params=params,
        )(extents, mixed, now, previous)
    return result.reshape(modes_now.shape)


def solution(mesh):
    return jax.shard_map(
        shards,
        mesh=mesh,
        in_specs=(P("region", "line", None), P("region", "line", None), P(), P(), P()),
        out_specs=P("region", "line", None),
        check_vma=False,
    )
```

profile of v0, /device:TPU:1, one launch (start us, length us, event | category | flops | bytes accessed | tf_op | source)
XLA Modules:
  0.0 124.2 jit_solution(17430827570232700065)
XLA Ops:
  0.0 0.8 copy.6
  0.8 0.1 reshape.12.extents
  0.9 0.0 copy-start
  1.0 1.4 %copy-done = f32[6,64,1024]{2,1,0:T(8,128)S(1)} copy-done((f32[6,64,1024]{2,1,0:T(8,128)S(1)}, f32[6,64,1024]{2,1,0:T(8,128)}, u32[]{:S(2)}) %copy-start) | copy-done | bytes 1572888
  2.4 2.4 %encode.1 = f32[16,3,64,128]{3,2,1,0:T(8,128)S(1)} custom-call(s32[384]{0:T(512)S(1)} %reshape.12.extents, f32[2,3,64,1024]{3,2,1,0:T(8,128)S(1)} %bitcast.3), custom_call_target="tpu_custom_call" | custom-call | tf_op jit(solution)/shard_map/encode/pallas_call | solution.py:242
  4.7 49.1 %all_to_all.10.modes = f32[16,3,64,128]{3,2,1,0:T(8,128)S(1)} all-to-all(f32[16,3,64,128]{3,2,1,0:T(8,128)S(1)} %encode.1), channel_id=1, replica_groups=mesh['region'=32,'line'=16] {'line'}, dimensions={0} | all-to-all | bytes 3145728 | tf_op jit(solution)/shard_map/all_to_all | solution.py:250
  53.9 0.0 copy-start.3
  53.9 0.0 copy-start.4
  53.9 1.2 rows.1
  55.1 3.1 %collective-permute-start.1 = (f32[3,6,32,128]{3,2,1,0:T(8,128)S(1)}, f32[3,6,32,128]{3,2,1,0:T(8,128)S(1)}, u32[]{:S(2)}, u32[]{:S(2)}) collective-permute-start(f32[3,6,32,128]{3,2,1,0:T(8,128)S(1)} %get-tuple-element.7.own), channel_id=1, source_target_pairs={{0,16},{16,32},{32,48},{48,64},{64,80},{80,96},{96,112},{112,128},... | collective-permute-start | bytes 884744 | tf_op jit(solution)/shard_map/ppermute | solution.py:261
  58.2 10.8 %collective-permute-start = (f32[3,6,32,128]{3,2,1,0:T(8,128)S(1)}, f32[3,6,32,128]{3,2,1,0:T(8,128)S(1)}, u32[]{:S(2)}, u32[]{:S(2)}) collective-permute-start(f32[3,6,32,128]{3,2,1,0:T(8,128)S(1)} %get-tuple-element.7.own), channel_id=1, source_target_pairs={{16,0},{32,16},{48,32},{64,48},{80,64},{96,80},{112,96},{128,112},... | collective-permute-start | bytes 884744 | tf_op jit(solution)/shard_map/ppermute | solution.py:260
  68.9 4.3 %collective-permute-done.1.down = f32[3,6,32,128]{3,2,1,0:T(8,128)S(1)} collective-permute-done((f32[3,6,32,128]{3,2,1,0:T(8,128)S(1)}, f32[3,6,32,128]{3,2,1,0:T(8,128)S(1)}, u32[]{:S(2)}, u32[]{:S(2)}) %collective-permute-start.1) | collective-permute-done | bytes 294944 | tf_op jit(solution)/shard_map/ppermute | solution.py:261
  73.3 1.8 %collective-permute-done.up = f32[3,6,32,128]{3,2,1,0:T(8,128)S(1)} collective-permute-done((f32[3,6,32,128]{3,2,1,0:T(8,128)S(1)}, f32[3,6,32,128]{3,2,1,0:T(8,128)S(1)}, u32[]{:S(2)}, u32[]{:S(2)}) %collective-permute-start) | collective-permute-done | bytes 294944 | tf_op jit(solution)/shard_map/ppermute | solution.py:260
  75.0 0.0 copy-done.3
  75.0 0.0 copy-done.4
  75.0 1.5 %force.1 = f32[16,3,64,128]{3,2,1,0:T(8,128)S(1)} custom-call(s32[384]{0:T(512)S(1)} %reshape.12.extents, s32[192]{0:T(256)S(1)} %copy-done.3, s32[192]{0:T(256)S(1)} %copy-done.4, f32[3,6,32,128]{3,2,1,0:T(8,128)S(1)} %get-tuple-element.7.own, f32[3,6,32,128]{3,2,1,0:T(8,128)S(1)} %collective-permute-done.up, ...), custom_call_target="tpu_custom_call" | custom-call | tf_op jit(solution)/shard_map/force/pallas_call | solution.py:263
  76.5 0.0 copy-start.1
  76.5 0.0 copy-start.2
  76.5 43.5 %all_to_all.11.mixed = f32[16,3,64,128]{3,2,1,0:T(8,128)S(1)} all-to-all(f32[16,3,64,128]{3,2,1,0:T(8,128)S(1)} %force.1), channel_id=1, replica_groups=mesh['region'=32,'line'=16] {'line'}, dimensions={0} | all-to-all | bytes 3145728 | tf_op jit(solution)/shard_map/all_to_all | solution.py:271
  120.0 0.0 copy-done.1
  120.0 0.0 copy-done.2
  120.0 4.2 %update.1 = f32[2,3,64,1024]{3,2,1,0:T(8,128)} custom-call(s32[384]{0:T(512)S(1)} %reshape.12.extents, f32[16,3,64,128]{3,2,1,0:T(8,128)S(1)} %all_to_all.11.mixed, f32[2,3,64,1024]{3,2,1,0:T(8,128)S(1)} %bitcast.4, f32[2,3,64,1024]{3,2,1,0:T(8,128)S(1)} %bitcast.5), custom_call_target="tpu_custom_call" | custom-call | tf_op jit(solution)/shard_map/update/pallas_call | solution.py:273
Async XLA Ops:
  0.9 1.4 %copy-start = (f32[6,64,1024]{2,1,0:T(8,128)S(1)}, f32[6,64,1024]{2,1,0:T(8,128)}, u32[]{:S(2)}) copy-start(f32[6,64,1024]{2,1,0:T(8,128)} %param.5) | copy-start | bytes 4718596
  53.9 21.1 %copy-start.3 = (s32[192]{0:T(256)S(1)}, s32[192]{0:T(256)}, u32[]{:S(2)}) copy-start(s32[192]{0:T(256)} %partner.1) | copy-start | bytes 2308
  53.9 21.1 %copy-start.4 = (s32[192]{0:T(256)S(1)}, s32[192]{0:T(256)}, u32[]{:S(2)}) copy-start(s32[192]{0:T(256)} %offset.1) | copy-start | bytes 2308
  55.1 18.2 %collective-permute-start.1 = (f32[3,6,32,128]{3,2,1,0:T(8,128)S(1)}, f32[3,6,32,128]{3,2,1,0:T(8,128)S(1)}, u32[]{:S(2)}, u32[]{:S(2)}) collective-permute-start(f32[3,6,32,128]{3,2,1,0:T(8,128)S(1)} %get-tuple-element.7.own), channel_id=1, source_target_pairs={{0,16},{16,32},{32,48},{48,64},{64,80},{80,96},{96,112},{112,128},... | collective-permute-start | bytes 884744 | tf_op jit(solution)/shard_map/ppermute | solution.py:261
  58.2 16.9 %collective-permute-start = (f32[3,6,32,128]{3,2,1,0:T(8,128)S(1)}, f32[3,6,32,128]{3,2,1,0:T(8,128)S(1)}, u32[]{:S(2)}, u32[]{:S(2)}) collective-permute-start(f32[3,6,32,128]{3,2,1,0:T(8,128)S(1)} %get-tuple-element.7.own), channel_id=1, source_target_pairs={{16,0},{32,16},{48,32},{64,48},{80,64},{96,80},{112,96},{128,112},... | collective-permute-start | bytes 884744 | tf_op jit(solution)/shard_map/ppermute | solution.py:260
  76.5 43.5 %copy-start.1 = (f32[6,64,1024]{2,1,0:T(8,128)S(1)}, f32[6,64,1024]{2,1,0:T(8,128)}, u32[]{:S(2)}) copy-start(f32[6,64,1024]{2,1,0:T(8,128)} %param.5) | copy-start | bytes 4718596
  76.5 43.5 %copy-start.2 = (f32[6,64,1024]{2,1,0:T(8,128)S(1)}, f32[6,64,1024]{2,1,0:T(8,128)}, u32[]{:S(2)}) copy-start(f32[6,64,1024]{2,1,0:T(8,128)} %param.6) | copy-start | bytes 4718596
where the time goes:
time: 124 us
  blocking collectives  92.6 us (75%)
  starting transfers between devices  13.8 us (11%)
  Pallas kernels  9.24 us (7%)
  waiting for transfers between devices  6.07 us (5%)
  local copies, waits for them, and re-layouts  2.36 us (2%)
    all_to_all x1, blocking collectives, shards(): held = lax.all_to_all(sent, 'line', 0, 0, tiled=True)  49.1 us
    all_to_all x1, blocking collectives, shards(): mixed = lax.all_to_all(forced, 'line', 0, 0, tiled=True)  43.5 us
    ppermute x1, starting transfers between devices, shards(): lax.ppermute(rows, 'region', [((i + 1) % count, i) for i in range(count)])  10.8 us
    ppermute x1, waiting for transfers between devices, shards(): lax.ppermute(rows, 'region', [(i, (i + 1) % count) for i in range(count)])  4.31 us
    pallas_call x1, Pallas kernels, shards(): pl.pallas_call(update_kernel, grid=(PAIRS,), out_shape=jax.ShapeDtypeStru...  4.21 us
    ppermute x1, starting transfers between devices, shards(): lax.ppermute(rows, 'region', [(i, (i + 1) % count) for i in range(count)])  3.06 us
  transfers between devices with their start and end apart: 2, of which 2 were waited for; matrix products, arithmetic and copies ran while one was open for 0% of the time, Pallas kernels for 0%

commit v1 on v0

v1 whole, which is shorter than its diff:
```python
import math

import jax
import jax.numpy as jnp
from jax import lax
from jax.experimental import pallas as pl
from jax.experimental.pallas import tpu as pltpu
from jax.sharding import PartitionSpec as P

SIDE = 32
PAIRS = 3
OWN = 6
LANES = 128
A1, A2, A3 = 1.5, -0.15, 1.0 / 90.0
VMEM_LIMIT = 16 * 1024 * 1024
ENCODE_LIMIT = 63 * 1024 * 1024

SERIES = [2.0 * (-1.0) ** k / math.factorial(2 * k + 2) for k in range(10)]


def series(u, terms):
    total = jnp.full_like(u, SERIES[terms - 1])
    for coefficient in SERIES[: terms - 1][::-1]:
        total = total * u + coefficient
    return total


def cosine_entry(freq, cell, live):
    inverse = 1.0 / live
    turn = 4.0 * live
    steps = freq * (2.0 * cell + 1.0)
    steps = steps - turn * jnp.floor((steps + 0.5) * (0.25 * inverse))
    steps = jnp.minimum(steps, turn - steps)
    flip = steps > live
    steps = jnp.where(flip, 2.0 * live - steps, steps)
    angle = (0.5 * math.pi) * (steps * inverse)
    u = angle * angle
    value = 1.0 - 0.5 * u * series(u, 7)
    value = jnp.where(flip, -value, value)
    weight = jnp.sqrt(jnp.where(freq == 0.0, 1.0, 2.0) * inverse)
    return jnp.where((freq < live) & (cell < live), weight * value, 0.0)


def z_table(live_z, to_cells):
    shape = (SIDE, LANES)
    row = lax.broadcasted_iota(jnp.int32, shape, 0).astype(jnp.float32)
    lane = lax.broadcasted_iota(jnp.int32, shape, 1)
    column = (lane % SIDE).astype(jnp.float32)
    freq, cell = (column, row) if to_cells else (row, column)
    table = cosine_entry(freq, cell, jnp.full(shape, live_z, jnp.float32))
    high = table.astype(jnp.bfloat16).astype(jnp.float32)
    return jnp.where(lane < LANES // 2, high, table - high).astype(jnp.bfloat16)


def z_apply(table, parts):
    values = jnp.concatenate(parts, axis=1)
    high = values.astype(jnp.bfloat16)
    low = (values - high.astype(jnp.float32)).astype(jnp.bfloat16)
    stacked = jnp.concatenate([high, low, high, low], axis=0)
    both = jnp.dot(table, stacked, preferred_element_type=jnp.float32)
    left = left_half((SIDE, LANES))
    return [
        jnp.where(
            left,
            both[:SIDE, i * LANES : (i + 1) * LANES],
            both[SIDE:, i * LANES : (i + 1) * LANES],
        )
        for i in range(len(parts))
    ]


def live(extents, rect, which):
    return extents[which, rect].astype(jnp.float32)


def left_half(shape):
    return lax.broadcasted_iota(jnp.int32, shape, len(shape) - 1) < LANES // 2


def encode_kernel(now, out, held, made, arrived, sent):
    left = left_half((2 * SIDE, LANES))
    inward = [
        pltpu.make_async_copy(now.at[:, i], held.at[i], arrived.at[i]) for i in range(PAIRS)
    ]
    outward = [
        pltpu.make_async_copy(made.at[i], out.at[:, i], sent.at[i]) for i in range(PAIRS)
    ]
    for copy in inward:
        copy.start()
    for pair in range(PAIRS):
        inward[pair].wait()
        for chip in range(8):
            lanes = slice(chip * LANES, chip * LANES + LANES)
            a = held[pair, 0, :, lanes]
            b = held[pair, 1, :, lanes]
            made[pair, 2 * chip] = jnp.where(left, a, pltpu.roll(b, LANES // 2, 1))
            made[pair, 2 * chip + 1] = jnp.where(left, pltpu.roll(a, LANES // 2, 1), b)
        outward[pair].start()
    for copy in outward:
        copy.wait()


def plan_kernel(extents, partner, offset, y_tables, to_cells, to_modes, masks, places):
    region = lax.axis_index("region")
    count = lax.axis_size("region")
    first = region * OWN
    total = count * OWN
    left = left_half((3 * SIDE, LANES))
    index = lax.broadcasted_iota(jnp.int32, (3 * SIDE, LANES), 0)
    freq = (index % SIDE).astype(jnp.float32)
    cell = (index // SIDE).astype(jnp.float32)
    for pair in range(PAIRS):
        one, two = first + pair, first + pair + PAIRS
        live_y = jnp.where(left, live(extents, one, 0), live(extents, two, 0))
        y_tables[pair] = cosine_entry(freq, cell, live_y)
        for h, rect in ((0, one), (1, two)):
            live_z = live(extents, rect, 1)
            to_cells[pair, h * SIDE : (h + 1) * SIDE] = z_table(live_z, True)
            to_modes[pair, h * SIDE : (h + 1) * SIDE] = z_table(live_z, False)
    lower_of = [jnp.int32(0)] * OWN
    for w in range(3 * OWN):
        rect = lax.rem(first + total + w - OWN, total)
        target = partner[rect] - first
        for r in range(OWN):
            lower_of[r] = jnp.where(target == r, rect, lower_of[r])
    z = lax.broadcasted_iota(jnp.int32, (SIDE, LANES), 0)
    left = left_half((SIDE, LANES))
    for pair in range(PAIRS):
        for face in range(2):
            parts = []
            for half in range(2):
                r = pair + PAIRS * half
                rect = first + r
                if face == 1:
                    other = partner[rect]
                    shift = offset[rect]
                else:
                    other = lower_of[r]
                    shift = -offset[other]
                place = lax.div(other, OWN)
                slot = other - place * OWN
                side = lax.div(slot, PAIRS)
                at = 3 * ((pair * 2 + face) * 2 + half)
                places[at] = lax.rem(place - region + 1 + count, count) * PAIRS + slot - side * PAIRS
                places[at + 1] = lax.rem(shift + SIDE, SIDE)
                places[at + 2] = side
                source = z - shift
                inside = (source >= 0) & (source < extents[1, other]) & (z < extents[1, rect])
                parts.append(jnp.where(inside, 1.0, 0.0))
            masks[pair, face] = jnp.where(left, parts[0], parts[1])


def free_kernel(extents, now, previous, base, gain):
    first = lax.axis_index("region") * OWN
    line = lax.axis_index("line")
    row = lax.broadcasted_iota(jnp.int32, (2 * SIDE, 256), 0)
    freq_y = (2 * line + row // SIDE).astype(jnp.float32)
    freq_z = (row % SIDE).astype(jnp.float32)
    column = lax.broadcasted_iota(jnp.int32, (1, 256), 1)
    quarter = (0.5 * math.pi) ** 2
    for r in range(OWN):
        h, pair = r // PAIRS, r % PAIRS
        live_y = live(extents, first + r, 0)
        live_z = live(extents, first + r, 1)
        y = freq_y / live_y
        z = freq_z / live_z
        across = quarter * (y * y + z * z)
        active = (freq_y < live_y) & (freq_z < live_z)
        for chunk in range(4):
            lanes = slice(chunk * 256, chunk * 256 + 256)
            x = (column + chunk * 256).astype(jnp.float32) * (1.0 / 1024.0)
            u = across + quarter * (x * x)
            s = series(u, 9)
            stepped = (2.0 - u * s) * now[h, pair, :, lanes] - previous[h, pair, :, lanes]
            base[h, pair, :, lanes] = jnp.where(active, stepped, 0.0)
            gain[h, pair, :, lanes] = jnp.where(active, 0.25 * s, 0.0)


def rows_kernel(tables, to_cells, modes, rows):
    for pair in range(PAIRS):
        even, odd = [None] * 3, [None] * 3
        for source in range(16):
            for which, total in ((0, even), (1, odd)):
                block = modes[source, pair, which * SIDE : (which + 1) * SIDE]
                for e in range(3):
                    at = e * SIDE + 2 * source + which
                    term = tables[pair, at : at + 1] * block
                    total[e] = term if total[e] is None else total[e] + term
        lower = [even[e] + odd[e] for e in range(3)]
        upper = [even[e] - odd[e] for e in range(3)]
        for i, cells in enumerate(z_apply(to_cells[pair], lower + upper)):
            rows[pair, i] = cells


def spread(d):
    return [A1 * d[0] + A2 * d[1] + A3 * d[2], A2 * d[0] + A3 * d[1], A3 * d[0]]


def force_kernel(places, tables, to_modes, masks, own, up, down, out, near, made, sent):
    copies = []
    for pair in range(PAIRS):
        near[pair] = down[pair]
        near[PAIRS + pair] = own[pair]
        near[2 * PAIRS + pair] = up[pair]
    left = left_half((3, SIDE, LANES))
    for pair in range(PAIRS):
        taken = []
        for face in range(2):
            pieces = []
            for half in range(2):
                at = 3 * ((pair * 2 + face) * 2 + half)
                row = 0 if face == 1 else 3
                cells = near[places[at], row : row + 3]
                cells = pltpu.roll(cells, places[at + 1], 1)
                pieces.append(
                    jnp.where(places[at + 2] == half, cells, pltpu.roll(cells, LANES // 2, 2))
                )
            both = jnp.where(left, pieces[0], pieces[1])
            mask = masks[pair, face]
            taken.append(spread([mask * (both[e] - own[pair, 3 * face + e]) for e in range(3)]))
        even = [taken[0][e] + taken[1][e] for e in range(3)]
        odd = [taken[0][e] - taken[1][e] for e in range(3)]
        sixfold = z_apply(to_modes[pair], even + odd)
        for target in range(16):
            for which, parts in ((0, sixfold[:3]), (1, sixfold[3:])):
                value = None
                for e in range(3):
                    at = e * SIDE + 2 * target + which
                    term = tables[pair, at : at + 1] * parts[e]
                    value = term if value is None else value + term
                made[pair, target, which * SIDE : (which + 1) * SIDE] = value
        copies.append(pltpu.make_async_copy(made.at[pair], out.at[:, pair], sent.at[pair]))
        copies[-1].start()
    for copy in copies:
        copy.wait()


def update_kernel(mixed, base, gain, out, made, sent):
    left = left_half((2 * SIDE, LANES))
    copies = []
    for pair in range(PAIRS):
        for chip in range(8):
            lanes = slice(chip * LANES, chip * LANES + LANES)
            a = mixed[2 * chip, pair]
            b = mixed[2 * chip + 1, pair]
            one = jnp.where(left, a, pltpu.roll(b, LANES // 2, 1))
            two = jnp.where(left, pltpu.roll(a, LANES // 2, 1), b)
            for h, spectral in ((0, one), (1, two)):
                made[pair, h, :, lanes] = base[h, pair, :, lanes] + gain[h, pair, :, lanes] * spectral
        copies.append(pltpu.make_async_copy(made.at[pair], out.at[:, pair], sent.at[pair]))
        copies[-1].start()
    for copy in copies:
        copy.wait()


def smem():
    return pl.BlockSpec(memory_space=pltpu.SMEM)


def vmem():
    return pl.BlockSpec(memory_space=pltpu.VMEM)


def hbm():
    return pl.BlockSpec(memory_space=pltpu.HBM)


def cost(flops, nbytes):
    return pl.CostEstimate(flops=flops, bytes_accessed=nbytes, transcendentals=0)


def shards(modes_now, modes_prev, extents, partner, offset):
    f32 = jnp.float32
    extents = extents.T
    now = modes_now.reshape(2, PAIRS, 2 * SIDE, 1024)
    previous = modes_prev.reshape(2, PAIRS, 2 * SIDE, 1024)
    nbytes = now.size * 4
    wide_shape = jax.ShapeDtypeStruct(now.shape, f32)
    packed_shape = jax.ShapeDtypeStruct((16, PAIRS, 2 * SIDE, LANES), f32)
    rows_shape = jax.ShapeDtypeStruct((PAIRS, 6, SIDE, LANES), f32)
    table_shape = jax.ShapeDtypeStruct((PAIRS, 2 * SIDE, LANES), jnp.bfloat16)
    params = pltpu.CompilerParams(vmem_limit_bytes=VMEM_LIMIT)
    wide_scratch = pltpu.VMEM((PAIRS, 2, 2 * SIDE, 1024), f32)
    packed_scratch = pltpu.VMEM((PAIRS, 16, 2 * SIDE, LANES), f32)
    copied = pltpu.SemaphoreType.DMA((PAIRS,))

    with jax.named_scope("encode"):
        sent = pl.pallas_call(
            encode_kernel,
            out_shape=packed_shape,
            in_specs=[hbm()],
            out_specs=hbm(),
            scratch_shapes=[wide_scratch, packed_scratch, copied, copied],
            compiler_params=pltpu.CompilerParams(vmem_limit_bytes=ENCODE_LIMIT),
            cost_estimate=cost(10**6, 2 * nbytes),
        )(now)
    held = lax.all_to_all(sent, "line", 0, 0, tiled=True)
    with jax.named_scope("plan"):
        y_tables, to_cells, to_modes, masks, places = pl.pallas_call(
            plan_kernel,
            out_shape=(
                jax.ShapeDtypeStruct((PAIRS, 3 * SIDE, LANES), f32),
                table_shape,
                table_shape,
                jax.ShapeDtypeStruct((PAIRS, 2, SIDE, LANES), f32),
                jax.ShapeDtypeStruct((36,), jnp.int32),
            ),
            in_specs=[smem(), smem(), smem()],
            out_specs=(vmem(), vmem(), vmem(), vmem(), smem()),
            compiler_params=params,
            cost_estimate=cost(10**8, 10**6),
        )(extents, partner, offset)
    with jax.named_scope("rows"):
        rows = pl.pallas_call(
            rows_kernel,
            out_shape=rows_shape,
            in_specs=[vmem()] * 3,
            out_specs=vmem(),
            compiler_params=params,
            cost_estimate=cost(10**7, nbytes),
        )(y_tables, to_cells, held)
    count = lax.axis_size("region")
    up = lax.ppermute(rows, "region", [((i + 1) % count, i) for i in range(count)])
    down = lax.ppermute(rows, "region", [(i, (i + 1) % count) for i in range(count)])
    with jax.named_scope("free"):
        base, gain = pl.pallas_call(
            free_kernel,
            out_shape=(wide_shape, wide_shape),
            in_specs=[smem(), vmem(), vmem()],
            out_specs=(vmem(), vmem()),
            compiler_params=params,
            cost_estimate=cost(10**9, 4 * nbytes),
        )(extents, *lax.optimization_barrier((now, previous, rows))[:2])
    up, base, gain = lax.optimization_barrier((up, base, gain))
    with jax.named_scope("force"):
        forced = pl.pallas_call(
            force_kernel,
            out_shape=packed_shape,
            in_specs=[smem()] + [vmem()] * 6,
            out_specs=hbm(),
            scratch_shapes=[pltpu.VMEM((3 * PAIRS, 6, SIDE, LANES), f32), packed_scratch, copied],
            compiler_params=params,
            cost_estimate=cost(10**7, nbytes),
        )(places, y_tables, to_modes, masks, rows, up, down)
    mixed = lax.all_to_all(forced, "line", 0, 0, tiled=True)
    with jax.named_scope("update"):
        result = pl.pallas_call(
            update_kernel,
            out_shape=wide_shape,
            in_specs=[vmem()] * 3,
            out_specs=hbm(),
            scratch_shapes=[wide_scratch, copied],
            compiler_params=params,
            cost_estimate=cost(10**7, 4 * nbytes),
        )(mixed, base, gain)
    return result.reshape(modes_now.shape)


def solution(mesh):
    return jax.shard_map(
        shards,
        mesh=mesh,
        in_specs=(P("region", "line", None), P("region", "line", None), P(), P(), P()),
        out_specs=P("region", "line", None),
        check_vma=False,
    )
```

time: 124 us -> 125 us (level)
  blocking collectives: 92.6 us -> 44.1 us
  waiting for transfers between devices: 6.07 us -> 45.1 us
  starting transfers between devices: 13.8 us -> 23.5 us
    all_to_all x1 -> x0, blocking collectives: 49.1 us -> none  [shards(): held = lax.all_to_all(sent, 'line', 0, 0, tiled=True)]
    all_to_all x0 -> x1, waiting for transfers between devices: none -> 36.5 us  [shards(): held = lax.all_to_all(sent, 'line', 0, 0, tiled=True)]
    all_to_all x0 -> x1, starting transfers between devices: none -> 10.5 us  [shards(): held = lax.all_to_all(sent, 'line', 0, 0, tiled=True)]
    ppermute x1, waiting for transfers between devices: 4.31 us -> 7.17 us  [shards(): lax.ppermute(rows, 'region', [(i, (i + 1) % count) for i in range(count)])]
    pallas_call x4 -> x6, Pallas kernels: 9.24 us -> 10.4 us  [the longest x1 2.5 us: shards(): pl.pallas_call(encode_kernel, out_shape=packed_shape, in_specs=[hbm()], o...]
  transfers between devices with their start and end apart: 2 -> 3, of which waited for: 2 -> 3; matrix products, arithmetic and copies ran while one was open for 0% -> 0% of each run, Pallas kernels for 0% -> 3%
where the time goes in v1:
time: 125 us
  waiting for transfers between devices  45.1 us (36%)
  blocking collectives  44.1 us (35%)
  starting transfers between devices  23.5 us (19%)
  Pallas kernels  10.4 us (8%)
  local copies, waits for them, and re-layouts  1.43 us (1%)
    all_to_all x1, blocking collectives, shards(): mixed = lax.all_to_all(forced, 'line', 0, 0, tiled=True)  44.1 us
    all_to_all x1, waiting for transfers between devices, shards(): held = lax.all_to_all(sent, 'line', 0, 0, tiled=True)  36.5 us
    ppermute x1, starting transfers between devices, shards(): lax.ppermute(rows, 'region', [((i + 1) % count, i) for i in range(count)])  11.1 us
    all_to_all x1, starting transfers between devices, shards(): held = lax.all_to_all(sent, 'line', 0, 0, tiled=True)  10.5 us
    ppermute x1, waiting for transfers between devices, shards(): lax.ppermute(rows, 'region', [(i, (i + 1) % count) for i in range(count)])  7.17 us
  transfers between devices with their start and end apart: 3, of which 3 were waited for; matrix products, arithmetic and copies ran while one was open for 0% of the time, Pallas kernels for 3%

profile of v1, /device:TPU:1, one launch (start us, length us, event | category | flops | bytes accessed | tf_op | source)
XLA Modules:
  0.0 124.6 jit_solution(5400256276851845340)
XLA Ops:
  0.0 2.5 %encode.1 = f32[16,3,64,128]{3,2,1,0:T(8,128)} custom-call(f32[2,3,64,1024]{3,2,1,0:T(8,128)} %bitcast.4), custom_call_target="tpu_custom_call" | custom-call | flops 1000000 | bytes 3145728 | tf_op jit(solution)/shard_map/encode/pallas_call | solution.py:288
  2.5 0.0 copy-start.2
  2.5 0.0 copy-start.3
  2.5 0.0 copy-start.4
  2.5 10.5 %all-to-all-start = ((f32[16,3,64,128]{3,2,1,0:T(8,128)}), f32[16,3,64,128]{3,2,1,0:T(8,128)S(1)}, u32[]{:S(2)}, u32[]{:S(2)}) async-start(f32[16,3,64,128]{3,2,1,0:T(8,128)} %encode.1), calls=%async_computation | async-start | bytes 3145728 | tf_op jit(solution)/shard_map/all_to_all | solution.py:297
  13.1 0.0 copy-start
  13.1 0.0 copy-done.2
  13.1 0.0 copy-done.3
  13.1 0.0 copy-done.4
  13.1 1.9 %plan.1 = (f32[3,96,128]{2,1,0:T(8,128)S(1)}, bf16[3,64,128]{2,1,0:T(8,128)(2,1)S(1)}, bf16[3,64,128]{2,1,0:T(8,128)(2,1)S(1)}, f32[3,2,32,128]{3,2,1,0:T(8,128)S(1)}, s32[36]{0:T(128)S(1)}) custom-call(s32[2,192]{1,0:T(2,128)S(1)} %bitcast.7, s32[192]{0:T(256)S(1)} %copy-done.3, s32[192]{0:T(256)S(1)} %copy-done.4), custom_call_target="tpu_custom_call" | custom-call | flops 100000000 | bytes 1000000 | tf_op jit(solution)/shard_map/plan/pallas_call | solution.py:299
  15.0 36.5 %all-to-all-done.modes = f32[16,3,64,128]{3,2,1,0:T(8,128)S(1)} async-done(((f32[16,3,64,128]{3,2,1,0:T(8,128)}), f32[16,3,64,128]{3,2,1,0:T(8,128)S(1)}, u32[]{:S(2)}, u32[]{:S(2)}) %all-to-all-start) | async-done | bytes 1572896 | tf_op jit(solution)/shard_map/all_to_all | solution.py:297
  51.5 0.6 rows.1.own
  52.1 11.1 %collective-permute-start = (f32[3,6,32,128]{3,2,1,0:T(8,128)S(1)}, f32[3,6,32,128]{3,2,1,0:T(8,128)S(1)}, u32[]{:S(2)}, u32[]{:S(2)}) collective-permute-start(f32[3,6,32,128]{3,2,1,0:T(8,128)S(1)} %rows.1.own), channel_id=1, source_target_pairs={{16,0},{32,16},{48,32},{64,48},{80,64},{96,80},{112,96},{128,112},... | collective-permute-start | bytes 884744 | tf_op jit(solution)/shard_map/ppermute | solution.py:323
  63.2 1.9 %collective-permute-start.1 = (f32[3,6,32,128]{3,2,1,0:T(8,128)S(1)}, f32[3,6,32,128]{3,2,1,0:T(8,128)S(1)}, u32[]{:S(2)}, u32[]{:S(2)}) collective-permute-start(f32[3,6,32,128]{3,2,1,0:T(8,128)S(1)} %rows.1.own), channel_id=1, source_target_pairs={{0,16},{16,32},{32,48},{48,64},{64,80},{80,96},{96,112},{112,128},... | collective-permute-start | bytes 884744 | tf_op jit(solution)/shard_map/ppermute | solution.py:324
  65.1 0.0 copy-done
  65.1 0.0 copy-start.1
  65.2 1.4 %copy-done.1 = f32[6,64,1024]{2,1,0:T(8,128)S(1)} copy-done((f32[6,64,1024]{2,1,0:T(8,128)S(1)}, f32[6,64,1024]{2,1,0:T(8,128)}, u32[]{:S(2)}) %copy-start.1) | copy-done | bytes 1572888
  66.6 2.0 %free.1 = (f32[2,3,64,1024]{3,2,1,0:T(8,128)S(1)}, f32[2,3,64,1024]{3,2,1,0:T(8,128)S(1)}) custom-call(s32[2,192]{1,0:T(2,128)S(1)} %bitcast.8, f32[2,3,64,1024]{3,2,1,0:T(8,128)S(1)} %bitcast.5, f32[2,3,64,1024]{3,2,1,0:T(8,128)S(1)} %bitcast.6), custom_call_target="tpu_custom_call" | custom-call | flops 1000000000 | bytes 6291456 | tf_op jit(solution)/shard_map/free/pallas_call | solution.py:326
  68.6 1.4 %collective-permute-done.up = f32[3,6,32,128]{3,2,1,0:T(8,128)S(1)} collective-permute-done((f32[3,6,32,128]{3,2,1,0:T(8,128)S(1)}, f32[3,6,32,128]{3,2,1,0:T(8,128)S(1)}, u32[]{:S(2)}, u32[]{:S(2)}) %collective-permute-start) | collective-permute-done | bytes 294944 | tf_op jit(solution)/shard_map/ppermute | solution.py:323
  70.0 7.2 %collective-permute-done.1.down = f32[3,6,32,128]{3,2,1,0:T(8,128)S(1)} collective-permute-done((f32[3,6,32,128]{3,2,1,0:T(8,128)S(1)}, f32[3,6,32,128]{3,2,1,0:T(8,128)S(1)}, u32[]{:S(2)}, u32[]{:S(2)}) %collective-permute-start.1) | collective-permute-done | bytes 294944 | tf_op jit(solution)/shard_map/ppermute | solution.py:324
  77.2 2.0 %force.1 = f32[16,3,64,128]{3,2,1,0:T(8,128)S(1)} custom-call(s32[36]{0:T(128)S(1)} %get-tuple-element.17.places, f32[3,96,128]{2,1,0:T(8,128)S(1)} %get-tuple-element.18.tables, bf16[3,64,128]{2,1,0:T(8,128)(2,1)S(1)} %get-tuple-element.19.to_modes, f32[3,2,32,128]{3,2,1,0:T(8,128)S(1)} %get-tuple-element.20.masks, f32[3,6,32,128]{3,2,1,0:T(8,128)S(1)} %rows.1.own, ...), custom_call_target="tpu_custom_call" | custom-call | flops 10000000 | bytes 1572864 | tf_op jit(solution)/shard_map/force/pallas_call | solution.py:336
  79.2 44.1 %all_to_all.10.mixed = f32[16,3,64,128]{3,2,1,0:T(8,128)S(1)} all-to-all(f32[16,3,64,128]{3,2,1,0:T(8,128)S(1)} %force.1), channel_id=1, replica_groups=mesh['region'=32,'line'=16] {'line'}, dimensions={0} | all-to-all | bytes 3145728 | tf_op jit(solution)/shard_map/all_to_all | solution.py:345
  123.3 1.4 %update.1 = f32[2,3,64,1024]{3,2,1,0:T(8,128)} custom-call(f32[16,3,64,128]{3,2,1,0:T(8,128)S(1)} %all_to_all.10.mixed, f32[2,3,64,1024]{3,2,1,0:T(8,128)S(1)} %get-tuple-element.27.base, f32[2,3,64,1024]{3,2,1,0:T(8,128)S(1)} %get-tuple-element.28.gain), custom_call_target="tpu_custom_call" | custom-call | flops 10000000 | bytes 6291456 | tf_op jit(solution)/shard_map/update/pallas_call | solution.py:347
Async XLA Ops:
  2.5 10.6 %copy-start.2 = (s32[192,2]{0,1:T(2,128)S(1)}, s32[192,2]{0,1:T(2,128)}, u32[]{:S(2)}) copy-start(s32[192,2]{0,1:T(2,128)} %param.7) | copy-start | bytes 4612
  2.5 10.6 %copy-start.3 = (s32[192]{0:T(256)S(1)}, s32[192]{0:T(256)}, u32[]{:S(2)}) copy-start(s32[192]{0:T(256)} %partner.1) | copy-start | bytes 2308
  2.5 10.6 %copy-start.4 = (s32[192]{0:T(256)S(1)}, s32[192]{0:T(256)}, u32[]{:S(2)}) copy-start(s32[192]{0:T(256)} %offset.1) | copy-start | bytes 2308
  2.5 49.0 %all-to-all-start = ((f32[16,3,64,128]{3,2,1,0:T(8,128)}), f32[16,3,64,128]{3,2,1,0:T(8,128)S(1)}, u32[]{:S(2)}, u32[]{:S(2)}) async-start(f32[16,3,64,128]{3,2,1,0:T(8,128)} %encode.1), calls=%async_computation | async-start | bytes 3145728 | tf_op jit(solution)/shard_map/all_to_all | solution.py:297
  13.1 52.1 %copy-start = (f32[6,64,1024]{2,1,0:T(8,128)S(1)}, f32[6,64,1024]{2,1,0:T(8,128)}, u32[]{:S(2)}) copy-start(f32[6,64,1024]{2,1,0:T(8,128)} %param.5) | copy-start | bytes 4718596
  52.1 17.9 %collective-permute-start = (f32[3,6,32,128]{3,2,1,0:T(8,128)S(1)}, f32[3,6,32,128]{3,2,1,0:T(8,128)S(1)}, u32[]{:S(2)}, u32[]{:S(2)}) collective-permute-start(f32[3,6,32,128]{3,2,1,0:T(8,128)S(1)} %rows.1.own), channel_id=1, source_target_pairs={{16,0},{32,16},{48,32},{64,48},{80,64},{96,80},{112,96},{128,112},... | collective-permute-start | bytes 884744 | tf_op jit(solution)/shard_map/ppermute | solution.py:323
  63.2 14.0 %collective-permute-start.1 = (f32[3,6,32,128]{3,2,1,0:T(8,128)S(1)}, f32[3,6,32,128]{3,2,1,0:T(8,128)S(1)}, u32[]{:S(2)}, u32[]{:S(2)}) collective-permute-start(f32[3,6,32,128]{3,2,1,0:T(8,128)S(1)} %rows.1.own), channel_id=1, source_target_pairs={{0,16},{16,32},{32,48},{48,64},{64,80},{80,96},{96,112},{112,128},... | collective-permute-start | bytes 884744 | tf_op jit(solution)/shard_map/ppermute | solution.py:324
  65.1 1.4 %copy-start.1 = (f32[6,64,1024]{2,1,0:T(8,128)S(1)}, f32[6,64,1024]{2,1,0:T(8,128)}, u32[]{:S(2)}) copy-start(f32[6,64,1024]{2,1,0:T(8,128)} %param.6) | copy-start | bytes 4718596

commit v2 on v1

--- a/solution.py
+++ b/solution.py
@@ -14,6 +14,7 @@
 A1, A2, A3 = 1.5, -0.15, 1.0 / 90.0
 VMEM_LIMIT = 16 * 1024 * 1024
 ENCODE_LIMIT = 63 * 1024 * 1024
+FORCE_LIMIT = 52 * 1024 * 1024
 
 SERIES = [2.0 * (-1.0) ** k / math.factorial(2 * k + 2) for k in range(10)]
 
@@ -79,23 +80,23 @@
 
 def encode_kernel(now, out, held, made, arrived, sent):
     left = left_half((2 * SIDE, LANES))
-    inward = [
-        pltpu.make_async_copy(now.at[:, i], held.at[i], arrived.at[i]) for i in range(PAIRS)
-    ]
-    outward = [
-        pltpu.make_async_copy(made.at[i], out.at[:, i], sent.at[i]) for i in range(PAIRS)
-    ]
-    for copy in inward:
-        copy.start()
-    for pair in range(PAIRS):
-        inward[pair].wait()
-        for chip in range(8):
+    inward, outward = [], []
+    for part in range(2 * PAIRS):
+        pair, half = part // 2, part % 2
+        source = now.at[:, pair, :, pl.ds(half * 512, 512)]
+        target = out.at[pl.ds(half * 8, 8), pair]
+        inward.append(pltpu.make_async_copy(source, held.at[part], arrived.at[part]))
+        outward.append(pltpu.make_async_copy(made.at[part], target, sent.at[part]))
+        inward[-1].start()
+    for part in range(2 * PAIRS):
+        inward[part].wait()
+        for chip in range(4):
             lanes = slice(chip * LANES, chip * LANES + LANES)
-            a = held[pair, 0, :, lanes]
-            b = held[pair, 1, :, lanes]
-            made[pair, 2 * chip] = jnp.where(left, a, pltpu.roll(b, LANES // 2, 1))
-            made[pair, 2 * chip + 1] = jnp.where(left, pltpu.roll(a, LANES // 2, 1), b)
-        outward[pair].start()
+            a = held[part, 0, :, lanes]
+            b = held[part, 1, :, lanes]
+            made[part, 2 * chip] = jnp.where(left, a, pltpu.roll(b, LANES // 2, 1))
+            made[part, 2 * chip + 1] = jnp.where(left, pltpu.roll(a, LANES // 2, 1), b)
+        outward[part].start()
     for copy in outward:
         copy.wait()
 
@@ -150,7 +151,7 @@
             masks[pair, face] = jnp.where(left, parts[0], parts[1])
 
 
-def free_kernel(extents, now, previous, base, gain):
+def free_kernel(extents, now, previous, both):
     first = lax.axis_index("region") * OWN
     line = lax.axis_index("line")
     row = lax.broadcasted_iota(jnp.int32, (2 * SIDE, 256), 0)
@@ -160,20 +161,27 @@
     quarter = (0.5 * math.pi) ** 2
     for r in range(OWN):
         h, pair = r // PAIRS, r % PAIRS
-        live_y = live(extents, first + r, 0)
-        live_z = live(extents, first + r, 1)
-        y = freq_y / live_y
-        z = freq_z / live_z
+        y = freq_y / live(extents, first + r, 0)
+        z = freq_z / live(extents, first + r, 1)
         across = quarter * (y * y + z * z)
-        active = (freq_y < live_y) & (freq_z < live_z)
         for chunk in range(4):
             lanes = slice(chunk * 256, chunk * 256 + 256)
             x = (column + chunk * 256).astype(jnp.float32) * (1.0 / 1024.0)
             u = across + quarter * (x * x)
             s = series(u, 9)
-            stepped = (2.0 - u * s) * now[h, pair, :, lanes] - previous[h, pair, :, lanes]
-            base[h, pair, :, lanes] = jnp.where(active, stepped, 0.0)
-            gain[h, pair, :, lanes] = jnp.where(active, 0.25 * s, 0.0)
+            both[0, h, pair, :, lanes] = (2.0 - u * s) * now[h, pair, :, lanes] - previous[h, pair, :, lanes]
+            both[1, h, pair, :, lanes] = 0.25 * s
+
+
+def active_kernel(extents, active):
+    first = lax.axis_index("region") * OWN
+    line = lax.axis_index("line")
+    row = lax.broadcasted_iota(jnp.int32, (2 * SIDE, LANES), 0)
+    freq_y = 2 * line + row // SIDE
+    freq_z = row % SIDE
+    for r in range(OWN):
+        inside = (freq_y < extents[0, first + r]) & (freq_z < extents[1, first + r])
+        active[r // PAIRS, r % PAIRS] = jnp.where(inside, 1.0, 0.0)
 
 
 def rows_kernel(tables, to_cells, modes, rows):
@@ -235,21 +243,31 @@
         copy.wait()
 
 
-def update_kernel(mixed, base, gain, out, made, sent):
+def update_kernel(mixed_hbm, active, both, out, mixed, made, arrived, sent):
     left = left_half((2 * SIDE, LANES))
-    copies = []
-    for pair in range(PAIRS):
-        for chip in range(8):
-            lanes = slice(chip * LANES, chip * LANES + LANES)
-            a = mixed[2 * chip, pair]
-            b = mixed[2 * chip + 1, pair]
+    inward, outward = [], []
+    for part in range(2 * PAIRS):
+        pair, half = part // 2, part % 2
+        source = mixed_hbm.at[pl.ds(half * 8, 8), pair]
+        target = out.at[:, pair, :, pl.ds(half * 512, 512)]
+        inward.append(pltpu.make_async_copy(source, mixed.at[part], arrived.at[part]))
+        outward.append(pltpu.make_async_copy(made.at[part], target, sent.at[part]))
+        inward[-1].start()
+    for part in range(2 * PAIRS):
+        pair, half = part // 2, part % 2
+        inward[part].wait()
+        for chip in range(4):
+            here = slice(chip * LANES, chip * LANES + LANES)
+            lanes = slice(half * 512 + chip * LANES, half * 512 + chip * LANES + LANES)
+            a = mixed[part, 2 * chip]
+            b = mixed[part, 2 * chip + 1]
             one = jnp.where(left, a, pltpu.roll(b, LANES // 2, 1))
             two = jnp.where(left, pltpu.roll(a, LANES // 2, 1), b)
             for h, spectral in ((0, one), (1, two)):
-                made[pair, h, :, lanes] = base[h, pair, :, lanes] + gain[h, pair, :, lanes] * spectral
-        copies.append(pltpu.make_async_copy(made.at[pair], out.at[:, pair], sent.at[pair]))
-        copies[-1].start()
-    for copy in copies:
+                stepped = both[0, h, pair, :, lanes] + both[1, h, pair, :, lanes] * spectral
+                made[part, h, :, here] = jnp.where(active[h, pair] > 0.0, stepped, 0.0)
+        outward[part].start()
+    for copy in outward:
         copy.wait()
 
 
@@ -280,7 +298,9 @@
     rows_shape = jax.ShapeDtypeStruct((PAIRS, 6, SIDE, LANES), f32)
     table_shape = jax.ShapeDtypeStruct((PAIRS, 2 * SIDE, LANES), jnp.bfloat16)
     params = pltpu.CompilerParams(vmem_limit_bytes=VMEM_LIMIT)
-    wide_scratch = pltpu.VMEM((PAIRS, 2, 2 * SIDE, 1024), f32)
+    wide_parts = pltpu.VMEM((2 * PAIRS, 2, 2 * SIDE, 512), f32)
+    packed_parts = pltpu.VMEM((2 * PAIRS, 8, 2 * SIDE, LANES), f32)
+    copied_parts = pltpu.SemaphoreType.DMA((2 * PAIRS,))
     packed_scratch = pltpu.VMEM((PAIRS, 16, 2 * SIDE, LANES), f32)
     copied = pltpu.SemaphoreType.DMA((PAIRS,))
 
@@ -290,7 +310,7 @@
             out_shape=packed_shape,
             in_specs=[hbm()],
             out_specs=hbm(),
-            scratch_shapes=[wide_scratch, packed_scratch, copied, copied],
+            scratch_shapes=[wide_parts, packed_parts, copied_parts, copied_parts],
             compiler_params=pltpu.CompilerParams(vmem_limit_bytes=ENCODE_LIMIT),
             cost_estimate=cost(10**6, 2 * nbytes),
         )(now)
@@ -323,15 +343,24 @@
     up = lax.ppermute(rows, "region", [((i + 1) % count, i) for i in range(count)])
     down = lax.ppermute(rows, "region", [(i, (i + 1) % count) for i in range(count)])
     with jax.named_scope("free"):
-        base, gain = pl.pallas_call(
+        both = pl.pallas_call(
             free_kernel,
-            out_shape=(wide_shape, wide_shape),
+            out_shape=jax.ShapeDtypeStruct((2, *now.shape), f32),
             in_specs=[smem(), vmem(), vmem()],
-            out_specs=(vmem(), vmem()),
+            out_specs=vmem(),
             compiler_params=params,
             cost_estimate=cost(10**9, 4 * nbytes),
         )(extents, *lax.optimization_barrier((now, previous, rows))[:2])
-    up, base, gain = lax.optimization_barrier((up, base, gain))
+    down, both = lax.optimization_barrier((down, both))
+    with jax.named_scope("active"):
+        active = pl.pallas_call(
+            active_kernel,
+            out_shape=jax.ShapeDtypeStruct((2, PAIRS, 2 * SIDE, LANES), f32),
+            in_specs=[smem()],
+            out_specs=vmem(),
+            compiler_params=params,
+            cost_estimate=cost(10**9, nbytes),
+        )(extents)
     with jax.named_scope("force"):
         forced = pl.pallas_call(
             force_kernel,
@@ -339,7 +368,7 @@
             in_specs=[smem()] + [vmem()] * 6,
             out_specs=hbm(),
             scratch_shapes=[pltpu.VMEM((3 * PAIRS, 6, SIDE, LANES), f32), packed_scratch, copied],
-            compiler_params=params,
+            compiler_params=pltpu.CompilerParams(vmem_limit_bytes=FORCE_LIMIT),
             cost_estimate=cost(10**7, nbytes),
         )(places, y_tables, to_modes, masks, rows, up, down)
     mixed = lax.all_to_all(forced, "line", 0, 0, tiled=True)
@@ -347,12 +376,12 @@
         result = pl.pallas_call(
             update_kernel,
             out_shape=wide_shape,
-            in_specs=[vmem()] * 3,
+            in_specs=[hbm(), vmem(), vmem()],
             out_specs=hbm(),
-            scratch_shapes=[wide_scratch, copied],
+            scratch_shapes=[packed_parts, wide_parts, copied_parts, copied_parts],
             compiler_params=params,
             cost_estimate=cost(10**7, 4 * nbytes),
-        )(mixed, base, gain)
+        )(mixed, active, both)
     return result.reshape(modes_now.shape)
 
 

time: 125 us -> 120 us (0.960)
  blocking collectives: 44.1 us -> 0 us
  waiting for transfers between devices: 45.1 us -> 76.6 us
  starting transfers between devices: 23.5 us -> 28 us
  Pallas kernels: 10.4 us -> 12.4 us
  local copies, waits for them, and re-layouts: 1.43 us -> 2.83 us
    all_to_all x1 -> x0, blocking collectives: 44.1 us -> none  [shards(): mixed = lax.all_to_all(forced, 'line', 0, 0, tiled=True)]
    all_to_all x0 -> x1, waiting for transfers between devices: none -> 38 us  [shards(): mixed = lax.all_to_all(forced, 'line', 0, 0, tiled=True)]
    ppermute x1, waiting for transfers between devices: 7.17 us -> 0.34 us  [shards(): lax.ppermute(rows, 'region', [(i, (i + 1) % count) for i in range(count)])]
    all_to_all x0 -> x1, starting transfers between devices: none -> 4.51 us  [shards(): mixed = lax.all_to_all(forced, 'line', 0, 0, tiled=True)]
    pallas_call x2 -> x3, Pallas kernels: 3.4 us -> 5.09 us  [the longest x1 2.62 us: shards(): pl.pallas_call(update_kernel, out_shape=wide_shape, in_specs=[hbm(), vmem...]
    unnamed x10, local copies, waits for them, and re-layouts: 1.43 us -> 2.83 us
  transfers between devices with their start and end apart: 3 -> 4, of which waited for: 3 -> 4; matrix products, arithmetic and copies ran while one was open for 0% -> 0% of each run, Pallas kernels for 3% -> 4%
where the time goes in v2:
time: 120 us
  waiting for transfers between devices  76.6 us (64%)
  starting transfers between devices  28 us (23%)
  Pallas kernels  12.4 us (10%)
  local copies, waits for them, and re-layouts  2.83 us (2%)
    all_to_all x1, waiting for transfers between devices, shards(): mixed = lax.all_to_all(forced, 'line', 0, 0, tiled=True)  38 us
    all_to_all x1, waiting for transfers between devices, shards(): held = lax.all_to_all(sent, 'line', 0, 0, tiled=True)  36.5 us
    ppermute x1, starting transfers between devices, shards(): lax.ppermute(rows, 'region', [((i + 1) % count, i) for i in range(count)])  10.8 us
    all_to_all x1, starting transfers between devices, shards(): held = lax.all_to_all(sent, 'line', 0, 0, tiled=True)  10.5 us
    all_to_all x1, starting transfers between devices, shards(): mixed = lax.all_to_all(forced, 'line', 0, 0, tiled=True)  4.51 us
    unnamed x10, local copies, waits for them, and re-layouts  2.83 us
    pallas_call x1, Pallas kernels, shards(): pl.pallas_call(update_kernel, out_shape=wide_shape, in_specs=[hbm(), vmem...  2.62 us
    pallas_call x1, Pallas kernels, shards(): pl.pallas_call(encode_kernel, out_shape=packed_shape, in_specs=[hbm()], o...  2.58 us
  transfers between devices with their start and end apart: 4, of which 4 were waited for; matrix products, arithmetic and copies ran while one was open for 0% of the time, Pallas kernels for 4%

profile of v2, /device:TPU:1, one launch (start us, length us, event | category | flops | bytes accessed | tf_op | source)
XLA Modules:
  0.0 120.0 jit_solution(5443446222202876807)
XLA Ops:
  0.0 2.6 %encode.1 = f32[16,3,64,128]{3,2,1,0:T(8,128)} custom-call(f32[2,3,64,1024]{3,2,1,0:T(8,128)} %bitcast.4), custom_call_target="tpu_custom_call" | custom-call | flops 1000000 | bytes 3145728 | tf_op jit(solution)/shard_map/encode/pallas_call | solution.py:308
  2.6 0.0 copy-start.2
  2.6 0.0 copy-start.3
  2.6 0.0 copy-start.4
  2.6 10.5 %all-to-all-start = ((f32[16,3,64,128]{3,2,1,0:T(8,128)}), f32[16,3,64,128]{3,2,1,0:T(8,128)S(1)}, u32[]{:S(2)}, u32[]{:S(2)}) async-start(f32[16,3,64,128]{3,2,1,0:T(8,128)} %encode.1), calls=%async_computation | async-start | bytes 3145728 | tf_op jit(solution)/shard_map/all_to_all | solution.py:317
  13.1 0.0 copy-done.2
  13.1 0.0 copy-done.3
  13.2 0.0 copy-done.4
  13.2 1.9 %plan.1 = (f32[3,96,128]{2,1,0:T(8,128)S(1)}, bf16[3,64,128]{2,1,0:T(8,128)(2,1)S(1)}, bf16[3,64,128]{2,1,0:T(8,128)(2,1)S(1)}, f32[3,2,32,128]{3,2,1,0:T(8,128)S(1)}, s32[36]{0:T(128)S(1)}) custom-call(s32[2,192]{1,0:T(2,128)S(1)} %bitcast.7, s32[192]{0:T(256)S(1)} %copy-done.3, s32[192]{0:T(256)S(1)} %copy-done.4), custom_call_target="tpu_custom_call" | custom-call | flops 100000000 | bytes 1000000 | tf_op jit(solution)/shard_map/plan/pallas_call | solution.py:319
  15.1 36.5 %all-to-all-done.modes = f32[16,3,64,128]{3,2,1,0:T(8,128)S(1)} async-done(((f32[16,3,64,128]{3,2,1,0:T(8,128)}), f32[16,3,64,128]{3,2,1,0:T(8,128)S(1)}, u32[]{:S(2)}, u32[]{:S(2)}) %all-to-all-start) | async-done | bytes 1572896 | tf_op jit(solution)/shard_map/all_to_all | solution.py:317
  51.6 0.6 rows.1.own
  52.2 2.2 %collective-permute-start.1 = (f32[3,6,32,128]{3,2,1,0:T(8,128)S(1)}, f32[3,6,32,128]{3,2,1,0:T(8,128)S(1)}, u32[]{:S(2)}, u32[]{:S(2)}) collective-permute-start(f32[3,6,32,128]{3,2,1,0:T(8,128)S(1)} %rows.1.own), channel_id=1, source_target_pairs={{0,16},{16,32},{32,48},{48,64},{64,80},{80,96},{96,112},{112,128},... | collective-permute-start | bytes 884744 | tf_op jit(solution)/shard_map/ppermute | solution.py:344
  54.4 10.8 %collective-permute-start = (f32[3,6,32,128]{3,2,1,0:T(8,128)S(1)}, f32[3,6,32,128]{3,2,1,0:T(8,128)S(1)}, u32[]{:S(2)}, u32[]{:S(2)}) collective-permute-start(f32[3,6,32,128]{3,2,1,0:T(8,128)S(1)} %rows.1.own), channel_id=1, source_target_pairs={{16,0},{32,16},{48,32},{64,48},{80,64},{96,80},{112,96},{128,112},... | collective-permute-start | bytes 884744 | tf_op jit(solution)/shard_map/ppermute | solution.py:343
  65.2 0.0 copy-start
  65.3 1.4 %copy-done = f32[6,64,1024]{2,1,0:T(8,128)S(1)} copy-done((f32[6,64,1024]{2,1,0:T(8,128)S(1)}, f32[6,64,1024]{2,1,0:T(8,128)}, u32[]{:S(2)}) %copy-start) | copy-done | bytes 1572888
  66.7 0.0 copy-start.1
  66.7 1.4 %copy-done.1 = f32[6,64,1024]{2,1,0:T(8,128)S(1)} copy-done((f32[6,64,1024]{2,1,0:T(8,128)S(1)}, f32[6,64,1024]{2,1,0:T(8,128)}, u32[]{:S(2)}) %copy-start.1) | copy-done | bytes 1572888
  68.1 1.9 %free.1.both = f32[2,2,3,64,1024]{4,3,2,1,0:T(8,128)S(1)} custom-call(s32[2,192]{1,0:T(2,128)S(1)} %bitcast.8, f32[2,3,64,1024]{3,2,1,0:T(8,128)S(1)} %bitcast.5, f32[2,3,64,1024]{3,2,1,0:T(8,128)S(1)} %bitcast.6), custom_call_target="tpu_custom_call" | custom-call | flops 1000000000 | bytes 6291456 | tf_op jit(solution)/shard_map/free/pallas_call | solution.py:346
  69.9 0.3 collective-permute-done.1.down
  70.3 1.8 %collective-permute-done.up = f32[3,6,32,128]{3,2,1,0:T(8,128)S(1)} collective-permute-done((f32[3,6,32,128]{3,2,1,0:T(8,128)S(1)}, f32[3,6,32,128]{3,2,1,0:T(8,128)S(1)}, u32[]{:S(2)}, u32[]{:S(2)}) %collective-permute-start) | collective-permute-done | bytes 294944 | tf_op jit(solution)/shard_map/ppermute | solution.py:343
  72.0 2.2 %force.1 = f32[16,3,64,128]{3,2,1,0:T(8,128)} custom-call(s32[36]{0:T(128)S(1)} %get-tuple-element.14.places, f32[3,96,128]{2,1,0:T(8,128)S(1)} %get-tuple-element.15.tables, bf16[3,64,128]{2,1,0:T(8,128)(2,1)S(1)} %get-tuple-element.16.to_modes, f32[3,2,32,128]{3,2,1,0:T(8,128)S(1)} %get-tuple-element.17.masks, f32[3,6,32,128]{3,2,1,0:T(8,128)S(1)} %rows.1.own, ...), custom_call_target="tpu_custom_call" | custom-call | flops 10000000 | bytes 1572864 | tf_op jit(solution)/shard_map/force/pallas_call | solution.py:365
  74.3 4.5 %all-to-all-start.1 = ((f32[16,3,64,128]{3,2,1,0:T(8,128)}), f32[16,3,64,128]{3,2,1,0:T(8,128)}, u32[]{:S(2)}, u32[]{:S(2)}) async-start(f32[16,3,64,128]{3,2,1,0:T(8,128)} %force.1), calls=%async_computation.1 | async-start | bytes 3145728 | tf_op jit(solution)/shard_map/all_to_all | solution.py:374
  78.8 0.6 active.1
  79.4 38.0 %all-to-all-done.1.mixed_hbm = f32[16,3,64,128]{3,2,1,0:T(8,128)} async-done(((f32[16,3,64,128]{3,2,1,0:T(8,128)}), f32[16,3,64,128]{3,2,1,0:T(8,128)}, u32[]{:S(2)}, u32[]{:S(2)}) %all-to-all-start.1) | async-done | bytes 1572896 | tf_op jit(solution)/shard_map/all_to_all | solution.py:374
  117.4 2.6 %update.1 = f32[2,3,64,1024]{3,2,1,0:T(8,128)} custom-call(f32[16,3,64,128]{3,2,1,0:T(8,128)} %all-to-all-done.1.mixed_hbm, f32[2,3,64,128]{3,2,1,0:T(8,128)S(1)} %active.1, f32[2,2,3,64,1024]{4,3,2,1,0:T(8,128)S(1)} %free.1.both), custom_call_target="tpu_custom_call" | custom-call | flops 10000000 | bytes 6291456 | tf_op jit(solution)/shard_map/update/pallas_call | solution.py:376
Async XLA Ops:
  2.6 10.6 %copy-start.2 = (s32[192,2]{0,1:T(2,128)S(1)}, s32[192,2]{0,1:T(2,128)}, u32[]{:S(2)}) copy-start(s32[192,2]{0,1:T(2,128)} %param.7) | copy-start | bytes 4612
  2.6 10.6 %copy-start.3 = (s32[192]{0:T(256)S(1)}, s32[192]{0:T(256)}, u32[]{:S(2)}) copy-start(s32[192]{0:T(256)} %partner.1) | copy-start | bytes 2308
  2.6 10.5 %copy-start.4 = (s32[192]{0:T(256)S(1)}, s32[192]{0:T(256)}, u32[]{:S(2)}) copy-start(s32[192]{0:T(256)} %offset.1) | copy-start | bytes 2308
  2.6 49.0 %all-to-all-start = ((f32[16,3,64,128]{3,2,1,0:T(8,128)}), f32[16,3,64,128]{3,2,1,0:T(8,128)S(1)}, u32[]{:S(2)}, u32[]{:S(2)}) async-start(f32[16,3,64,128]{3,2,1,0:T(8,128)} %encode.1), calls=%async_computation | async-start | bytes 3145728 | tf_op jit(solution)/shard_map/all_to_all | solution.py:317
  52.2 18.0 %collective-permute-start.1 = (f32[3,6,32,128]{3,2,1,0:T(8,128)S(1)}, f32[3,6,32,128]{3,2,1,0:T(8,128)S(1)}, u32[]{:S(2)}, u32[]{:S(2)}) collective-permute-start(f32[3,6,32,128]{3,2,1,0:T(8,128)S(1)} %rows.1.own), channel_id=1, source_target_pairs={{0,16},{16,32},{32,48},{48,64},{64,80},{80,96},{96,112},{112,128},... | collective-permute-start | bytes 884744 | tf_op jit(solution)/shard_map/ppermute | solution.py:344
  54.4 17.6 %collective-permute-start = (f32[3,6,32,128]{3,2,1,0:T(8,128)S(1)}, f32[3,6,32,128]{3,2,1,0:T(8,128)S(1)}, u32[]{:S(2)}, u32[]{:S(2)}) collective-permute-start(f32[3,6,32,128]{3,2,1,0:T(8,128)S(1)} %rows.1.own), channel_id=1, source_target_pairs={{16,0},{32,16},{48,32},{64,48},{80,64},{96,80},{112,96},{128,112},... | collective-permute-start | bytes 884744 | tf_op jit(solution)/shard_map/ppermute | solution.py:343
  65.2 1.4 %copy-start = (f32[6,64,1024]{2,1,0:T(8,128)S(1)}, f32[6,64,1024]{2,1,0:T(8,128)}, u32[]{:S(2)}) copy-start(f32[6,64,1024]{2,1,0:T(8,128)} %param.5) | copy-start | bytes 4718596
  66.7 1.4 %copy-start.1 = (f32[6,64,1024]{2,1,0:T(8,128)S(1)}, f32[6,64,1024]{2,1,0:T(8,128)}, u32[]{:S(2)}) copy-start(f32[6,64,1024]{2,1,0:T(8,128)} %param.6) | copy-start | bytes 4718596
  74.3 43.1 %all-to-all-start.1 = ((f32[16,3,64,128]{3,2,1,0:T(8,128)}), f32[16,3,64,128]{3,2,1,0:T(8,128)}, u32[]{:S(2)}, u32[]{:S(2)}) async-start(f32[16,3,64,128]{3,2,1,0:T(8,128)} %force.1), calls=%async_computation.1 | async-start | bytes 3145728 | tf_op jit(solution)/shard_map/all_to_all | solution.py:374

commit v3 on v1

--- a/solution.py
+++ b/solution.py
@@ -79,23 +79,23 @@
 
 def encode_kernel(now, out, held, made, arrived, sent):
     left = left_half((2 * SIDE, LANES))
-    inward = [
-        pltpu.make_async_copy(now.at[:, i], held.at[i], arrived.at[i]) for i in range(PAIRS)
-    ]
-    outward = [
-        pltpu.make_async_copy(made.at[i], out.at[:, i], sent.at[i]) for i in range(PAIRS)
-    ]
-    for copy in inward:
-        copy.start()
-    for pair in range(PAIRS):
-        inward[pair].wait()
-        for chip in range(8):
+    inward, outward = [], []
+    for part in range(2 * PAIRS):
+        pair, half = part // 2, part % 2
+        source = now.at[:, pair, :, pl.ds(half * 512, 512)]
+        target = out.at[pl.ds(half * 8, 8), pair]
+        inward.append(pltpu.make_async_copy(source, held.at[part], arrived.at[part]))
+        outward.append(pltpu.make_async_copy(made.at[part], target, sent.at[part]))
+        inward[-1].start()
+    for part in range(2 * PAIRS):
+        inward[part].wait()
+        for chip in range(4):
             lanes = slice(chip * LANES, chip * LANES + LANES)
-            a = held[pair, 0, :, lanes]
-            b = held[pair, 1, :, lanes]
-            made[pair, 2 * chip] = jnp.where(left, a, pltpu.roll(b, LANES // 2, 1))
-            made[pair, 2 * chip + 1] = jnp.where(left, pltpu.roll(a, LANES // 2, 1), b)
-        outward[pair].start()
+            a = held[part, 0, :, lanes]
+            b = held[part, 1, :, lanes]
+            made[part, 2 * chip] = jnp.where(left, a, pltpu.roll(b, LANES // 2, 1))
+            made[part, 2 * chip + 1] = jnp.where(left, pltpu.roll(a, LANES // 2, 1), b)
+        outward[part].start()
     for copy in outward:
         copy.wait()
 
@@ -196,8 +196,7 @@
     return [A1 * d[0] + A2 * d[1] + A3 * d[2], A2 * d[0] + A3 * d[1], A3 * d[0]]
 
 
-def force_kernel(places, tables, to_modes, masks, own, up, down, out, near, made, sent):
-    copies = []
+def force_kernel(places, tables, to_modes, masks, own, up, down, out, near):
     for pair in range(PAIRS):
         near[pair] = down[pair]
         near[PAIRS + pair] = own[pair]
@@ -228,11 +227,7 @@
                     at = e * SIDE + 2 * target + which
                     term = tables[pair, at : at + 1] * parts[e]
                     value = term if value is None else value + term
-                made[pair, target, which * SIDE : (which + 1) * SIDE] = value
-        copies.append(pltpu.make_async_copy(made.at[pair], out.at[:, pair], sent.at[pair]))
-        copies[-1].start()
-    for copy in copies:
-        copy.wait()
+                out[target, pair, which * SIDE : (which + 1) * SIDE] = value
 
 
 def update_kernel(mixed, base, gain, out, made, sent):
@@ -280,9 +275,9 @@
     rows_shape = jax.ShapeDtypeStruct((PAIRS, 6, SIDE, LANES), f32)
     table_shape = jax.ShapeDtypeStruct((PAIRS, 2 * SIDE, LANES), jnp.bfloat16)
     params = pltpu.CompilerParams(vmem_limit_bytes=VMEM_LIMIT)
-    wide_scratch = pltpu.VMEM((PAIRS, 2, 2 * SIDE, 1024), f32)
-    packed_scratch = pltpu.VMEM((PAIRS, 16, 2 * SIDE, LANES), f32)
-    copied = pltpu.SemaphoreType.DMA((PAIRS,))
+    wide_parts = pltpu.VMEM((2 * PAIRS, 2, 2 * SIDE, 512), f32)
+    packed_parts = pltpu.VMEM((2 * PAIRS, 8, 2 * SIDE, LANES), f32)
+    copied_parts = pltpu.SemaphoreType.DMA((2 * PAIRS,))
 
     with jax.named_scope("encode"):
         sent = pl.pallas_call(
@@ -290,7 +285,7 @@
             out_shape=packed_shape,
             in_specs=[hbm()],
             out_specs=hbm(),
-            scratch_shapes=[wide_scratch, packed_scratch, copied, copied],
+            scratch_shapes=[wide_parts, packed_parts, copied_parts, copied_parts],
             compiler_params=pltpu.CompilerParams(vmem_limit_bytes=ENCODE_LIMIT),
             cost_estimate=cost(10**6, 2 * nbytes),
         )(now)
@@ -331,14 +326,14 @@
             compiler_params=params,
             cost_estimate=cost(10**9, 4 * nbytes),
         )(extents, *lax.optimization_barrier((now, previous, rows))[:2])
-    up, base, gain = lax.optimization_barrier((up, base, gain))
+    down, base, gain = lax.optimization_barrier((down, base, gain))
     with jax.named_scope("force"):
         forced = pl.pallas_call(
             force_kernel,
             out_shape=packed_shape,
             in_specs=[smem()] + [vmem()] * 6,
-            out_specs=hbm(),
-            scratch_shapes=[pltpu.VMEM((3 * PAIRS, 6, SIDE, LANES), f32), packed_scratch, copied],
+            out_specs=vmem(),
+            scratch_shapes=[pltpu.VMEM((3 * PAIRS, 6, SIDE, LANES), f32)],
             compiler_params=params,
             cost_estimate=cost(10**7, nbytes),
         )(places, y_tables, to_modes, masks, rows, up, down)
@@ -349,7 +344,7 @@
             out_shape=wide_shape,
             in_specs=[vmem()] * 3,
             out_specs=hbm(),
-            scratch_shapes=[wide_scratch, copied],
+            scratch_shapes=[pltpu.VMEM((PAIRS, 2, 2 * SIDE, 1024), f32), pltpu.SemaphoreType.DMA((PAIRS,))],
             compiler_params=params,
             cost_estimate=cost(10**7, 4 * nbytes),
         )(mixed, base, gain)

time: 125 us -> 119 us (0.952)
  waiting for transfers between devices: 45.1 us -> 39.9 us
    ppermute x1, waiting for transfers between devices: 7.17 us -> 1.58 us  [shards(): lax.ppermute(rows, 'region', [(i, (i + 1) % count) for i in range(count)])]
where the time goes in v3:
time: 119 us
  blocking collectives  43.8 us (37%)
  waiting for transfers between devices  39.9 us (34%)
  starting transfers between devices  23.5 us (20%)
  Pallas kernels  9.79 us (8%)
  local copies, waits for them, and re-layouts  1.43 us (1%)
    all_to_all x1, blocking collectives, shards(): mixed = lax.all_to_all(forced, 'line', 0, 0, tiled=True)  43.8 us
    all_to_all x1, waiting for transfers between devices, shards(): held = lax.all_to_all(sent, 'line', 0, 0, tiled=True)  36.5 us
    ppermute x1, starting transfers between devices, shards(): lax.ppermute(rows, 'region', [((i + 1) % count, i) for i in range(count)])  10.8 us
    all_to_all x1, starting transfers between devices, shards(): held = lax.all_to_all(sent, 'line', 0, 0, tiled=True)  10.5 us
    pallas_call x1, Pallas kernels, shards(): pl.pallas_call(encode_kernel, out_shape=packed_shape, in_specs=[hbm()], o...  2.58 us
  transfers between devices with their start and end apart: 3, of which 3 were waited for; matrix products, arithmetic and copies ran while one was open for 0% of the time, Pallas kernels for 3%

profile of v3, /device:TPU:1, one launch (start us, length us, event | category | flops | bytes accessed | tf_op | source)
XLA Modules:
  0.0 118.6 jit_solution(13541327165274094279)
XLA Ops:
  0.0 2.6 %encode.1 = f32[16,3,64,128]{3,2,1,0:T(8,128)} custom-call(f32[2,3,64,1024]{3,2,1,0:T(8,128)} %bitcast.4), custom_call_target="tpu_custom_call" | custom-call | flops 1000000 | bytes 3145728 | tf_op jit(solution)/shard_map/encode/pallas_call | solution.py:283
  2.6 0.0 copy-start.2
  2.6 0.0 copy-start.3
  2.6 0.0 copy-start.4
  2.6 10.5 %all-to-all-start = ((f32[16,3,64,128]{3,2,1,0:T(8,128)}), f32[16,3,64,128]{3,2,1,0:T(8,128)S(1)}, u32[]{:S(2)}, u32[]{:S(2)}) async-start(f32[16,3,64,128]{3,2,1,0:T(8,128)} %encode.1), calls=%async_computation | async-start | bytes 3145728 | tf_op jit(solution)/shard_map/all_to_all | solution.py:292
  13.1 0.0 copy-start
  13.1 0.0 copy-done.2
  13.2 0.0 copy-done.3
  13.2 0.0 copy-done.4
  13.2 1.9 %plan.1 = (f32[3,96,128]{2,1,0:T(8,128)S(1)}, bf16[3,64,128]{2,1,0:T(8,128)(2,1)S(1)}, bf16[3,64,128]{2,1,0:T(8,128)(2,1)S(1)}, f32[3,2,32,128]{3,2,1,0:T(8,128)S(1)}, s32[36]{0:T(128)S(1)}) custom-call(s32[2,192]{1,0:T(2,128)S(1)} %bitcast.7, s32[192]{0:T(256)S(1)} %copy-done.3, s32[192]{0:T(256)S(1)} %copy-done.4), custom_call_target="tpu_custom_call" | custom-call | flops 100000000 | bytes 1000000 | tf_op jit(solution)/shard_map/plan/pallas_call | solution.py:294
  15.1 36.5 %all-to-all-done.modes = f32[16,3,64,128]{3,2,1,0:T(8,128)S(1)} async-done(((f32[16,3,64,128]{3,2,1,0:T(8,128)}), f32[16,3,64,128]{3,2,1,0:T(8,128)S(1)}, u32[]{:S(2)}, u32[]{:S(2)}) %all-to-all-start) | async-done | bytes 1572896 | tf_op jit(solution)/shard_map/all_to_all | solution.py:292
  51.6 0.6 rows.1.own
  52.2 2.2 %collective-permute-start.1 = (f32[3,6,32,128]{3,2,1,0:T(8,128)S(1)}, f32[3,6,32,128]{3,2,1,0:T(8,128)S(1)}, u32[]{:S(2)}, u32[]{:S(2)}) collective-permute-start(f32[3,6,32,128]{3,2,1,0:T(8,128)S(1)} %rows.1.own), channel_id=1, source_target_pairs={{0,16},{16,32},{32,48},{48,64},{64,80},{80,96},{96,112},{112,128},... | collective-permute-start | bytes 884744 | tf_op jit(solution)/shard_map/ppermute | solution.py:319
  54.4 10.8 %collective-permute-start = (f32[3,6,32,128]{3,2,1,0:T(8,128)S(1)}, f32[3,6,32,128]{3,2,1,0:T(8,128)S(1)}, u32[]{:S(2)}, u32[]{:S(2)}) collective-permute-start(f32[3,6,32,128]{3,2,1,0:T(8,128)S(1)} %rows.1.own), channel_id=1, source_target_pairs={{16,0},{32,16},{48,32},{64,48},{80,64},{96,80},{112,96},{128,112},... | collective-permute-start | bytes 884744 | tf_op jit(solution)/shard_map/ppermute | solution.py:318
  65.2 0.0 copy-done
  65.2 0.0 copy-start.1
  65.2 1.4 %copy-done.1 = f32[6,64,1024]{2,1,0:T(8,128)S(1)} copy-done((f32[6,64,1024]{2,1,0:T(8,128)S(1)}, f32[6,64,1024]{2,1,0:T(8,128)}, u32[]{:S(2)}) %copy-start.1) | copy-done | bytes 1572888
  66.6 2.0 %free.1 = (f32[2,3,64,1024]{3,2,1,0:T(8,128)S(1)}, f32[2,3,64,1024]{3,2,1,0:T(8,128)S(1)}) custom-call(s32[2,192]{1,0:T(2,128)S(1)} %bitcast.8, f32[2,3,64,1024]{3,2,1,0:T(8,128)S(1)} %bitcast.5, f32[2,3,64,1024]{3,2,1,0:T(8,128)S(1)} %bitcast.6), custom_call_target="tpu_custom_call" | custom-call | flops 1000000000 | bytes 6291456 | tf_op jit(solution)/shard_map/free/pallas_call | solution.py:321
  68.7 1.6 %collective-permute-done.1.down = f32[3,6,32,128]{3,2,1,0:T(8,128)S(1)} collective-permute-done((f32[3,6,32,128]{3,2,1,0:T(8,128)S(1)}, f32[3,6,32,128]{3,2,1,0:T(8,128)S(1)}, u32[]{:S(2)}, u32[]{:S(2)}) %collective-permute-start.1) | collective-permute-done | bytes 294944 | tf_op jit(solution)/shard_map/ppermute | solution.py:319
  70.2 1.8 %collective-permute-done.up = f32[3,6,32,128]{3,2,1,0:T(8,128)S(1)} collective-permute-done((f32[3,6,32,128]{3,2,1,0:T(8,128)S(1)}, f32[3,6,32,128]{3,2,1,0:T(8,128)S(1)}, u32[]{:S(2)}, u32[]{:S(2)}) %collective-permute-start) | collective-permute-done | bytes 294944 | tf_op jit(solution)/shard_map/ppermute | solution.py:318
  72.0 1.3 %force.1 = f32[16,3,64,128]{3,2,1,0:T(8,128)S(1)} custom-call(s32[36]{0:T(128)S(1)} %get-tuple-element.17.places, f32[3,96,128]{2,1,0:T(8,128)S(1)} %get-tuple-element.18.tables, bf16[3,64,128]{2,1,0:T(8,128)(2,1)S(1)} %get-tuple-element.19.to_modes, f32[3,2,32,128]{3,2,1,0:T(8,128)S(1)} %get-tuple-element.20.masks, f32[3,6,32,128]{3,2,1,0:T(8,128)S(1)} %rows.1.own, ...), custom_call_target="tpu_custom_call" | custom-call | flops 10000000 | bytes 1572864 | tf_op jit(solution)/shard_map/force/pallas_call | solution.py:331
  73.3 43.8 %all_to_all.10.mixed = f32[16,3,64,128]{3,2,1,0:T(8,128)S(1)} all-to-all(f32[16,3,64,128]{3,2,1,0:T(8,128)S(1)} %force.1), channel_id=1, replica_groups=mesh['region'=32,'line'=16] {'line'}, dimensions={0} | all-to-all | bytes 3145728 | tf_op jit(solution)/shard_map/all_to_all | solution.py:340
  117.2 1.4 %update.1 = f32[2,3,64,1024]{3,2,1,0:T(8,128)} custom-call(f32[16,3,64,128]{3,2,1,0:T(8,128)S(1)} %all_to_all.10.mixed, f32[2,3,64,1024]{3,2,1,0:T(8,128)S(1)} %get-tuple-element.27.base, f32[2,3,64,1024]{3,2,1,0:T(8,128)S(1)} %get-tuple-element.28.gain), custom_call_target="tpu_custom_call" | custom-call | flops 10000000 | bytes 6291456 | tf_op jit(solution)/shard_map/update/pallas_call | solution.py:342
Async XLA Ops:
  2.6 10.6 %copy-start.2 = (s32[192,2]{0,1:T(2,128)S(1)}, s32[192,2]{0,1:T(2,128)}, u32[]{:S(2)}) copy-start(s32[192,2]{0,1:T(2,128)} %param.7) | copy-start | bytes 4612
  2.6 10.6 %copy-start.3 = (s32[192]{0:T(256)S(1)}, s32[192]{0:T(256)}, u32[]{:S(2)}) copy-start(s32[192]{0:T(256)} %partner.1) | copy-start | bytes 2308
  2.6 10.6 %copy-start.4 = (s32[192]{0:T(256)S(1)}, s32[192]{0:T(256)}, u32[]{:S(2)}) copy-start(s32[192]{0:T(256)} %offset.1) | copy-start | bytes 2308
  2.6 49.0 %all-to-all-start = ((f32[16,3,64,128]{3,2,1,0:T(8,128)}), f32[16,3,64,128]{3,2,1,0:T(8,128)S(1)}, u32[]{:S(2)}, u32[]{:S(2)}) async-start(f32[16,3,64,128]{3,2,1,0:T(8,128)} %encode.1), calls=%async_computation | async-start | bytes 3145728 | tf_op jit(solution)/shard_map/all_to_all | solution.py:292
  13.1 52.1 %copy-start = (f32[6,64,1024]{2,1,0:T(8,128)S(1)}, f32[6,64,1024]{2,1,0:T(8,128)}, u32[]{:S(2)}) copy-start(f32[6,64,1024]{2,1,0:T(8,128)} %param.5) | copy-start | bytes 4718596
  52.2 18.0 %collective-permute-start.1 = (f32[3,6,32,128]{3,2,1,0:T(8,128)S(1)}, f32[3,6,32,128]{3,2,1,0:T(8,128)S(1)}, u32[]{:S(2)}, u32[]{:S(2)}) collective-permute-start(f32[3,6,32,128]{3,2,1,0:T(8,128)S(1)} %rows.1.own), channel_id=1, source_target_pairs={{0,16},{16,32},{32,48},{48,64},{64,80},{80,96},{96,112},{112,128},... | collective-permute-start | bytes 884744 | tf_op jit(solution)/shard_map/ppermute | solution.py:319
  54.4 17.6 %collective-permute-start = (f32[3,6,32,128]{3,2,1,0:T(8,128)S(1)}, f32[3,6,32,128]{3,2,1,0:T(8,128)S(1)}, u32[]{:S(2)}, u32[]{:S(2)}) collective-permute-start(f32[3,6,32,128]{3,2,1,0:T(8,128)S(1)} %rows.1.own), channel_id=1, source_target_pairs={{16,0},{32,16},{48,32},{64,48},{80,64},{96,80},{112,96},{128,112},... | collective-permute-start | bytes 884744 | tf_op jit(solution)/shard_map/ppermute | solution.py:318
  65.2 1.4 %copy-start.1 = (f32[6,64,1024]{2,1,0:T(8,128)S(1)}, f32[6,64,1024]{2,1,0:T(8,128)}, u32[]{:S(2)}) copy-start(f32[6,64,1024]{2,1,0:T(8,128)} %param.6) | copy-start | bytes 4718596

commit v4 on v1

v4 whole, which is shorter than its diff:
```python
import functools
import math

import jax
import jax.numpy as jnp
from jax import lax
from jax.experimental import pallas as pl
from jax.experimental.pallas import tpu as pltpu
from jax.sharding import PartitionSpec as P

SIDE = 32
PAIRS = 3
OWN = 6
LANES = 128
A1, A2, A3 = 1.5, -0.15, 1.0 / 90.0
VMEM_LIMIT = 16 * 1024 * 1024
ENCODE_LIMIT = 63 * 1024 * 1024

SERIES = [2.0 * (-1.0) ** k / math.factorial(2 * k + 2) for k in range(10)]


def series(u, terms):
    total = jnp.full_like(u, SERIES[terms - 1])
    for coefficient in SERIES[: terms - 1][::-1]:
        total = total * u + coefficient
    return total


def cosine_entry(freq, cell, live):
    inverse = 1.0 / live
    turn = 4.0 * live
    steps = freq * (2.0 * cell + 1.0)
    steps = steps - turn * jnp.floor((steps + 0.5) * (0.25 * inverse))
    steps = jnp.minimum(steps, turn - steps)
    flip = steps > live
    steps = jnp.where(flip, 2.0 * live - steps, steps)
    angle = (0.5 * math.pi) * (steps * inverse)
    u = angle * angle
    value = 1.0 - 0.5 * u * series(u, 7)
    value = jnp.where(flip, -value, value)
    weight = jnp.sqrt(jnp.where(freq == 0.0, 1.0, 2.0) * inverse)
    return jnp.where((freq < live) & (cell < live), weight * value, 0.0)


def z_table(live_z, to_cells):
    shape = (SIDE, LANES)
    row = lax.broadcasted_iota(jnp.int32, shape, 0).astype(jnp.float32)
    lane = lax.broadcasted_iota(jnp.int32, shape, 1)
    column = (lane % SIDE).astype(jnp.float32)
    freq, cell = (column, row) if to_cells else (row, column)
    table = cosine_entry(freq, cell, jnp.full(shape, live_z, jnp.float32))
    high = table.astype(jnp.bfloat16).astype(jnp.float32)
    return jnp.where(lane < LANES // 2, high, table - high).astype(jnp.bfloat16)


def z_apply(table, parts):
    values = jnp.concatenate(parts, axis=1)
    high = values.astype(jnp.bfloat16)
    low = (values - high.astype(jnp.float32)).astype(jnp.bfloat16)
    stacked = jnp.concatenate([high, low, high, low], axis=0)
    both = jnp.dot(table, stacked, preferred_element_type=jnp.float32)
    first = even_group((SIDE, LANES))
    return [
        jnp.where(
            first,
            both[:SIDE, i * LANES : (i + 1) * LANES],
            both[SIDE:, i * LANES : (i + 1) * LANES],
        )
        for i in range(len(parts))
    ]


def live(extents, rect, which):
    return extents[which, rect].astype(jnp.float32)


def lanes_of(shape):
    return lax.broadcasted_iota(jnp.int32, shape, len(shape) - 1)


def left_half(shape):
    return lanes_of(shape) < LANES // 2


def even_group(shape):
    return (lanes_of(shape) // SIDE) % 2 == 0


def regroup(tiles):
    left, even = left_half(tiles[0].shape), even_group(tiles[0].shape)
    half = [None] * 4
    for i in range(2):
        a, b = tiles[i], tiles[i + 2]
        half[i] = jnp.where(left, a, pltpu.roll(b, 64, 1))
        half[i + 2] = jnp.where(left, pltpu.roll(a, 64, 1), b)
    out = [None] * 4
    for i in (0, 2):
        a, b = half[i], half[i + 1]
        out[i] = jnp.where(even, a, pltpu.roll(b, 32, 1))
        out[i + 1] = jnp.where(even, pltpu.roll(a, 96, 1), b)
    return out


def encode_kernel(part, now, out, held, made, arrived, sent):
    inward = [
        pltpu.make_async_copy(now.at[:, i], held.at[i], arrived.at[i]) for i in range(PAIRS)
    ]
    outward = [
        pltpu.make_async_copy(made.at[i], out.at[:, i], sent.at[i]) for i in range(PAIRS)
    ]
    for copy in inward:
        copy.start()
    for pair in range(PAIRS):
        inward[pair].wait()
        for chip in range(8):
            lanes = slice(chip * LANES, chip * LANES + LANES)
            tiles = [
                held[pair, h, parity * SIDE : (parity + 1) * SIDE, lanes]
                for parity in range(2)
                for h in range(2)
            ]
            tiles = regroup(tiles)
            for core in range(2):
                made[pair, 2 * chip + core] = tiles[2 * core + part]
        outward[pair].start()
    for copy in outward:
        copy.wait()


def plan_kernel(extents, partner, offset, y_tables, to_cells, to_modes, masks, places):
    region = lax.axis_index("region")
    count = lax.axis_size("region")
    first = region * OWN
    total = count * OWN
    shape = (48, LANES)
    index = lax.broadcasted_iota(jnp.int32, shape, 0)
    parity = lanes_of(shape) // (2 * SIDE)
    even = even_group(shape)
    freq = (2 * (index % 16) + parity).astype(jnp.float32)
    cell = (index // 16).astype(jnp.float32)
    for pair in range(PAIRS):
        one, two = first + pair, first + pair + PAIRS
        live_y = jnp.where(even, live(extents, one, 0), live(extents, two, 0))
        y_tables[pair] = cosine_entry(freq, cell, live_y)
        for h, rect in ((0, one), (1, two)):
            live_z = live(extents, rect, 1)
            to_cells[pair, h * SIDE : (h + 1) * SIDE] = z_table(live_z, True)
            to_modes[pair, h * SIDE : (h + 1) * SIDE] = z_table(live_z, False)
    lower_of = [jnp.int32(0)] * OWN
    for w in range(3 * OWN):
        rect = lax.rem(first + total + w - OWN, total)
        target = partner[rect] - first
        for r in range(OWN):
            lower_of[r] = jnp.where(target == r, rect, lower_of[r])
    z = lax.broadcasted_iota(jnp.int32, (SIDE, LANES), 0)
    group = lanes_of((SIDE, LANES)) // SIDE
    for pair in range(PAIRS):
        mask = jnp.zeros((SIDE, LANES), jnp.float32)
        for face in range(2):
            for half in range(2):
                r = pair + PAIRS * half
                rect = first + r
                if face == 1:
                    other = partner[rect]
                    shift = offset[rect]
                else:
                    other = lower_of[r]
                    shift = -offset[other]
                place = lax.div(other, OWN)
                slot = other - place * OWN
                side = lax.div(slot, PAIRS)
                to = 2 * face + half
                at = 3 * (4 * pair + to)
                places[at] = lax.rem(place - region + 1 + count, count) * PAIRS + slot - side * PAIRS
                places[at + 1] = lax.rem(shift + SIDE, SIDE)
                places[at + 2] = lax.rem((to - 2 * (1 - face) - side + 4) * SIDE, LANES)
                source = z - shift
                inside = (source >= 0) & (source < extents[1, other]) & (z < extents[1, rect])
                mask = jnp.where((group == to) & inside, 1.0, mask)
        masks[pair] = mask


def free_kernel(extents, now, previous, base, gain):
    first = lax.axis_index("region") * OWN
    line = lax.axis_index("line")
    row = lax.broadcasted_iota(jnp.int32, (2 * SIDE, 256), 0)
    freq_y = (2 * line + row // SIDE).astype(jnp.float32)
    freq_z = (row % SIDE).astype(jnp.float32)
    column = lax.broadcasted_iota(jnp.int32, (1, 256), 1)
    quarter = (0.5 * math.pi) ** 2
    for r in range(OWN):
        h, pair = r // PAIRS, r % PAIRS
        live_y = live(extents, first + r, 0)
        live_z = live(extents, first + r, 1)
        y = freq_y / live_y
        z = freq_z / live_z
        across = quarter * (y * y + z * z)
        active = (freq_y < live_y) & (freq_z < live_z)
        for chunk in range(4):
            lanes = slice(chunk * 256, chunk * 256 + 256)
            x = (column + chunk * 256).astype(jnp.float32) * (1.0 / 1024.0)
            u = across + quarter * (x * x)
            s = series(u, 9)
            stepped = (2.0 - u * s) * now[h, pair, :, lanes] - previous[h, pair, :, lanes]
            base[h, pair, :, lanes] = jnp.where(active, stepped, 0.0)
            gain[h, pair, :, lanes] = jnp.where(active, 0.25 * s, 0.0)


def fold(packed):
    swapped = pltpu.roll(packed, LANES // 2, 1)
    return jnp.where(left_half(packed.shape), packed + swapped, swapped - packed)


def rows_kernel(tables, to_cells, modes, rows):
    for pair in range(PAIRS):
        totals = [None] * 3
        for source in range(16):
            block = modes[source, pair]
            for e in range(3):
                at = e * 16 + source
                term = tables[pair, at : at + 1] * block
                totals[e] = term if totals[e] is None else totals[e] + term
        for e, cells in enumerate(z_apply(to_cells[pair], [fold(t) for t in totals])):
            rows[pair, e] = cells


def spread(d):
    return [A1 * d[0] + A2 * d[1] + A3 * d[2], A2 * d[0] + A3 * d[1], A3 * d[0]]


def force_kernel(places, tables, to_modes, masks, own, up, down, out, near):
    for pair in range(PAIRS):
        near[pair] = down[pair]
        near[PAIRS + pair] = own[pair]
        near[2 * PAIRS + pair] = up[pair]
    group = lanes_of((3, SIDE, LANES)) // SIDE
    for pair in range(PAIRS):
        both = None
        for to in range(4):
            at = 3 * (4 * pair + to)
            cells = pltpu.roll(near[places[at]], places[at + 1], 1)
            cells = pltpu.roll(cells, places[at + 2], 2)
            both = cells if both is None else jnp.where(group == to, cells, both)
        mask = masks[pair]
        parts = spread([mask * (both[e] - own[pair, e]) for e in range(3)])
        parts = z_apply(to_modes[pair], [fold(part) for part in parts])
        for target in range(16):
            value = None
            for e in range(3):
                at = e * 16 + target
                term = tables[pair, at : at + 1] * parts[e]
                value = term if value is None else value + term
            out[target, pair] = value


def update_kernel(mixed_one, mixed_two, base, gain, out, made, sent):
    copies = []
    for pair in range(PAIRS):
        for chip in range(8):
            lanes = slice(chip * LANES, chip * LANES + LANES)
            tiles = regroup(
                [mixed[2 * chip + core, pair] for core in range(2) for mixed in (mixed_one, mixed_two)]
            )
            for parity in range(2):
                modes = slice(parity * SIDE, parity * SIDE + SIDE)
                for h in range(2):
                    made[pair, h, modes, lanes] = (
                        base[h, pair, modes, lanes]
                        + gain[h, pair, modes, lanes] * tiles[2 * parity + h]
                    )
        copies.append(pltpu.make_async_copy(made.at[pair], out.at[:, pair], sent.at[pair]))
        copies[-1].start()
    for copy in copies:
        copy.wait()


def smem():
    return pl.BlockSpec(memory_space=pltpu.SMEM)


def vmem():
    return pl.BlockSpec(memory_space=pltpu.VMEM)


def hbm():
    return pl.BlockSpec(memory_space=pltpu.HBM)


def cost(flops, nbytes):
    return pl.CostEstimate(flops=flops, bytes_accessed=nbytes, transcendentals=0)


def shards(modes_now, modes_prev, extents, partner, offset):
    f32 = jnp.float32
    extents = extents.T
    now = modes_now.reshape(2, PAIRS, 2 * SIDE, 1024)
    previous = modes_prev.reshape(2, PAIRS, 2 * SIDE, 1024)
    nbytes = now.size * 4
    wide_shape = jax.ShapeDtypeStruct(now.shape, f32)
    packed_shape = jax.ShapeDtypeStruct((16, PAIRS, SIDE, LANES), f32)
    rows_shape = jax.ShapeDtypeStruct((PAIRS, 3, SIDE, LANES), f32)
    table_shape = jax.ShapeDtypeStruct((PAIRS, 2 * SIDE, LANES), jnp.bfloat16)
    params = pltpu.CompilerParams(vmem_limit_bytes=VMEM_LIMIT)
    wide_scratch = pltpu.VMEM((PAIRS, 2, 2 * SIDE, 1024), f32)
    copied = pltpu.SemaphoreType.DMA((PAIRS,))
    count = lax.axis_size("region")
    upward = [((i + 1) % count, i) for i in range(count)]
    downward = [(i, (i + 1) % count) for i in range(count)]

    with jax.named_scope("plan"):
        y_tables, to_cells, to_modes, masks, places = pl.pallas_call(
            plan_kernel,
            out_shape=(
                jax.ShapeDtypeStruct((PAIRS, 48, LANES), f32),
                table_shape,
                table_shape,
                jax.ShapeDtypeStruct((PAIRS, SIDE, LANES), f32),
                jax.ShapeDtypeStruct((36,), jnp.int32),
            ),
            in_specs=[smem(), smem(), smem()],
            out_specs=(vmem(), vmem(), vmem(), vmem(), smem()),
            compiler_params=params,
            cost_estimate=cost(10**8, 10**6),
        )(extents, partner, offset)

    def encode(part):
        with jax.named_scope("encode"):
            return pl.pallas_call(
                functools.partial(encode_kernel, part),
                out_shape=packed_shape,
                in_specs=[hbm()],
                out_specs=hbm(),
                scratch_shapes=[
                    wide_scratch,
                    pltpu.VMEM((PAIRS, 16, SIDE, LANES), f32),
                    copied,
                    copied,
                ],
                compiler_params=pltpu.CompilerParams(vmem_limit_bytes=ENCODE_LIMIT),
                cost_estimate=cost(10**6, 2 * nbytes),
            )(now)

    def rows_of(held):
        with jax.named_scope("rows"):
            return pl.pallas_call(
                rows_kernel,
                out_shape=rows_shape,
                in_specs=[vmem()] * 3,
                out_specs=vmem(),
                compiler_params=params,
                cost_estimate=cost(10**7, nbytes),
            )(y_tables, to_cells, held)

    def force(rows, up, down):
        with jax.named_scope("force"):
            return pl.pallas_call(
                force_kernel,
                out_shape=packed_shape,
                in_specs=[smem()] + [vmem()] * 6,
                out_specs=vmem(),
                scratch_shapes=[pltpu.VMEM((3 * PAIRS, 3, SIDE, LANES), f32)],
                compiler_params=params,
                cost_estimate=cost(10**7, nbytes),
            )(places, y_tables, to_modes, masks, rows, up, down)

    def exchange(blocks):
        return lax.all_to_all(blocks, "line", 0, 0, tiled=True)

    def halo(rows):
        return lax.ppermute(rows, "region", upward), lax.ppermute(rows, "region", downward)

    sent_one = encode(0)
    held_one = exchange(sent_one)
    sent_two = encode(1)
    held_two = exchange(sent_two)
    rows_one = rows_of(held_one)
    up_one, down_one = halo(rows_one)
    with jax.named_scope("free"):
        base, gain = pl.pallas_call(
            free_kernel,
            out_shape=(wide_shape, wide_shape),
            in_specs=[smem(), vmem(), vmem()],
            out_specs=(vmem(), vmem()),
            compiler_params=params,
            cost_estimate=cost(10**9, 4 * nbytes),
        )(extents, *lax.optimization_barrier((now, previous, rows_one))[:2])
    down_one, base, gain = lax.optimization_barrier((down_one, base, gain))
    mixed_one = exchange(force(rows_one, up_one, down_one))
    rows_two = rows_of(held_two)
    up_two, down_two = halo(rows_two)
    mixed_two = exchange(force(rows_two, up_two, down_two))
    with jax.named_scope("update"):
        result = pl.pallas_call(
            update_kernel,
            out_shape=wide_shape,
            in_specs=[vmem()] * 4,
            out_specs=hbm(),
            scratch_shapes=[wide_scratch, copied],
            compiler_params=params,
            cost_estimate=cost(10**7, 4 * nbytes),
        )(mixed_one, mixed_two, base, gain)
    return result.reshape(modes_now.shape)


def solution(mesh):
    return jax.shard_map(
        shards,
        mesh=mesh,
        in_specs=(P("region", "line", None), P("region", "line", None), P(), P(), P()),
        out_specs=P("region", "line", None),
        check_vma=False,
    )
```

time: 125 us -> 121 us (0.968)
  starting transfers between devices: 23.5 us -> 43.5 us
  blocking collectives: 44.1 us -> 25.9 us
  waiting for transfers between devices: 45.1 us -> 28.8 us
  Pallas kernels: 10.4 us -> 16.3 us
  local copies, waits for them, and re-layouts: 1.43 us -> 6.02 us
    all_to_all x1, blocking collectives: 44.1 us -> 25.9 us  [exchange(): return lax.all_to_all(blocks, 'line', 0, 0, tiled=True)]
    all_to_all x1 -> x3, waiting for transfers between devices: 36.5 us -> 25.4 us  [exchange(): return lax.all_to_all(blocks, 'line', 0, 0, tiled=True)]
    ppermute x2 -> x4, starting transfers between devices: 13 us -> 23.9 us  [the longest x2 19.7 us: halo(): lax.ppermute(rows, 'region', upward)]
    all_to_all x1 -> x3, starting transfers between devices: 10.5 us -> 19.6 us  [exchange(): return lax.all_to_all(blocks, 'line', 0, 0, tiled=True)]
    pallas_call x5 -> x8, Pallas kernels: 8.34 us -> 14.2 us  [the longest x2 6.36 us: encode(): pl.pallas_call(functools.partial(encode_kernel, part), out_shape=packed_s...]
    ppermute x2 -> x4, waiting for transfers between devices: 8.6 us -> 3.43 us  [the longest x2 2.34 us: halo(): lax.ppermute(rows, 'region', downward)]
    unnamed x10 -> x24, local copies, waits for them, and re-layouts: 1.43 us -> 6.02 us
  transfers between devices with their start and end apart: 3 -> 7, of which waited for: 3 -> 5; matrix products, arithmetic and copies ran while one was open for 0% -> 0% of each run, Pallas kernels for 3% -> 8%
where the time goes in v4:
time: 121 us
  starting transfers between devices  43.5 us (36%)
  waiting for transfers between devices  28.8 us (24%)
  blocking collectives  25.9 us (21%)
  Pallas kernels  16.3 us (13%)
  local copies, waits for them, and re-layouts  6.02 us (5%)
    all_to_all x1, blocking collectives, exchange(): return lax.all_to_all(blocks, 'line', 0, 0, tiled=True)  25.9 us
    all_to_all x3, waiting for transfers between devices, exchange(): return lax.all_to_all(blocks, 'line', 0, 0, tiled=True)  25.4 us
    ppermute x2, starting transfers between devices, halo(): lax.ppermute(rows, 'region', upward)  19.7 us
    all_to_all x3, starting transfers between devices, exchange(): return lax.all_to_all(blocks, 'line', 0, 0, tiled=True)  19.6 us
    pallas_call x2, Pallas kernels, encode(): pl.pallas_call(functools.partial(encode_kernel, part), out_shape=packed_s...  6.36 us
    unnamed x24, local copies, waits for them, and re-layouts  6.02 us
    ppermute x2, starting transfers between devices, halo(): lax.ppermute(rows, 'region', downward)  4.22 us
    pallas_call x1, Pallas kernels, shards(): pl.pallas_call(update_kernel, out_shape=wide_shape, in_specs=[vmem()] * 4...  2.96 us
  transfers between devices with their start and end apart: 7, of which 5 were waited for; matrix products, arithmetic and copies ran while one was open for 0% of the time, Pallas kernels for 8%

profile of v4, /device:TPU:1, one launch (start us, length us, event | category | flops | bytes accessed | tf_op | source)
XLA Modules:
  0.0 120.7 jit_solution(6583316916082770792)
XLA Ops:
  0.0 3.1 %encode.3 = f32[16,3,32,128]{3,2,1,0:T(8,128)} custom-call(f32[2,3,64,1024]{3,2,1,0:T(8,128)} %bitcast.4), custom_call_target="tpu_custom_call" | custom-call | flops 1000000 | bytes 3145728 | tf_op jit(solution)/shard_map/encode/pallas_call | solution.py:328
  3.1 10.3 %all-to-all-start.2 = ((f32[16,3,32,128]{3,2,1,0:T(8,128)}), f32[16,3,32,128]{3,2,1,0:T(8,128)S(1)}, u32[]{:S(2)}, u32[]{:S(2)}) async-start(f32[16,3,32,128]{3,2,1,0:T(8,128)} %encode.3), calls=%async_computation.2 | async-start | bytes 1572864 | tf_op jit(solution)/shard_map/all_to_all | solution.py:367
  13.4 0.0 copy-start.9
  13.4 0.0 copy-start.10
  13.4 0.0 copy-start.11
  13.5 3.2 %encode.2 = f32[16,3,32,128]{3,2,1,0:T(8,128)} custom-call(f32[2,3,64,1024]{3,2,1,0:T(8,128)} %bitcast.5), custom_call_target="tpu_custom_call" | custom-call | flops 1000000 | bytes 3145728 | tf_op jit(solution)/shard_map/encode/pallas_call | solution.py:328
  16.7 19.4 %all-to-all-done.2.modes = f32[16,3,32,128]{3,2,1,0:T(8,128)S(1)} async-done(((f32[16,3,32,128]{3,2,1,0:T(8,128)}), f32[16,3,32,128]{3,2,1,0:T(8,128)S(1)}, u32[]{:S(2)}, u32[]{:S(2)}) %all-to-all-start.2) | async-done | bytes 786464 | tf_op jit(solution)/shard_map/all_to_all | solution.py:367
  36.1 3.5 %all-to-all-start = ((f32[16,3,32,128]{3,2,1,0:T(8,128)}), f32[16,3,32,128]{3,2,1,0:T(8,128)S(1)}, u32[]{:S(2)}, u32[]{:S(2)}) async-start(f32[16,3,32,128]{3,2,1,0:T(8,128)} %encode.2), calls=%async_computation | async-start | bytes 1572864 | tf_op jit(solution)/shard_map/all_to_all | solution.py:367
  39.7 0.0 copy-done.9
  39.7 0.0 copy-done.10
  39.7 0.0 copy-done.11
  39.7 1.8 %plan.1 = (f32[3,48,128]{2,1,0:T(8,128)S(1)}, bf16[3,64,128]{2,1,0:T(8,128)(2,1)S(1)}, bf16[3,64,128]{2,1,0:T(8,128)(2,1)S(1)}, f32[3,32,128]{2,1,0:T(8,128)S(1)}, s32[36]{0:T(128)S(1)}) custom-call(s32[2,192]{1,0:T(2,128)S(1)} %bitcast.8, s32[192]{0:T(256)S(1)} %copy-done.10, s32[192]{0:T(256)S(1)} %copy-done.11), custom_call_target="tpu_custom_call" | custom-call | flops 100000000 | bytes 1000000 | tf_op jit(solution)/shard_map/plan/pallas_call | solution.py:311
  41.5 0.0 copy-start.6
  41.5 0.4 rows.3.own
  41.9 2.3 %collective-permute-start.3 = (f32[3,3,32,128]{3,2,1,0:T(8,128)S(1)}, f32[3,3,32,128]{3,2,1,0:T(8,128)S(1)}, u32[]{:S(2)}, u32[]{:S(2)}) collective-permute-start(f32[3,3,32,128]{3,2,1,0:T(8,128)S(1)} %rows.3.own), channel_id=1, source_target_pairs={{0,16},{16,32},{32,48},{48,64},{64,80},{80,96},{96,112},{112,128},... | collective-permute-start | bytes 442376 | tf_op jit(solution)/shard_map/ppermute | solution.py:370
  44.2 10.8 %collective-permute-start.2 = (f32[3,3,32,128]{3,2,1,0:T(8,128)S(1)}, f32[3,3,32,128]{3,2,1,0:T(8,128)S(1)}, u32[]{:S(2)}, u32[]{:S(2)}) collective-permute-start(f32[3,3,32,128]{3,2,1,0:T(8,128)S(1)} %rows.3.own), channel_id=1, source_target_pairs={{16,0},{32,16},{48,32},{64,48},{80,64},{96,80},{112,96},{128,112},... | collective-permute-start | bytes 442376 | tf_op jit(solution)/shard_map/ppermute | solution.py:370
  55.0 2.3 %collective-permute-done.3.down = f32[3,3,32,128]{3,2,1,0:T(8,128)S(1)} collective-permute-done((f32[3,3,32,128]{3,2,1,0:T(8,128)S(1)}, f32[3,3,32,128]{3,2,1,0:T(8,128)S(1)}, u32[]{:S(2)}, u32[]{:S(2)}) %collective-permute-start.3) | collective-permute-done | bytes 147488 | tf_op jit(solution)/shard_map/ppermute | solution.py:370
  57.4 1.1 collective-permute-done.2.up
  58.4 0.0 copy-done.6
  58.4 0.0 copy-start.7
  58.4 1.1 force.3
  59.6 0.0 copy-start.1
  59.6 0.9 copy-done.1
  60.5 0.0 copy-start
  60.5 1.5 %all-to-all-done.modes = f32[16,3,32,128]{3,2,1,0:T(8,128)S(1)} async-done(((f32[16,3,32,128]{3,2,1,0:T(8,128)}), f32[16,3,32,128]{3,2,1,0:T(8,128)S(1)}, u32[]{:S(2)}, u32[]{:S(2)}) %all-to-all-start) | async-done | bytes 786464 | tf_op jit(solution)/shard_map/all_to_all | solution.py:367
  62.0 5.8 %all-to-all-start.3 = ((f32[16,3,32,128]{3,2,1,0:T(8,128)}), f32[16,3,32,128]{3,2,1,0:T(8,128)S(1)}, u32[]{:S(2)}, u32[]{:S(2)}) async-start(f32[16,3,32,128]{3,2,1,0:T(8,128)} %copy-done.1), calls=%async_computation.3 | async-start | bytes 1572864 | tf_op jit(solution)/shard_map/all_to_all | solution.py:367
  67.8 0.0 copy-done.7
  67.8 0.4 rows.2.own
  68.2 1.9 %collective-permute-start.1 = (f32[3,3,32,128]{3,2,1,0:T(8,128)S(1)}, f32[3,3,32,128]{3,2,1,0:T(8,128)S(1)}, u32[]{:S(2)}, u32[]{:S(2)}) collective-permute-start(f32[3,3,32,128]{3,2,1,0:T(8,128)S(1)} %rows.2.own), channel_id=1, source_target_pairs={{0,16},{16,32},{32,48},{48,64},{64,80},{80,96},{96,112},{112,128},... | collective-permute-start | bytes 442376 | tf_op jit(solution)/shard_map/ppermute | solution.py:370
  70.1 8.9 %collective-permute-start = (f32[3,3,32,128]{3,2,1,0:T(8,128)S(1)}, f32[3,3,32,128]{3,2,1,0:T(8,128)S(1)}, u32[]{:S(2)}, u32[]{:S(2)}) collective-permute-start(f32[3,3,32,128]{3,2,1,0:T(8,128)S(1)} %rows.2.own), channel_id=1, source_target_pairs={{16,0},{32,16},{48,32},{64,48},{80,64},{96,80},{112,96},{128,112},... | collective-permute-start | bytes 442376 | tf_op jit(solution)/shard_map/ppermute | solution.py:370
  79.0 0.0 copy-done
  79.0 0.0 copy-start.8
  79.1 1.4 %copy-done.8 = f32[6,64,1024]{2,1,0:T(8,128)S(1)} copy-done((f32[6,64,1024]{2,1,0:T(8,128)S(1)}, f32[6,64,1024]{2,1,0:T(8,128)}, u32[]{:S(2)}) %copy-start.8) | copy-done | bytes 1572888
  80.5 2.0 %free.1 = (f32[2,3,64,1024]{3,2,1,0:T(8,128)S(1)}, f32[2,3,64,1024]{3,2,1,0:T(8,128)S(1)}) custom-call(s32[2,192]{1,0:T(2,128)S(1)} %bitcast.9, f32[2,3,64,1024]{3,2,1,0:T(8,128)S(1)} %bitcast.6, f32[2,3,64,1024]{3,2,1,0:T(8,128)S(1)} %bitcast.7), custom_call_target="tpu_custom_call" | custom-call | flops 1000000000 | bytes 6291456 | tf_op jit(solution)/shard_map/free/pallas_call | solution.py:379
  82.5 0.0 copy-start.2
  82.5 1.1 copy-done.2
  83.6 0.0 copy-start.4
  83.6 1.2 copy-done.4
  84.8 0.0 collective-permute-done.1.down
  84.8 0.0 copy-start.3
  84.8 0.0 collective-permute-done.up
  84.8 1.1 force.2
  85.9 4.5 %all-to-all-done.3.mixed_two = f32[16,3,32,128]{3,2,1,0:T(8,128)S(1)} async-done(((f32[16,3,32,128]{3,2,1,0:T(8,128)}), f32[16,3,32,128]{3,2,1,0:T(8,128)S(1)}, u32[]{:S(2)}, u32[]{:S(2)}) %all-to-all-start.3) | async-done | bytes 786464 | tf_op jit(solution)/shard_map/all_to_all | solution.py:367
  90.4 25.9 %all_to_all.20.mixed_one = f32[16,3,32,128]{3,2,1,0:T(8,128)S(1)} all-to-all(f32[16,3,32,128]{3,2,1,0:T(8,128)S(1)} %force.2), channel_id=1, replica_groups=mesh['region'=32,'line'=16] {'line'}, dimensions={0} | all-to-all | bytes 1572864 | tf_op jit(solution)/shard_map/all_to_all | solution.py:367
  116.3 0.0 copy-done.3
  116.3 0.0 copy-start.5
  116.3 1.4 %copy-done.5 = f32[2,3,64,1024]{3,2,1,0:T(8,128)S(1)} copy-done((f32[2,3,64,1024]{3,2,1,0:T(8,128)S(1)}, f32[2,3,64,1024]{3,2,1,0:T(8,128)}, u32[]{:S(2)}) %copy-start.5) | copy-done | bytes 1572888
  117.7 3.0 %update.1 = f32[2,3,64,1024]{3,2,1,0:T(8,128)} custom-call(f32[16,3,32,128]{3,2,1,0:T(8,128)S(1)} %all_to_all.20.mixed_one, f32[16,3,32,128]{3,2,1,0:T(8,128)S(1)} %all-to-all-done.3.mixed_two, f32[2,3,64,1024]{3,2,1,0:T(8,128)S(1)} %copy-done.3, f32[2,3,64,1024]{3,2,1,0:T(8,128)S(1)} %copy-done.5), custom_call_target="tpu_custom_call" | custom-call | flops 10000000 | bytes 6291456 | tf_op jit(solution)/shard_map/update/pallas_call | solution.py:393
Async XLA Ops:
  3.1 33.0 %all-to-all-start.2 = ((f32[16,3,32,128]{3,2,1,0:T(8,128)}), f32[16,3,32,128]{3,2,1,0:T(8,128)S(1)}, u32[]{:S(2)}, u32[]{:S(2)}) async-start(f32[16,3,32,128]{3,2,1,0:T(8,128)} %encode.3), calls=%async_computation.2 | async-start | bytes 1572864 | tf_op jit(solution)/shard_map/all_to_all | solution.py:367
  13.4 26.2 %copy-start.9 = (s32[192,2]{0,1:T(2,128)S(1)}, s32[192,2]{0,1:T(2,128)}, u32[]{:S(2)}) copy-start(s32[192,2]{0,1:T(2,128)} %param.7) | copy-start | bytes 4612
  13.4 26.2 %copy-start.10 = (s32[192]{0:T(256)S(1)}, s32[192]{0:T(256)}, u32[]{:S(2)}) copy-start(s32[192]{0:T(256)} %partner.1) | copy-start | bytes 2308
  13.4 26.2 %copy-start.11 = (s32[192]{0:T(256)S(1)}, s32[192]{0:T(256)}, u32[]{:S(2)}) copy-start(s32[192]{0:T(256)} %offset.1) | copy-start | bytes 2308
  36.1 25.8 %all-to-all-start = ((f32[16,3,32,128]{3,2,1,0:T(8,128)}), f32[16,3,32,128]{3,2,1,0:T(8,128)S(1)}, u32[]{:S(2)}, u32[]{:S(2)}) async-start(f32[16,3,32,128]{3,2,1,0:T(8,128)} %encode.2), calls=%async_computation | async-start | bytes 1572864 | tf_op jit(solution)/shard_map/all_to_all | solution.py:367
  41.5 17.0 %copy-start.6 = (bf16[3,64,128]{2,1,0:T(8,128)(2,1)}, bf16[3,64,128]{2,1,0:T(8,128)(2,1)S(1)}, u32[]{:S(2)}) copy-start(bf16[3,64,128]{2,1,0:T(8,128)(2,1)S(1)} %get-tuple-element.21.to_cells) | copy-start | bytes 147460
  41.9 15.4 %collective-permute-start.3 = (f32[3,3,32,128]{3,2,1,0:T(8,128)S(1)}, f32[3,3,32,128]{3,2,1,0:T(8,128)S(1)}, u32[]{:S(2)}, u32[]{:S(2)}) collective-permute-start(f32[3,3,32,128]{3,2,1,0:T(8,128)S(1)} %rows.3.own), channel_id=1, source_target_pairs={{0,16},{16,32},{32,48},{48,64},{64,80},{80,96},{96,112},{112,128},... | collective-permute-start | bytes 442376 | tf_op jit(solution)/shard_map/ppermute | solution.py:370
  44.2 14.2 %collective-permute-start.2 = (f32[3,3,32,128]{3,2,1,0:T(8,128)S(1)}, f32[3,3,32,128]{3,2,1,0:T(8,128)S(1)}, u32[]{:S(2)}, u32[]{:S(2)}) collective-permute-start(f32[3,3,32,128]{3,2,1,0:T(8,128)S(1)} %rows.3.own), channel_id=1, source_target_pairs={{16,0},{32,16},{48,32},{64,48},{80,64},{96,80},{112,96},{128,112},... | collective-permute-start | bytes 442376 | tf_op jit(solution)/shard_map/ppermute | solution.py:370
  58.4 9.3 %copy-start.7 = (bf16[3,64,128]{2,1,0:T(8,128)(2,1)S(1)}, bf16[3,64,128]{2,1,0:T(8,128)(2,1)}, u32[]{:S(2)}) copy-start(bf16[3,64,128]{2,1,0:T(8,128)(2,1)} %copy-done.6) | copy-start | bytes 147460
  59.6 0.9 copy-start.1
  60.5 18.6 %copy-start = (f32[6,64,1024]{2,1,0:T(8,128)S(1)}, f32[6,64,1024]{2,1,0:T(8,128)}, u32[]{:S(2)}) copy-start(f32[6,64,1024]{2,1,0:T(8,128)} %param.5) | copy-start | bytes 4718596
  62.0 28.4 %all-to-all-start.3 = ((f32[16,3,32,128]{3,2,1,0:T(8,128)}), f32[16,3,32,128]{3,2,1,0:T(8,128)S(1)}, u32[]{:S(2)}, u32[]{:S(2)}) async-start(f32[16,3,32,128]{3,2,1,0:T(8,128)} %copy-done.1), calls=%async_computation.3 | async-start | bytes 1572864 | tf_op jit(solution)/shard_map/all_to_all | solution.py:367
  68.2 16.6 %collective-permute-start.1 = (f32[3,3,32,128]{3,2,1,0:T(8,128)S(1)}, f32[3,3,32,128]{3,2,1,0:T(8,128)S(1)}, u32[]{:S(2)}, u32[]{:S(2)}) collective-permute-start(f32[3,3,32,128]{3,2,1,0:T(8,128)S(1)} %rows.2.own), channel_id=1, source_target_pairs={{0,16},{16,32},{32,48},{48,64},{64,80},{80,96},{96,112},{112,128},... | collective-permute-start | bytes 442376 | tf_op jit(solution)/shard_map/ppermute | solution.py:370
  70.1 14.7 %collective-permute-start = (f32[3,3,32,128]{3,2,1,0:T(8,128)S(1)}, f32[3,3,32,128]{3,2,1,0:T(8,128)S(1)}, u32[]{:S(2)}, u32[]{:S(2)}) collective-permute-start(f32[3,3,32,128]{3,2,1,0:T(8,128)S(1)} %rows.2.own), channel_id=1, source_target_pairs={{16,0},{32,16},{48,32},{64,48},{80,64},{96,80},{112,96},{128,112},... | collective-permute-start | bytes 442376 | tf_op jit(solution)/shard_map/ppermute | solution.py:370
  79.0 1.4 %copy-start.8 = (f32[6,64,1024]{2,1,0:T(8,128)S(1)}, f32[6,64,1024]{2,1,0:T(8,128)}, u32[]{:S(2)}) copy-start(f32[6,64,1024]{2,1,0:T(8,128)} %param.6) | copy-start | bytes 4718596
  82.5 1.1 copy-start.2
  83.6 1.2 copy-start.4
  84.8 31.5 %copy-start.3 = (f32[2,3,64,1024]{3,2,1,0:T(8,128)S(1)}, f32[2,3,64,1024]{3,2,1,0:T(8,128)}, u32[]{:S(2)}) copy-start(f32[2,3,64,1024]{3,2,1,0:T(8,128)} %copy-done.2) | copy-start | bytes 4718596
  116.3 1.4 %copy-start.5 = (f32[2,3,64,1024]{3,2,1,0:T(8,128)S(1)}, f32[2,3,64,1024]{3,2,1,0:T(8,128)}, u32[]{:S(2)}) copy-start(f32[2,3,64,1024]{3,2,1,0:T(8,128)} %copy-done.4) | copy-start | bytes 4718596

commit v5 on v4

--- a/solution.py
+++ b/solution.py
@@ -15,6 +15,7 @@
 A1, A2, A3 = 1.5, -0.15, 1.0 / 90.0
 VMEM_LIMIT = 16 * 1024 * 1024
 ENCODE_LIMIT = 63 * 1024 * 1024
+FREE_LIMIT = 52 * 1024 * 1024
 
 SERIES = [2.0 * (-1.0) ** k / math.factorial(2 * k + 2) for k in range(10)]
 
@@ -86,19 +87,20 @@
     return (lanes_of(shape) // SIDE) % 2 == 0
 
 
-def regroup(tiles):
-    left, even = left_half(tiles[0].shape), even_group(tiles[0].shape)
-    half = [None] * 4
-    for i in range(2):
-        a, b = tiles[i], tiles[i + 2]
-        half[i] = jnp.where(left, a, pltpu.roll(b, 64, 1))
-        half[i + 2] = jnp.where(left, pltpu.roll(a, 64, 1), b)
-    out = [None] * 4
-    for i in (0, 2):
-        a, b = half[i], half[i + 1]
-        out[i] = jnp.where(even, a, pltpu.roll(b, 32, 1))
-        out[i + 1] = jnp.where(even, pltpu.roll(a, 96, 1), b)
-    return out
+def regroup(tiles, wanted=range(4)):
+    group = lanes_of(tiles[0].shape) // SIDE
+    at = [group == i for i in range(3)]
+
+    def pick(four):
+        return jnp.where(
+            at[0], four[0], jnp.where(at[1], four[1], jnp.where(at[2], four[2], four[3]))
+        )
+
+    turned = []
+    for k in range(4):
+        diagonal = pick([tiles[(g + k) % 4] for g in range(4)])
+        turned.append(pltpu.roll(diagonal, k * SIDE, 1) if k else diagonal)
+    return [pick([turned[(q - g) % 4] for q in range(4)]) for g in wanted]
 
 
 def encode_kernel(part, now, out, held, made, arrived, sent):
@@ -119,9 +121,8 @@
                 for parity in range(2)
                 for h in range(2)
             ]
-            tiles = regroup(tiles)
-            for core in range(2):
-                made[pair, 2 * chip + core] = tiles[2 * core + part]
+            for core, tile in enumerate(regroup(tiles, (part, 2 + part))):
+                made[pair, 2 * chip + core] = tile
         outward[pair].start()
     for copy in outward:
         copy.wait()
@@ -180,7 +181,23 @@
         masks[pair] = mask
 
 
-def free_kernel(extents, now, previous, base, gain):
+def free_kernel(extents, now_hbm, previous_hbm, base_hbm, gain_hbm, now, previous, base, gain, copied):
+    inward, outward = [], []
+    for h in range(2):
+        inward.append(
+            (
+                pltpu.make_async_copy(now_hbm.at[h], now.at[h], copied.at[h, 0]),
+                pltpu.make_async_copy(previous_hbm.at[h], previous.at[h], copied.at[h, 1]),
+            )
+        )
+        outward.append(
+            (
+                pltpu.make_async_copy(base.at[h], base_hbm.at[h], copied.at[h, 2]),
+                pltpu.make_async_copy(gain.at[h], gain_hbm.at[h], copied.at[h, 3]),
+            )
+        )
+        for copy in inward[h]:
+            copy.start()
     first = lax.axis_index("region") * OWN
     line = lax.axis_index("line")
     row = lax.broadcasted_iota(jnp.int32, (2 * SIDE, 256), 0)
@@ -190,6 +207,9 @@
     quarter = (0.5 * math.pi) ** 2
     for r in range(OWN):
         h, pair = r // PAIRS, r % PAIRS
+        if pair == 0:
+            for copy in inward[h]:
+                copy.wait()
         live_y = live(extents, first + r, 0)
         live_z = live(extents, first + r, 1)
         y = freq_y / live_y
@@ -204,6 +224,12 @@
             stepped = (2.0 - u * s) * now[h, pair, :, lanes] - previous[h, pair, :, lanes]
             base[h, pair, :, lanes] = jnp.where(active, stepped, 0.0)
             gain[h, pair, :, lanes] = jnp.where(active, 0.25 * s, 0.0)
+        if pair == PAIRS - 1:
+            for copy in outward[h]:
+                copy.start()
+    for copies in outward:
+        for copy in copies:
+            copy.wait()
 
 
 def fold(packed):
@@ -379,9 +405,10 @@
         base, gain = pl.pallas_call(
             free_kernel,
             out_shape=(wide_shape, wide_shape),
-            in_specs=[smem(), vmem(), vmem()],
-            out_specs=(vmem(), vmem()),
-            compiler_params=params,
+            in_specs=[smem(), hbm(), hbm()],
+            out_specs=(hbm(), hbm()),
+            scratch_shapes=[pltpu.VMEM(now.shape, f32)] * 4 + [pltpu.SemaphoreType.DMA((2, 4))],
+            compiler_params=pltpu.CompilerParams(vmem_limit_bytes=FREE_LIMIT),
             cost_estimate=cost(10**9, 4 * nbytes),
         )(extents, *lax.optimization_barrier((now, previous, rows_one))[:2])
     down_one, base, gain = lax.optimization_barrier((down_one, base, gain))

time: 121 us -> 118 us (0.975)
  local copies, waits for them, and re-layouts: 6.02 us -> 0.02 us
  waiting for transfers between devices: 28.8 us -> 30.9 us
    unnamed x24 -> x8, local copies, waits for them, and re-layouts: 6.02 us -> 0.02 us
    pallas_call x1, Pallas kernels: 2.01 us -> 4.43 us  [shards(): pl.pallas_call(free_kernel, out_shape=(wide_shape, wide_shape), in_specs=...]
    all_to_all x3, waiting for transfers between devices: 25.4 us -> 27.5 us  [exchange(): return lax.all_to_all(blocks, 'line', 0, 0, tiled=True)]
    pallas_call x2, Pallas kernels: 6.36 us -> 4.69 us  [encode(): pl.pallas_call(functools.partial(encode_kernel, part), out_shape=packed_s...]
    pallas_call x1, Pallas kernels: 2.96 us -> 1.42 us  [shards(): pl.pallas_call(update_kernel, out_shape=wide_shape, in_specs=[vmem()] * 4...]
  transfers between devices with their start and end apart: 7 -> 7, of which waited for: 5 -> 5; matrix products, arithmetic and copies ran while one was open for 0% -> 0% of each run, Pallas kernels for 8% -> 11%
where the time goes in v5:
time: 118 us; the launch traced here: 117 us
  starting transfers between devices  43.5 us (37%)
  waiting for transfers between devices  30.9 us (26%)
  blocking collectives  26 us (22%)
  Pallas kernels  16.4 us (14%)
    all_to_all x3, waiting for transfers between devices, exchange(): return lax.all_to_all(blocks, 'line', 0, 0, tiled=True)  27.5 us
    all_to_all x1, blocking collectives, exchange(): return lax.all_to_all(blocks, 'line', 0, 0, tiled=True)  26 us
    ppermute x2, starting transfers between devices, halo(): lax.ppermute(rows, 'region', upward)  19.8 us
    all_to_all x3, starting transfers between devices, exchange(): return lax.all_to_all(blocks, 'line', 0, 0, tiled=True)  19.4 us
    pallas_call x2, Pallas kernels, encode(): pl.pallas_call(functools.partial(encode_kernel, part), out_shape=packed_s...  4.69 us
    pallas_call x1, Pallas kernels, shards(): pl.pallas_call(free_kernel, out_shape=(wide_shape, wide_shape), in_specs=...  4.43 us
    ppermute x2, starting transfers between devices, halo(): lax.ppermute(rows, 'region', downward)  4.22 us
    pallas_call x2, Pallas kernels, force(): pl.pallas_call(force_kernel, out_shape=packed_shape, in_specs=[smem()] +...  3.21 us
  transfers between devices with their start and end apart: 7, of which 5 were waited for; matrix products, arithmetic and copies ran while one was open for 0% of the time, Pallas kernels for 11%

profile of v5, /device:TPU:1, one launch (start us, length us, event | category | flops | bytes accessed | tf_op | source)
XLA Modules:
  0.0 117.0 jit_solution(5084171491203130312)
XLA Ops:
  0.0 2.3 %encode.3 = f32[16,3,32,128]{3,2,1,0:T(8,128)} custom-call(f32[2,3,64,1024]{3,2,1,0:T(8,128)} %bitcast.6), custom_call_target="tpu_custom_call" | custom-call | flops 1000000 | bytes 3145728 | tf_op jit(solution)/shard_map/encode/pallas_call | solution.py:354
  2.4 10.3 %all-to-all-start.2 = ((f32[16,3,32,128]{3,2,1,0:T(8,128)}), f32[16,3,32,128]{3,2,1,0:T(8,128)S(1)}, u32[]{:S(2)}, u32[]{:S(2)}) async-start(f32[16,3,32,128]{3,2,1,0:T(8,128)} %encode.3), calls=%async_computation.2 | async-start | bytes 1572864 | tf_op jit(solution)/shard_map/all_to_all | solution.py:393
  12.6 0.0 copy-start.1
  12.7 0.0 copy-start.2
  12.7 0.0 copy-start.3
  12.7 2.3 %encode.2 = f32[16,3,32,128]{3,2,1,0:T(8,128)} custom-call(f32[2,3,64,1024]{3,2,1,0:T(8,128)} %bitcast.7), custom_call_target="tpu_custom_call" | custom-call | flops 1000000 | bytes 3145728 | tf_op jit(solution)/shard_map/encode/pallas_call | solution.py:354
  15.0 20.3 %all-to-all-done.2.modes = f32[16,3,32,128]{3,2,1,0:T(8,128)S(1)} async-done(((f32[16,3,32,128]{3,2,1,0:T(8,128)}), f32[16,3,32,128]{3,2,1,0:T(8,128)S(1)}, u32[]{:S(2)}, u32[]{:S(2)}) %all-to-all-start.2) | async-done | bytes 786464 | tf_op jit(solution)/shard_map/all_to_all | solution.py:393
  35.4 3.5 %all-to-all-start = ((f32[16,3,32,128]{3,2,1,0:T(8,128)}), f32[16,3,32,128]{3,2,1,0:T(8,128)S(1)}, u32[]{:S(2)}, u32[]{:S(2)}) async-start(f32[16,3,32,128]{3,2,1,0:T(8,128)} %encode.2), calls=%async_computation | async-start | bytes 1572864 | tf_op jit(solution)/shard_map/all_to_all | solution.py:393
  38.9 0.0 copy-done.1
  38.9 0.0 copy-done.2
  38.9 0.0 copy-done.3
  38.9 1.8 %plan.1 = (f32[3,48,128]{2,1,0:T(8,128)S(1)}, bf16[3,64,128]{2,1,0:T(8,128)(2,1)S(1)}, bf16[3,64,128]{2,1,0:T(8,128)(2,1)S(1)}, f32[3,32,128]{2,1,0:T(8,128)S(1)}, s32[36]{0:T(128)S(1)}) custom-call(s32[2,192]{1,0:T(2,128)S(1)} %bitcast.4, s32[192]{0:T(256)S(1)} %copy-done.2, s32[192]{0:T(256)S(1)} %copy-done.3), custom_call_target="tpu_custom_call" | custom-call | flops 100000000 | bytes 1000000 | tf_op jit(solution)/shard_map/plan/pallas_call | solution.py:337
  40.7 0.4 rows.3.own
  41.1 2.3 %collective-permute-start.3 = (f32[3,3,32,128]{3,2,1,0:T(8,128)S(1)}, f32[3,3,32,128]{3,2,1,0:T(8,128)S(1)}, u32[]{:S(2)}, u32[]{:S(2)}) collective-permute-start(f32[3,3,32,128]{3,2,1,0:T(8,128)S(1)} %rows.3.own), channel_id=1, source_target_pairs={{0,16},{16,32},{32,48},{48,64},{64,80},{80,96},{96,112},{112,128},... | collective-permute-start | bytes 442376 | tf_op jit(solution)/shard_map/ppermute | solution.py:396
  43.4 10.8 %collective-permute-start.2 = (f32[3,3,32,128]{3,2,1,0:T(8,128)S(1)}, f32[3,3,32,128]{3,2,1,0:T(8,128)S(1)}, u32[]{:S(2)}, u32[]{:S(2)}) collective-permute-start(f32[3,3,32,128]{3,2,1,0:T(8,128)S(1)} %rows.3.own), channel_id=1, source_target_pairs={{16,0},{32,16},{48,32},{64,48},{80,64},{96,80},{112,96},{128,112},... | collective-permute-start | bytes 442376 | tf_op jit(solution)/shard_map/ppermute | solution.py:396
  54.2 2.3 %collective-permute-done.3.down = f32[3,3,32,128]{3,2,1,0:T(8,128)S(1)} collective-permute-done((f32[3,3,32,128]{3,2,1,0:T(8,128)S(1)}, f32[3,3,32,128]{3,2,1,0:T(8,128)S(1)}, u32[]{:S(2)}, u32[]{:S(2)}) %collective-permute-start.3) | collective-permute-done | bytes 147488 | tf_op jit(solution)/shard_map/ppermute | solution.py:396
  56.6 1.1 collective-permute-done.2.up
  57.6 2.1 %force.3 = f32[16,3,32,128]{3,2,1,0:T(8,128)} custom-call(s32[36]{0:T(128)S(1)} %get-tuple-element.17.places, f32[3,48,128]{2,1,0:T(8,128)S(1)} %get-tuple-element.18.tables, bf16[3,64,128]{2,1,0:T(8,128)(2,1)S(1)} %get-tuple-element.19.to_modes, f32[3,32,128]{2,1,0:T(8,128)S(1)} %get-tuple-element.20.masks, f32[3,3,32,128]{3,2,1,0:T(8,128)S(1)} %rows.3.own, ...), custom_call_target="tpu_custom_call" | custom-call | flops 10000000 | bytes 1572864 | tf_op jit(solution)/shard_map/force/pallas_call | solution.py:382
  59.7 1.5 %all-to-all-done.modes = f32[16,3,32,128]{3,2,1,0:T(8,128)S(1)} async-done(((f32[16,3,32,128]{3,2,1,0:T(8,128)}), f32[16,3,32,128]{3,2,1,0:T(8,128)S(1)}, u32[]{:S(2)}, u32[]{:S(2)}) %all-to-all-start) | async-done | bytes 786464 | tf_op jit(solution)/shard_map/all_to_all | solution.py:393
  61.2 5.6 %all-to-all-start.3 = ((f32[16,3,32,128]{3,2,1,0:T(8,128)}), f32[16,3,32,128]{3,2,1,0:T(8,128)S(1)}, u32[]{:S(2)}, u32[]{:S(2)}) async-start(f32[16,3,32,128]{3,2,1,0:T(8,128)} %force.3), calls=%async_computation.3 | async-start | bytes 1572864 | tf_op jit(solution)/shard_map/all_to_all | solution.py:393
  66.8 0.4 rows.2.own
  67.3 1.9 %collective-permute-start.1 = (f32[3,3,32,128]{3,2,1,0:T(8,128)S(1)}, f32[3,3,32,128]{3,2,1,0:T(8,128)S(1)}, u32[]{:S(2)}, u32[]{:S(2)}) collective-permute-start(f32[3,3,32,128]{3,2,1,0:T(8,128)S(1)} %rows.2.own), channel_id=1, source_target_pairs={{0,16},{16,32},{32,48},{48,64},{64,80},{80,96},{96,112},{112,128},... | collective-permute-start | bytes 442376 | tf_op jit(solution)/shard_map/ppermute | solution.py:396
  69.2 9.0 %collective-permute-start = (f32[3,3,32,128]{3,2,1,0:T(8,128)S(1)}, f32[3,3,32,128]{3,2,1,0:T(8,128)S(1)}, u32[]{:S(2)}, u32[]{:S(2)}) collective-permute-start(f32[3,3,32,128]{3,2,1,0:T(8,128)S(1)} %rows.2.own), channel_id=1, source_target_pairs={{16,0},{32,16},{48,32},{64,48},{80,64},{96,80},{112,96},{128,112},... | collective-permute-start | bytes 442376 | tf_op jit(solution)/shard_map/ppermute | solution.py:396
  78.2 4.4 %free.1 = (f32[2,3,64,1024]{3,2,1,0:T(8,128)S(1)}, f32[2,3,64,1024]{3,2,1,0:T(8,128)}) custom-call(s32[2,192]{1,0:T(2,128)S(1)} %bitcast.5, f32[2,3,64,1024]{3,2,1,0:T(8,128)} %bitcast.8, f32[2,3,64,1024]{3,2,1,0:T(8,128)} %bitcast.9), custom_call_target="tpu_custom_call" | custom-call | flops 1000000000 | bytes 6291456 | tf_op jit(solution)/shard_map/free/pallas_call | solution.py:405
  82.7 0.0 collective-permute-done.1.down
  82.7 0.0 collective-permute-done.up
  82.7 1.1 force.2
  83.9 5.6 %all-to-all-done.3.mixed_two = f32[16,3,32,128]{3,2,1,0:T(8,128)S(1)} async-done(((f32[16,3,32,128]{3,2,1,0:T(8,128)}), f32[16,3,32,128]{3,2,1,0:T(8,128)S(1)}, u32[]{:S(2)}, u32[]{:S(2)}) %all-to-all-start.3) | async-done | bytes 786464 | tf_op jit(solution)/shard_map/all_to_all | solution.py:393
  89.5 0.0 copy-start
  89.5 26.0 %all_to_all.20.mixed_one = f32[16,3,32,128]{3,2,1,0:T(8,128)S(1)} all-to-all(f32[16,3,32,128]{3,2,1,0:T(8,128)S(1)} %force.2), channel_id=1, replica_groups=mesh['region'=32,'line'=16] {'line'}, dimensions={0} | all-to-all | bytes 1572864 | tf_op jit(solution)/shard_map/all_to_all | solution.py:393
  115.5 0.0 copy-done
  115.5 1.4 %update.1 = f32[2,3,64,1024]{3,2,1,0:T(8,128)} custom-call(f32[16,3,32,128]{3,2,1,0:T(8,128)S(1)} %all_to_all.20.mixed_one, f32[16,3,32,128]{3,2,1,0:T(8,128)S(1)} %all-to-all-done.3.mixed_two, f32[2,3,64,1024]{3,2,1,0:T(8,128)S(1)} %get-tuple-element.27.base, f32[2,3,64,1024]{3,2,1,0:T(8,128)S(1)} %copy-done), custom_call_target="tpu_custom_call" | custom-call | flops 10000000 | bytes 6291456 | tf_op jit(solution)/shard_map/update/pallas_call | solution.py:420
Async XLA Ops:
  2.4 33.0 %all-to-all-start.2 = ((f32[16,3,32,128]{3,2,1,0:T(8,128)}), f32[16,3,32,128]{3,2,1,0:T(8,128)S(1)}, u32[]{:S(2)}, u32[]{:S(2)}) async-start(f32[16,3,32,128]{3,2,1,0:T(8,128)} %encode.3), calls=%async_computation.2 | async-start | bytes 1572864 | tf_op jit(solution)/shard_map/all_to_all | solution.py:393
  12.6 26.2 %copy-start.1 = (s32[192,2]{0,1:T(2,128)S(1)}, s32[192,2]{0,1:T(2,128)}, u32[]{:S(2)}) copy-start(s32[192,2]{0,1:T(2,128)} %param.7) | copy-start | bytes 4612
  12.7 26.2 %copy-start.2 = (s32[192]{0:T(256)S(1)}, s32[192]{0:T(256)}, u32[]{:S(2)}) copy-start(s32[192]{0:T(256)} %partner.1) | copy-start | bytes 2308
  12.7 26.2 %copy-start.3 = (s32[192]{0:T(256)S(1)}, s32[192]{0:T(256)}, u32[]{:S(2)}) copy-start(s32[192]{0:T(256)} %offset.1) | copy-start | bytes 2308
  35.4 25.8 %all-to-all-start = ((f32[16,3,32,128]{3,2,1,0:T(8,128)}), f32[16,3,32,128]{3,2,1,0:T(8,128)S(1)}, u32[]{:S(2)}, u32[]{:S(2)}) async-start(f32[16,3,32,128]{3,2,1,0:T(8,128)} %encode.2), calls=%async_computation | async-start | bytes 1572864 | tf_op jit(solution)/shard_map/all_to_all | solution.py:393
  41.1 15.4 %collective-permute-start.3 = (f32[3,3,32,128]{3,2,1,0:T(8,128)S(1)}, f32[3,3,32,128]{3,2,1,0:T(8,128)S(1)}, u32[]{:S(2)}, u32[]{:S(2)}) collective-permute-start(f32[3,3,32,128]{3,2,1,0:T(8,128)S(1)} %rows.3.own), channel_id=1, source_target_pairs={{0,16},{16,32},{32,48},{48,64},{64,80},{80,96},{96,112},{112,128},... | collective-permute-start | bytes 442376 | tf_op jit(solution)/shard_map/ppermute | solution.py:396
  43.4 14.2 %collective-permute-start.2 = (f32[3,3,32,128]{3,2,1,0:T(8,128)S(1)}, f32[3,3,32,128]{3,2,1,0:T(8,128)S(1)}, u32[]{:S(2)}, u32[]{:S(2)}) collective-permute-start(f32[3,3,32,128]{3,2,1,0:T(8,128)S(1)} %rows.3.own), channel_id=1, source_target_pairs={{16,0},{32,16},{48,32},{64,48},{80,64},{96,80},{112,96},{128,112},... | collective-permute-start | bytes 442376 | tf_op jit(solution)/shard_map/ppermute | solution.py:396
  61.2 28.3 %all-to-all-start.3 = ((f32[16,3,32,128]{3,2,1,0:T(8,128)}), f32[16,3,32,128]{3,2,1,0:T(8,128)S(1)}, u32[]{:S(2)}, u32[]{:S(2)}) async-start(f32[16,3,32,128]{3,2,1,0:T(8,128)} %force.3), calls=%async_computation.3 | async-start | bytes 1572864 | tf_op jit(solution)/shard_map/all_to_all | solution.py:393
  67.3 15.4 %collective-permute-start.1 = (f32[3,3,32,128]{3,2,1,0:T(8,128)S(1)}, f32[3,3,32,128]{3,2,1,0:T(8,128)S(1)}, u32[]{:S(2)}, u32[]{:S(2)}) collective-permute-start(f32[3,3,32,128]{3,2,1,0:T(8,128)S(1)} %rows.2.own), channel_id=1, source_target_pairs={{0,16},{16,32},{32,48},{48,64},{64,80},{80,96},{96,112},{112,128},... | collective-permute-start | bytes 442376 | tf_op jit(solution)/shard_map/ppermute | solution.py:396
  69.2 13.5 %collective-permute-start = (f32[3,3,32,128]{3,2,1,0:T(8,128)S(1)}, f32[3,3,32,128]{3,2,1,0:T(8,128)S(1)}, u32[]{:S(2)}, u32[]{:S(2)}) collective-permute-start(f32[3,3,32,128]{3,2,1,0:T(8,128)S(1)} %rows.2.own), channel_id=1, source_target_pairs={{16,0},{32,16},{48,32},{64,48},{80,64},{96,80},{112,96},{128,112},... | collective-permute-start | bytes 442376 | tf_op jit(solution)/shard_map/ppermute | solution.py:396
  89.5 26.0 %copy-start = (f32[2,3,64,1024]{3,2,1,0:T(8,128)S(1)}, f32[2,3,64,1024]{3,2,1,0:T(8,128)}, u32[]{:S(2)}) copy-start(f32[2,3,64,1024]{3,2,1,0:T(8,128)} %get-tuple-element.28.gain) | copy-start | bytes 4718596

commit v6 on v5

--- a/solution.py
+++ b/solution.py
@@ -179,6 +179,13 @@
                 inside = (source >= 0) & (source < extents[1, other]) & (z < extents[1, rect])
                 mask = jnp.where((group == to) & inside, 1.0, mask)
         masks[pair] = mask
+
+
+def encode_plan_kernel(
+    extents, partner, offset, now, out, y_tables, to_cells, to_modes, masks, places, *scratch
+):
+    encode_kernel(0, now, out, *scratch)
+    plan_kernel(extents, partner, offset, y_tables, to_cells, to_modes, masks, places)
 
 
 def free_kernel(extents, now_hbm, previous_hbm, base_hbm, gain_hbm, now, previous, base, gain, copied):
@@ -333,38 +340,40 @@
     upward = [((i + 1) % count, i) for i in range(count)]
     downward = [(i, (i + 1) % count) for i in range(count)]
 
-    with jax.named_scope("plan"):
-        y_tables, to_cells, to_modes, masks, places = pl.pallas_call(
-            plan_kernel,
+    encode_scratch = [
+        wide_scratch,
+        pltpu.VMEM((PAIRS, 16, SIDE, LANES), f32),
+        copied,
+        copied,
+    ]
+    encode_params = pltpu.CompilerParams(vmem_limit_bytes=ENCODE_LIMIT)
+    with jax.named_scope("encode"):
+        sent_two = pl.pallas_call(
+            functools.partial(encode_kernel, 1),
+            out_shape=packed_shape,
+            in_specs=[hbm()],
+            out_specs=hbm(),
+            scratch_shapes=encode_scratch,
+            compiler_params=encode_params,
+            cost_estimate=cost(10**6, 2 * nbytes),
+        )(now)
+    with jax.named_scope("encode_plan"):
+        sent_one, y_tables, to_cells, to_modes, masks, places = pl.pallas_call(
+            encode_plan_kernel,
             out_shape=(
+                packed_shape,
                 jax.ShapeDtypeStruct((PAIRS, 48, LANES), f32),
                 table_shape,
                 table_shape,
                 jax.ShapeDtypeStruct((PAIRS, SIDE, LANES), f32),
                 jax.ShapeDtypeStruct((36,), jnp.int32),
             ),
-            in_specs=[smem(), smem(), smem()],
-            out_specs=(vmem(), vmem(), vmem(), vmem(), smem()),
-            compiler_params=params,
-            cost_estimate=cost(10**8, 10**6),
-        )(extents, partner, offset)
-
-    def encode(part):
-        with jax.named_scope("encode"):
-            return pl.pallas_call(
-                functools.partial(encode_kernel, part),
-                out_shape=packed_shape,
-                in_specs=[hbm()],
-                out_specs=hbm(),
-                scratch_shapes=[
-                    wide_scratch,
-                    pltpu.VMEM((PAIRS, 16, SIDE, LANES), f32),
-                    copied,
-                    copied,
-                ],
-                compiler_params=pltpu.CompilerParams(vmem_limit_bytes=ENCODE_LIMIT),
-                cost_estimate=cost(10**6, 2 * nbytes),
-            )(now)
+            in_specs=[smem(), smem(), smem(), hbm()],
+            out_specs=(hbm(), vmem(), vmem(), vmem(), vmem(), smem()),
+            scratch_shapes=encode_scratch,
+            compiler_params=encode_params,
+            cost_estimate=cost(10**6, 2 * nbytes),
+        )(extents, partner, offset, lax.optimization_barrier((now, sent_two))[0])
 
     def rows_of(held):
         with jax.named_scope("rows"):
@@ -395,9 +404,7 @@
     def halo(rows):
         return lax.ppermute(rows, "region", upward), lax.ppermute(rows, "region", downward)
 
-    sent_one = encode(0)
     held_one = exchange(sent_one)
-    sent_two = encode(1)
     held_two = exchange(sent_two)
     rows_one = rows_of(held_one)
     up_one, down_one = halo(rows_one)

time: 118 us -> 116 us (0.983)
  waiting for transfers between devices: 30.9 us -> 28.9 us
    all_to_all x3, waiting for transfers between devices: 27.5 us -> 25.5 us  [exchange(): return lax.all_to_all(blocks, 'line', 0, 0, tiled=True)]
    all_to_all x3, starting transfers between devices: 19.4 us -> 17.8 us  [exchange(): return lax.all_to_all(blocks, 'line', 0, 0, tiled=True)]
    ppermute x2, starting transfers between devices: 19.8 us -> 21.5 us  [halo(): lax.ppermute(rows, 'region', upward)]
    pallas_call x3 -> x2, Pallas kernels: 6.47 us -> 6.77 us  [the longest x1 4.42 us: shards(): pl.pallas_call(encode_plan_kernel, out_shape=(packed_shape, jax.ShapeDtyp...]
where the time goes in v6:
time: 116 us; the launch traced here: 115 us
  starting transfers between devices  43.5 us (38%)
  waiting for transfers between devices  28.9 us (25%)
  blocking collectives  26.1 us (22%)
  Pallas kernels  16.7 us (14%)
    all_to_all x1, blocking collectives, exchange(): return lax.all_to_all(blocks, 'line', 0, 0, tiled=True)  26.1 us
    all_to_all x3, waiting for transfers between devices, exchange(): return lax.all_to_all(blocks, 'line', 0, 0, tiled=True)  25.5 us
    ppermute x2, starting transfers between devices, halo(): lax.ppermute(rows, 'region', upward)  21.5 us
    all_to_all x3, starting transfers between devices, exchange(): return lax.all_to_all(blocks, 'line', 0, 0, tiled=True)  17.8 us
    pallas_call x1, Pallas kernels, shards(): pl.pallas_call(free_kernel, out_shape=(wide_shape, wide_shape), in_specs=...  4.43 us
    pallas_call x1, Pallas kernels, shards(): pl.pallas_call(encode_plan_kernel, out_shape=(packed_shape, jax.ShapeDtyp...  4.42 us
    ppermute x2, starting transfers between devices, halo(): lax.ppermute(rows, 'region', downward)  4.21 us
    pallas_call x2, Pallas kernels, force(): pl.pallas_call(force_kernel, out_shape=packed_shape, in_specs=[smem()] +...  3.19 us
  transfers between devices with their start and end apart: 7, of which 5 were waited for; matrix products, arithmetic and copies ran while one was open for 0% of the time, Pallas kernels for 11%

profile of v6, /device:TPU:1, one launch (start us, length us, event | category | flops | bytes accessed | tf_op | source)
XLA Modules:
  0.0 115.4 jit_solution(6693570610750040183)
XLA Ops:
  0.0 2.4 %encode.1 = f32[16,3,32,128]{3,2,1,0:T(8,128)} custom-call(f32[2,3,64,1024]{3,2,1,0:T(8,128)} %bitcast.6), custom_call_target="tpu_custom_call" | custom-call | flops 1000000 | bytes 3145728 | tf_op jit(solution)/shard_map/encode/pallas_call | solution.py:351
  2.4 10.3 %all-to-all-start.2 = ((f32[16,3,32,128]{3,2,1,0:T(8,128)}), f32[16,3,32,128]{3,2,1,0:T(8,128)S(1)}, u32[]{:S(2)}, u32[]{:S(2)}) async-start(f32[16,3,32,128]{3,2,1,0:T(8,128)} %encode.1), calls=%async_computation.2 | async-start | bytes 1572864 | tf_op jit(solution)/shard_map/all_to_all | solution.py:402
  12.7 4.4 %encode_plan.1 = (f32[16,3,32,128]{3,2,1,0:T(8,128)}, f32[3,48,128]{2,1,0:T(8,128)}, bf16[3,64,128]{2,1,0:T(8,128)(2,1)}, bf16[3,64,128]{2,1,0:T(8,128)(2,1)}, f32[3,32,128]{2,1,0:T(8,128)}, /*index=5*/s32[36]{0:T(128)}) custom-call(s32[2,192]{1,0:T(2,128)} %bitcast.4, s32[192]{0:T(256)} %partner.1, s32[192]{0:T(256)} %offset.1, f32[2,3,64,1024]{3,2,1,0:T(8,128)} %bitcast.7), custom_call_target="tpu_custom_call" | custom-call | flops 1000000 | bytes 3145728 | tf_op jit(solution)/shard_map/encode_plan/pallas_call | solution.py:361
  17.1 0.0 copy-start.1
  17.1 0.0 copy-start.4
  17.1 0.0 copy-start.2
  17.1 0.0 copy-start.3
  17.1 0.0 copy-start.5
  17.1 18.2 %all-to-all-done.2.modes = f32[16,3,32,128]{3,2,1,0:T(8,128)S(1)} async-done(((f32[16,3,32,128]{3,2,1,0:T(8,128)}), f32[16,3,32,128]{3,2,1,0:T(8,128)S(1)}, u32[]{:S(2)}, u32[]{:S(2)}) %all-to-all-start.2) | async-done | bytes 786464 | tf_op jit(solution)/shard_map/all_to_all | solution.py:402
  35.4 3.5 %all-to-all-start = ((f32[16,3,32,128]{3,2,1,0:T(8,128)}), f32[16,3,32,128]{3,2,1,0:T(8,128)S(1)}, u32[]{:S(2)}, u32[]{:S(2)}) async-start(f32[16,3,32,128]{3,2,1,0:T(8,128)} %get-tuple-element.25), calls=%async_computation | async-start | bytes 1572864 | tf_op jit(solution)/shard_map/all_to_all | solution.py:402
  38.9 0.0 copy-done.1
  38.9 0.0 copy-done.4
  38.9 0.4 rows.3.own
  39.3 2.3 %collective-permute-start.3 = (f32[3,3,32,128]{3,2,1,0:T(8,128)S(1)}, f32[3,3,32,128]{3,2,1,0:T(8,128)S(1)}, u32[]{:S(2)}, u32[]{:S(2)}) collective-permute-start(f32[3,3,32,128]{3,2,1,0:T(8,128)S(1)} %rows.3.own), channel_id=1, source_target_pairs={{0,16},{16,32},{32,48},{48,64},{64,80},{80,96},{96,112},{112,128},... | collective-permute-start | bytes 442376 | tf_op jit(solution)/shard_map/ppermute | solution.py:405
  41.6 10.8 %collective-permute-start.2 = (f32[3,3,32,128]{3,2,1,0:T(8,128)S(1)}, f32[3,3,32,128]{3,2,1,0:T(8,128)S(1)}, u32[]{:S(2)}, u32[]{:S(2)}) collective-permute-start(f32[3,3,32,128]{3,2,1,0:T(8,128)S(1)} %rows.3.own), channel_id=1, source_target_pairs={{16,0},{32,16},{48,32},{64,48},{80,64},{96,80},{112,96},{128,112},... | collective-permute-start | bytes 442376 | tf_op jit(solution)/shard_map/ppermute | solution.py:405
  52.4 2.3 %collective-permute-done.3.down = f32[3,3,32,128]{3,2,1,0:T(8,128)S(1)} collective-permute-done((f32[3,3,32,128]{3,2,1,0:T(8,128)S(1)}, f32[3,3,32,128]{3,2,1,0:T(8,128)S(1)}, u32[]{:S(2)}, u32[]{:S(2)}) %collective-permute-start.3) | collective-permute-done | bytes 147488 | tf_op jit(solution)/shard_map/ppermute | solution.py:405
  54.8 1.1 collective-permute-done.2.up
  55.9 0.0 copy-done.2
  55.9 0.0 copy-done.3
  55.9 0.0 copy-done.5
  55.9 2.0 %force.3 = f32[16,3,32,128]{3,2,1,0:T(8,128)} custom-call(s32[36]{0:T(128)S(1)} %copy-done.5, f32[3,48,128]{2,1,0:T(8,128)S(1)} %copy-done.1, bf16[3,64,128]{2,1,0:T(8,128)(2,1)S(1)} %copy-done.2, f32[3,32,128]{2,1,0:T(8,128)S(1)} %copy-done.3, f32[3,3,32,128]{3,2,1,0:T(8,128)S(1)} %rows.3.own, f32[3,3,32,128]{3,2,1,0:T(8,128)S(1)} %collective-permute-done.2.up, ...), custom_call_target="tpu_custom_call" | custom-call | flops 10000000 | bytes 1572864 | tf_op jit(solution)/shard_map/force/pallas_call | solution.py:391
  57.9 0.0 copy-start.6
  57.9 3.3 %all-to-all-done.modes = f32[16,3,32,128]{3,2,1,0:T(8,128)S(1)} async-done(((f32[16,3,32,128]{3,2,1,0:T(8,128)}), f32[16,3,32,128]{3,2,1,0:T(8,128)S(1)}, u32[]{:S(2)}, u32[]{:S(2)}) %all-to-all-start) | async-done | bytes 786464 | tf_op jit(solution)/shard_map/all_to_all | solution.py:402
  61.2 4.0 %all-to-all-start.3 = ((f32[16,3,32,128]{3,2,1,0:T(8,128)}), f32[16,3,32,128]{3,2,1,0:T(8,128)S(1)}, u32[]{:S(2)}, u32[]{:S(2)}) async-start(f32[16,3,32,128]{3,2,1,0:T(8,128)} %force.3), calls=%async_computation.3 | async-start | bytes 1572864 | tf_op jit(solution)/shard_map/all_to_all | solution.py:402
  65.2 0.4 rows.2.own
  65.6 1.9 %collective-permute-start.1 = (f32[3,3,32,128]{3,2,1,0:T(8,128)S(1)}, f32[3,3,32,128]{3,2,1,0:T(8,128)S(1)}, u32[]{:S(2)}, u32[]{:S(2)}) collective-permute-start(f32[3,3,32,128]{3,2,1,0:T(8,128)S(1)} %rows.2.own), channel_id=1, source_target_pairs={{0,16},{16,32},{32,48},{48,64},{64,80},{80,96},{96,112},{112,128},... | collective-permute-start | bytes 442376 | tf_op jit(solution)/shard_map/ppermute | solution.py:405
  67.5 10.7 %collective-permute-start = (f32[3,3,32,128]{3,2,1,0:T(8,128)S(1)}, f32[3,3,32,128]{3,2,1,0:T(8,128)S(1)}, u32[]{:S(2)}, u32[]{:S(2)}) collective-permute-start(f32[3,3,32,128]{3,2,1,0:T(8,128)S(1)} %rows.2.own), channel_id=1, source_target_pairs={{16,0},{32,16},{48,32},{64,48},{80,64},{96,80},{112,96},{128,112},... | collective-permute-start | bytes 442376 | tf_op jit(solution)/shard_map/ppermute | solution.py:405
  78.3 0.0 copy-done.6
  78.3 4.4 %free.1 = (f32[2,3,64,1024]{3,2,1,0:T(8,128)S(1)}, f32[2,3,64,1024]{3,2,1,0:T(8,128)}) custom-call(s32[2,192]{1,0:T(2,128)S(1)} %bitcast.5, f32[2,3,64,1024]{3,2,1,0:T(8,128)} %bitcast.8, f32[2,3,64,1024]{3,2,1,0:T(8,128)} %bitcast.9), custom_call_target="tpu_custom_call" | custom-call | flops 1000000000 | bytes 6291456 | tf_op jit(solution)/shard_map/free/pallas_call | solution.py:412
  82.7 0.0 collective-permute-done.1.down
  82.7 0.0 collective-permute-done.up
  82.7 1.1 force.2
  83.9 4.0 %all-to-all-done.3.mixed_two = f32[16,3,32,128]{3,2,1,0:T(8,128)S(1)} async-done(((f32[16,3,32,128]{3,2,1,0:T(8,128)}), f32[16,3,32,128]{3,2,1,0:T(8,128)S(1)}, u32[]{:S(2)}, u32[]{:S(2)}) %all-to-all-start.3) | async-done | bytes 786464 | tf_op jit(solution)/shard_map/all_to_all | solution.py:402
  87.8 0.0 copy-start
  87.8 26.1 %all_to_all.20.mixed_one = f32[16,3,32,128]{3,2,1,0:T(8,128)S(1)} all-to-all(f32[16,3,32,128]{3,2,1,0:T(8,128)S(1)} %force.2), channel_id=1, replica_groups=mesh['region'=32,'line'=16] {'line'}, dimensions={0} | all-to-all | bytes 1572864 | tf_op jit(solution)/shard_map/all_to_all | solution.py:402
  113.9 0.0 copy-done
  113.9 1.4 %update.1 = f32[2,3,64,1024]{3,2,1,0:T(8,128)} custom-call(f32[16,3,32,128]{3,2,1,0:T(8,128)S(1)} %all_to_all.20.mixed_one, f32[16,3,32,128]{3,2,1,0:T(8,128)S(1)} %all-to-all-done.3.mixed_two, f32[2,3,64,1024]{3,2,1,0:T(8,128)S(1)} %get-tuple-element.31.base, f32[2,3,64,1024]{3,2,1,0:T(8,128)S(1)} %copy-done), custom_call_target="tpu_custom_call" | custom-call | flops 10000000 | bytes 6291456 | tf_op jit(solution)/shard_map/update/pallas_call | solution.py:427
Async XLA Ops:
  2.4 33.0 %all-to-all-start.2 = ((f32[16,3,32,128]{3,2,1,0:T(8,128)}), f32[16,3,32,128]{3,2,1,0:T(8,128)S(1)}, u32[]{:S(2)}, u32[]{:S(2)}) async-start(f32[16,3,32,128]{3,2,1,0:T(8,128)} %encode.1), calls=%async_computation.2 | async-start | bytes 1572864 | tf_op jit(solution)/shard_map/all_to_all | solution.py:402
  17.1 21.8 %copy-start.1 = (f32[3,48,128]{2,1,0:T(8,128)S(1)}, f32[3,48,128]{2,1,0:T(8,128)}, u32[]{:S(2)}) copy-start(f32[3,48,128]{2,1,0:T(8,128)} %get-tuple-element.21.tables) | copy-start | bytes 221188
  17.1 21.8 %copy-start.4 = (bf16[3,64,128]{2,1,0:T(8,128)(2,1)S(1)}, bf16[3,64,128]{2,1,0:T(8,128)(2,1)}, u32[]{:S(2)}) copy-start(bf16[3,64,128]{2,1,0:T(8,128)(2,1)} %get-tuple-element.24.to_cells) | copy-start | bytes 147460
  17.1 38.8 %copy-start.2 = (bf16[3,64,128]{2,1,0:T(8,128)(2,1)S(1)}, bf16[3,64,128]{2,1,0:T(8,128)(2,1)}, u32[]{:S(2)}) copy-start(bf16[3,64,128]{2,1,0:T(8,128)(2,1)} %get-tuple-element.22.to_modes) | copy-start | bytes 147460
  17.1 38.8 %copy-start.3 = (f32[3,32,128]{2,1,0:T(8,128)S(1)}, f32[3,32,128]{2,1,0:T(8,128)}, u32[]{:S(2)}) copy-start(f32[3,32,128]{2,1,0:T(8,128)} %get-tuple-element.23.masks) | copy-start | bytes 147460
  17.1 38.7 %copy-start.5 = (s32[36]{0:T(128)S(1)}, s32[36]{0:T(128)}, u32[]{:S(2)}) copy-start(s32[36]{0:T(128)} %get-tuple-element.20.places) | copy-start | bytes 436
  35.4 25.8 %all-to-all-start = ((f32[16,3,32,128]{3,2,1,0:T(8,128)}), f32[16,3,32,128]{3,2,1,0:T(8,128)S(1)}, u32[]{:S(2)}, u32[]{:S(2)}) async-start(f32[16,3,32,128]{3,2,1,0:T(8,128)} %get-tuple-element.25), calls=%async_computation | async-start | bytes 1572864 | tf_op jit(solution)/shard_map/all_to_all | solution.py:402
  39.3 15.4 %collective-permute-start.3 = (f32[3,3,32,128]{3,2,1,0:T(8,128)S(1)}, f32[3,3,32,128]{3,2,1,0:T(8,128)S(1)}, u32[]{:S(2)}, u32[]{:S(2)}) collective-permute-start(f32[3,3,32,128]{3,2,1,0:T(8,128)S(1)} %rows.3.own), channel_id=1, source_target_pairs={{0,16},{16,32},{32,48},{48,64},{64,80},{80,96},{96,112},{112,128},... | collective-permute-start | bytes 442376 | tf_op jit(solution)/shard_map/ppermute | solution.py:405
  41.6 14.2 %collective-permute-start.2 = (f32[3,3,32,128]{3,2,1,0:T(8,128)S(1)}, f32[3,3,32,128]{3,2,1,0:T(8,128)S(1)}, u32[]{:S(2)}, u32[]{:S(2)}) collective-permute-start(f32[3,3,32,128]{3,2,1,0:T(8,128)S(1)} %rows.3.own), channel_id=1, source_target_pairs={{16,0},{32,16},{48,32},{64,48},{80,64},{96,80},{112,96},{128,112},... | collective-permute-start | bytes 442376 | tf_op jit(solution)/shard_map/ppermute | solution.py:405
  57.9 20.3 %copy-start.6 = (s32[192,2]{0,1:T(2,128)S(1)}, s32[192,2]{0,1:T(2,128)}, u32[]{:S(2)}) copy-start(s32[192,2]{0,1:T(2,128)} %param.7) | copy-start | bytes 4612
  61.2 26.6 %all-to-all-start.3 = ((f32[16,3,32,128]{3,2,1,0:T(8,128)}), f32[16,3,32,128]{3,2,1,0:T(8,128)S(1)}, u32[]{:S(2)}, u32[]{:S(2)}) async-start(f32[16,3,32,128]{3,2,1,0:T(8,128)} %force.3), calls=%async_computation.3 | async-start | bytes 1572864 | tf_op jit(solution)/shard_map/all_to_all | solution.py:402
  65.6 17.1 %collective-permute-start.1 = (f32[3,3,32,128]{3,2,1,0:T(8,128)S(1)}, f32[3,3,32,128]{3,2,1,0:T(8,128)S(1)}, u32[]{:S(2)}, u32[]{:S(2)}) collective-permute-start(f32[3,3,32,128]{3,2,1,0:T(8,128)S(1)} %rows.2.own), channel_id=1, source_target_pairs={{0,16},{16,32},{32,48},{48,64},{64,80},{80,96},{96,112},{112,128},... | collective-permute-start | bytes 442376 | tf_op jit(solution)/shard_map/ppermute | solution.py:405
  67.5 15.2 %collective-permute-start = (f32[3,3,32,128]{3,2,1,0:T(8,128)S(1)}, f32[3,3,32,128]{3,2,1,0:T(8,128)S(1)}, u32[]{:S(2)}, u32[]{:S(2)}) collective-permute-start(f32[3,3,32,128]{3,2,1,0:T(8,128)S(1)} %rows.2.own), channel_id=1, source_target_pairs={{16,0},{32,16},{48,32},{64,48},{80,64},{96,80},{112,96},{128,112},... | collective-permute-start | bytes 442376 | tf_op jit(solution)/shard_map/ppermute | solution.py:405
  87.8 26.1 %copy-start = (f32[2,3,64,1024]{3,2,1,0:T(8,128)S(1)}, f32[2,3,64,1024]{3,2,1,0:T(8,128)}, u32[]{:S(2)}) copy-start(f32[2,3,64,1024]{3,2,1,0:T(8,128)} %get-tuple-element.32.gain) | copy-start | bytes 4718596

commit v7 on v6

--- a/solution.py
+++ b/solution.py
@@ -190,20 +190,18 @@
 
 def free_kernel(extents, now_hbm, previous_hbm, base_hbm, gain_hbm, now, previous, base, gain, copied):
     inward, outward = [], []
-    for h in range(2):
-        inward.append(
-            (
-                pltpu.make_async_copy(now_hbm.at[h], now.at[h], copied.at[h, 0]),
-                pltpu.make_async_copy(previous_hbm.at[h], previous.at[h], copied.at[h, 1]),
-            )
+    for r in range(OWN):
+        h, pair = r // PAIRS, r % PAIRS
+        ends = (
+            (now_hbm.at[h, pair], now.at[h, pair]),
+            (previous_hbm.at[h, pair], previous.at[h, pair]),
+            (base.at[h, pair], base_hbm.at[h, pair]),
+            (gain.at[h, pair], gain_hbm.at[h, pair]),
         )
-        outward.append(
-            (
-                pltpu.make_async_copy(base.at[h], base_hbm.at[h], copied.at[h, 2]),
-                pltpu.make_async_copy(gain.at[h], gain_hbm.at[h], copied.at[h, 3]),
-            )
-        )
-        for copy in inward[h]:
+        copies = [pltpu.make_async_copy(*ends[i], copied.at[r, i]) for i in range(4)]
+        inward.append(copies[:2])
+        outward.append(copies[2:])
+        for copy in inward[r]:
             copy.start()
     first = lax.axis_index("region") * OWN
     line = lax.axis_index("line")
@@ -214,9 +212,8 @@
     quarter = (0.5 * math.pi) ** 2
     for r in range(OWN):
         h, pair = r // PAIRS, r % PAIRS
-        if pair == 0:
-            for copy in inward[h]:
-                copy.wait()
+        for copy in inward[r]:
+            copy.wait()
         live_y = live(extents, first + r, 0)
         live_z = live(extents, first + r, 1)
         y = freq_y / live_y
@@ -231,9 +228,8 @@
             stepped = (2.0 - u * s) * now[h, pair, :, lanes] - previous[h, pair, :, lanes]
             base[h, pair, :, lanes] = jnp.where(active, stepped, 0.0)
             gain[h, pair, :, lanes] = jnp.where(active, 0.25 * s, 0.0)
-        if pair == PAIRS - 1:
-            for copy in outward[h]:
-                copy.start()
+        for copy in outward[r]:
+            copy.start()
     for copies in outward:
         for copy in copies:
             copy.wait()
@@ -414,7 +410,7 @@
             out_shape=(wide_shape, wide_shape),
             in_specs=[smem(), hbm(), hbm()],
             out_specs=(hbm(), hbm()),
-            scratch_shapes=[pltpu.VMEM(now.shape, f32)] * 4 + [pltpu.SemaphoreType.DMA((2, 4))],
+            scratch_shapes=[pltpu.VMEM(now.shape, f32)] * 4 + [pltpu.SemaphoreType.DMA((OWN, 4))],
             compiler_params=pltpu.CompilerParams(vmem_limit_bytes=FREE_LIMIT),
             cost_estimate=cost(10**9, 4 * nbytes),
         )(extents, *lax.optimization_barrier((now, previous, rows_one))[:2])

time: 116 us -> 116 us (level)
  no operation moved by 1% of the time
where the time goes in v7:
time: 116 us; the launch traced here: 115 us
  starting transfers between devices  43.5 us (38%)
  waiting for transfers between devices  29.3 us (25%)
  blocking collectives  26 us (22%)
  Pallas kernels  16.4 us (14%)
    all_to_all x1, blocking collectives, exchange(): return lax.all_to_all(blocks, 'line', 0, 0, tiled=True)  26 us
    all_to_all x3, waiting for transfers between devices, exchange(): return lax.all_to_all(blocks, 'line', 0, 0, tiled=True)  25.8 us
    ppermute x2, starting transfers between devices, halo(): lax.ppermute(rows, 'region', upward)  21.5 us
    all_to_all x3, starting transfers between devices, exchange(): return lax.all_to_all(blocks, 'line', 0, 0, tiled=True)  17.8 us
    pallas_call x1, Pallas kernels, shards(): pl.pallas_call(encode_plan_kernel, out_shape=(packed_shape, jax.ShapeDtyp...  4.42 us
    ppermute x2, starting transfers between devices, halo(): lax.ppermute(rows, 'region', downward)  4.21 us
    pallas_call x1, Pallas kernels, shards(): pl.pallas_call(free_kernel, out_shape=(wide_shape, wide_shape), in_specs=...  4.1 us
    pallas_call x2, Pallas kernels, force(): pl.pallas_call(force_kernel, out_shape=packed_shape, in_specs=[smem()] +...  3.19 us
  transfers between devices with their start and end apart: 7, of which 5 were waited for; matrix products, arithmetic and copies ran while one was open for 0% of the time, Pallas kernels for 11%

profile of v7, /device:TPU:1, one launch (start us, length us, event | category | flops | bytes accessed | tf_op | source)
XLA Modules:
  0.0 115.3 jit_solution(276096937652085321)
XLA Ops:
  0.0 2.4 %encode.1 = f32[16,3,32,128]{3,2,1,0:T(8,128)} custom-call(f32[2,3,64,1024]{3,2,1,0:T(8,128)} %bitcast.6), custom_call_target="tpu_custom_call" | custom-call | flops 1000000 | bytes 3145728 | tf_op jit(solution)/shard_map/encode/pallas_call | solution.py:347
  2.4 10.3 %all-to-all-start.2 = ((f32[16,3,32,128]{3,2,1,0:T(8,128)}), f32[16,3,32,128]{3,2,1,0:T(8,128)S(1)}, u32[]{:S(2)}, u32[]{:S(2)}) async-start(f32[16,3,32,128]{3,2,1,0:T(8,128)} %encode.1), calls=%async_computation.2 | async-start | bytes 1572864 | tf_op jit(solution)/shard_map/all_to_all | solution.py:398
  12.7 4.4 %encode_plan.1 = (f32[16,3,32,128]{3,2,1,0:T(8,128)}, f32[3,48,128]{2,1,0:T(8,128)}, bf16[3,64,128]{2,1,0:T(8,128)(2,1)}, bf16[3,64,128]{2,1,0:T(8,128)(2,1)}, f32[3,32,128]{2,1,0:T(8,128)}, /*index=5*/s32[36]{0:T(128)}) custom-call(s32[2,192]{1,0:T(2,128)} %bitcast.4, s32[192]{0:T(256)} %partner.1, s32[192]{0:T(256)} %offset.1, f32[2,3,64,1024]{3,2,1,0:T(8,128)} %bitcast.7), custom_call_target="tpu_custom_call" | custom-call | flops 1000000 | bytes 3145728 | tf_op jit(solution)/shard_map/encode_plan/pallas_call | solution.py:357
  17.1 0.0 copy-start.1
  17.1 0.0 copy-start.4
  17.1 0.0 copy-start.2
  17.1 0.0 copy-start.3
  17.1 0.0 copy-start.5
  17.1 18.2 %all-to-all-done.2.modes = f32[16,3,32,128]{3,2,1,0:T(8,128)S(1)} async-done(((f32[16,3,32,128]{3,2,1,0:T(8,128)}), f32[16,3,32,128]{3,2,1,0:T(8,128)S(1)}, u32[]{:S(2)}, u32[]{:S(2)}) %all-to-all-start.2) | async-done | bytes 786464 | tf_op jit(solution)/shard_map/all_to_all | solution.py:398
  35.4 3.5 %all-to-all-start = ((f32[16,3,32,128]{3,2,1,0:T(8,128)}), f32[16,3,32,128]{3,2,1,0:T(8,128)S(1)}, u32[]{:S(2)}, u32[]{:S(2)}) async-start(f32[16,3,32,128]{3,2,1,0:T(8,128)} %get-tuple-element.25), calls=%async_computation | async-start | bytes 1572864 | tf_op jit(solution)/shard_map/all_to_all | solution.py:398
  38.9 0.0 copy-done.1
  38.9 0.0 copy-done.4
  38.9 0.4 rows.3.own
  39.3 2.3 %collective-permute-start.3 = (f32[3,3,32,128]{3,2,1,0:T(8,128)S(1)}, f32[3,3,32,128]{3,2,1,0:T(8,128)S(1)}, u32[]{:S(2)}, u32[]{:S(2)}) collective-permute-start(f32[3,3,32,128]{3,2,1,0:T(8,128)S(1)} %rows.3.own), channel_id=1, source_target_pairs={{0,16},{16,32},{32,48},{48,64},{64,80},{80,96},{96,112},{112,128},... | collective-permute-start | bytes 442376 | tf_op jit(solution)/shard_map/ppermute | solution.py:401
  41.6 10.8 %collective-permute-start.2 = (f32[3,3,32,128]{3,2,1,0:T(8,128)S(1)}, f32[3,3,32,128]{3,2,1,0:T(8,128)S(1)}, u32[]{:S(2)}, u32[]{:S(2)}) collective-permute-start(f32[3,3,32,128]{3,2,1,0:T(8,128)S(1)} %rows.3.own), channel_id=1, source_target_pairs={{16,0},{32,16},{48,32},{64,48},{80,64},{96,80},{112,96},{128,112},... | collective-permute-start | bytes 442376 | tf_op jit(solution)/shard_map/ppermute | solution.py:401
  52.4 2.3 %collective-permute-done.3.down = f32[3,3,32,128]{3,2,1,0:T(8,128)S(1)} collective-permute-done((f32[3,3,32,128]{3,2,1,0:T(8,128)S(1)}, f32[3,3,32,128]{3,2,1,0:T(8,128)S(1)}, u32[]{:S(2)}, u32[]{:S(2)}) %collective-permute-start.3) | collective-permute-done | bytes 147488 | tf_op jit(solution)/shard_map/ppermute | solution.py:401
  54.8 1.1 collective-permute-done.2.up
  55.9 0.0 copy-done.2
  55.9 0.0 copy-done.3
  55.9 0.0 copy-done.5
  55.9 2.0 %force.3 = f32[16,3,32,128]{3,2,1,0:T(8,128)} custom-call(s32[36]{0:T(128)S(1)} %copy-done.5, f32[3,48,128]{2,1,0:T(8,128)S(1)} %copy-done.1, bf16[3,64,128]{2,1,0:T(8,128)(2,1)S(1)} %copy-done.2, f32[3,32,128]{2,1,0:T(8,128)S(1)} %copy-done.3, f32[3,3,32,128]{3,2,1,0:T(8,128)S(1)} %rows.3.own, f32[3,3,32,128]{3,2,1,0:T(8,128)S(1)} %collective-permute-done.2.up, ...), custom_call_target="tpu_custom_call" | custom-call | flops 10000000 | bytes 1572864 | tf_op jit(solution)/shard_map/force/pallas_call | solution.py:387
  57.9 0.0 copy-start.6
  57.9 3.3 %all-to-all-done.modes = f32[16,3,32,128]{3,2,1,0:T(8,128)S(1)} async-done(((f32[16,3,32,128]{3,2,1,0:T(8,128)}), f32[16,3,32,128]{3,2,1,0:T(8,128)S(1)}, u32[]{:S(2)}, u32[]{:S(2)}) %all-to-all-start) | async-done | bytes 786464 | tf_op jit(solution)/shard_map/all_to_all | solution.py:398
  61.2 4.0 %all-to-all-start.3 = ((f32[16,3,32,128]{3,2,1,0:T(8,128)}), f32[16,3,32,128]{3,2,1,0:T(8,128)S(1)}, u32[]{:S(2)}, u32[]{:S(2)}) async-start(f32[16,3,32,128]{3,2,1,0:T(8,128)} %force.3), calls=%async_computation.3 | async-start | bytes 1572864 | tf_op jit(solution)/shard_map/all_to_all | solution.py:398
  65.2 0.4 rows.2.own
  65.6 1.9 %collective-permute-start.1 = (f32[3,3,32,128]{3,2,1,0:T(8,128)S(1)}, f32[3,3,32,128]{3,2,1,0:T(8,128)S(1)}, u32[]{:S(2)}, u32[]{:S(2)}) collective-permute-start(f32[3,3,32,128]{3,2,1,0:T(8,128)S(1)} %rows.2.own), channel_id=1, source_target_pairs={{0,16},{16,32},{32,48},{48,64},{64,80},{80,96},{96,112},{112,128},... | collective-permute-start | bytes 442376 | tf_op jit(solution)/shard_map/ppermute | solution.py:401
  67.5 10.7 %collective-permute-start = (f32[3,3,32,128]{3,2,1,0:T(8,128)S(1)}, f32[3,3,32,128]{3,2,1,0:T(8,128)S(1)}, u32[]{:S(2)}, u32[]{:S(2)}) collective-permute-start(f32[3,3,32,128]{3,2,1,0:T(8,128)S(1)} %rows.2.own), channel_id=1, source_target_pairs={{16,0},{32,16},{48,32},{64,48},{80,64},{96,80},{112,96},{128,112},... | collective-permute-start | bytes 442376 | tf_op jit(solution)/shard_map/ppermute | solution.py:401
  78.3 0.0 copy-done.6
  78.3 4.1 %free.1 = (f32[2,3,64,1024]{3,2,1,0:T(8,128)S(1)}, f32[2,3,64,1024]{3,2,1,0:T(8,128)}) custom-call(s32[2,192]{1,0:T(2,128)S(1)} %bitcast.5, f32[2,3,64,1024]{3,2,1,0:T(8,128)} %bitcast.8, f32[2,3,64,1024]{3,2,1,0:T(8,128)} %bitcast.9), custom_call_target="tpu_custom_call" | custom-call | flops 1000000000 | bytes 6291456 | tf_op jit(solution)/shard_map/free/pallas_call | solution.py:408
  82.4 0.0 collective-permute-done.1.down
  82.4 0.0 collective-permute-done.up
  82.4 1.1 force.2
  83.5 4.3 %all-to-all-done.3.mixed_two = f32[16,3,32,128]{3,2,1,0:T(8,128)S(1)} async-done(((f32[16,3,32,128]{3,2,1,0:T(8,128)}), f32[16,3,32,128]{3,2,1,0:T(8,128)S(1)}, u32[]{:S(2)}, u32[]{:S(2)}) %all-to-all-start.3) | async-done | bytes 786464 | tf_op jit(solution)/shard_map/all_to_all | solution.py:398
  87.8 0.0 copy-start
  87.8 26.0 %all_to_all.20.mixed_one = f32[16,3,32,128]{3,2,1,0:T(8,128)S(1)} all-to-all(f32[16,3,32,128]{3,2,1,0:T(8,128)S(1)} %force.2), channel_id=1, replica_groups=mesh['region'=32,'line'=16] {'line'}, dimensions={0} | all-to-all | bytes 1572864 | tf_op jit(solution)/shard_map/all_to_all | solution.py:398
  113.9 0.0 copy-done
  113.9 1.4 %update.1 = f32[2,3,64,1024]{3,2,1,0:T(8,128)} custom-call(f32[16,3,32,128]{3,2,1,0:T(8,128)S(1)} %all_to_all.20.mixed_one, f32[16,3,32,128]{3,2,1,0:T(8,128)S(1)} %all-to-all-done.3.mixed_two, f32[2,3,64,1024]{3,2,1,0:T(8,128)S(1)} %get-tuple-element.31.base, f32[2,3,64,1024]{3,2,1,0:T(8,128)S(1)} %copy-done), custom_call_target="tpu_custom_call" | custom-call | flops 10000000 | bytes 6291456 | tf_op jit(solution)/shard_map/update/pallas_call | solution.py:423
Async XLA Ops:
  2.4 33.0 %all-to-all-start.2 = ((f32[16,3,32,128]{3,2,1,0:T(8,128)}), f32[16,3,32,128]{3,2,1,0:T(8,128)S(1)}, u32[]{:S(2)}, u32[]{:S(2)}) async-start(f32[16,3,32,128]{3,2,1,0:T(8,128)} %encode.1), calls=%async_computation.2 | async-start | bytes 1572864 | tf_op jit(solution)/shard_map/all_to_all | solution.py:398
  17.1 21.8 %copy-start.1 = (f32[3,48,128]{2,1,0:T(8,128)S(1)}, f32[3,48,128]{2,1,0:T(8,128)}, u32[]{:S(2)}) copy-start(f32[3,48,128]{2,1,0:T(8,128)} %get-tuple-element.21.tables) | copy-start | bytes 221188
  17.1 21.8 %copy-start.4 = (bf16[3,64,128]{2,1,0:T(8,128)(2,1)S(1)}, bf16[3,64,128]{2,1,0:T(8,128)(2,1)}, u32[]{:S(2)}) copy-start(bf16[3,64,128]{2,1,0:T(8,128)(2,1)} %get-tuple-element.24.to_cells) | copy-start | bytes 147460
  17.1 38.8 %copy-start.2 = (bf16[3,64,128]{2,1,0:T(8,128)(2,1)S(1)}, bf16[3,64,128]{2,1,0:T(8,128)(2,1)}, u32[]{:S(2)}) copy-start(bf16[3,64,128]{2,1,0:T(8,128)(2,1)} %get-tuple-element.22.to_modes) | copy-start | bytes 147460
  17.1 38.8 %copy-start.3 = (f32[3,32,128]{2,1,0:T(8,128)S(1)}, f32[3,32,128]{2,1,0:T(8,128)}, u32[]{:S(2)}) copy-start(f32[3,32,128]{2,1,0:T(8,128)} %get-tuple-element.23.masks) | copy-start | bytes 147460
  17.1 38.7 %copy-start.5 = (s32[36]{0:T(128)S(1)}, s32[36]{0:T(128)}, u32[]{:S(2)}) copy-start(s32[36]{0:T(128)} %get-tuple-element.20.places) | copy-start | bytes 436
  35.4 25.8 %all-to-all-start = ((f32[16,3,32,128]{3,2,1,0:T(8,128)}), f32[16,3,32,128]{3,2,1,0:T(8,128)S(1)}, u32[]{:S(2)}, u32[]{:S(2)}) async-start(f32[16,3,32,128]{3,2,1,0:T(8,128)} %get-tuple-element.25), calls=%async_computation | async-start | bytes 1572864 | tf_op jit(solution)/shard_map/all_to_all | solution.py:398
  39.3 15.4 %collective-permute-start.3 = (f32[3,3,32,128]{3,2,1,0:T(8,128)S(1)}, f32[3,3,32,128]{3,2,1,0:T(8,128)S(1)}, u32[]{:S(2)}, u32[]{:S(2)}) collective-permute-start(f32[3,3,32,128]{3,2,1,0:T(8,128)S(1)} %rows.3.own), channel_id=1, source_target_pairs={{0,16},{16,32},{32,48},{48,64},{64,80},{80,96},{96,112},{112,128},... | collective-permute-start | bytes 442376 | tf_op jit(solution)/shard_map/ppermute | solution.py:401
  41.6 14.2 %collective-permute-start.2 = (f32[3,3,32,128]{3,2,1,0:T(8,128)S(1)}, f32[3,3,32,128]{3,2,1,0:T(8,128)S(1)}, u32[]{:S(2)}, u32[]{:S(2)}) collective-permute-start(f32[3,3,32,128]{3,2,1,0:T(8,128)S(1)} %rows.3.own), channel_id=1, source_target_pairs={{16,0},{32,16},{48,32},{64,48},{80,64},{96,80},{112,96},{128,112},... | collective-permute-start | bytes 442376 | tf_op jit(solution)/shard_map/ppermute | solution.py:401
  57.9 20.3 %copy-start.6 = (s32[192,2]{0,1:T(2,128)S(1)}, s32[192,2]{0,1:T(2,128)}, u32[]{:S(2)}) copy-start(s32[192,2]{0,1:T(2,128)} %param.7) | copy-start | bytes 4612
  61.2 26.6 %all-to-all-start.3 = ((f32[16,3,32,128]{3,2,1,0:T(8,128)}), f32[16,3,32,128]{3,2,1,0:T(8,128)S(1)}, u32[]{:S(2)}, u32[]{:S(2)}) async-start(f32[16,3,32,128]{3,2,1,0:T(8,128)} %force.3), calls=%async_computation.3 | async-start | bytes 1572864 | tf_op jit(solution)/shard_map/all_to_all | solution.py:398
  65.6 16.8 %collective-permute-start.1 = (f32[3,3,32,128]{3,2,1,0:T(8,128)S(1)}, f32[3,3,32,128]{3,2,1,0:T(8,128)S(1)}, u32[]{:S(2)}, u32[]{:S(2)}) collective-permute-start(f32[3,3,32,128]{3,2,1,0:T(8,128)S(1)} %rows.2.own), channel_id=1, source_target_pairs={{0,16},{16,32},{32,48},{48,64},{64,80},{80,96},{96,112},{112,128},... | collective-permute-start | bytes 442376 | tf_op jit(solution)/shard_map/ppermute | solution.py:401
  67.5 14.8 %collective-permute-start = (f32[3,3,32,128]{3,2,1,0:T(8,128)S(1)}, f32[3,3,32,128]{3,2,1,0:T(8,128)S(1)}, u32[]{:S(2)}, u32[]{:S(2)}) collective-permute-start(f32[3,3,32,128]{3,2,1,0:T(8,128)S(1)} %rows.2.own), channel_id=1, source_target_pairs={{16,0},{32,16},{48,32},{64,48},{80,64},{96,80},{112,96},{128,112},... | collective-permute-start | bytes 442376 | tf_op jit(solution)/shard_map/ppermute | solution.py:401
  87.8 26.0 %copy-start = (f32[2,3,64,1024]{3,2,1,0:T(8,128)S(1)}, f32[2,3,64,1024]{3,2,1,0:T(8,128)}, u32[]{:S(2)}) copy-start(f32[2,3,64,1024]{3,2,1,0:T(8,128)} %get-tuple-element.32.gain) | copy-start | bytes 4718596

commit v8 on v7

--- a/solution.py
+++ b/solution.py
@@ -297,8 +297,16 @@
                         base[h, pair, modes, lanes]
                         + gain[h, pair, modes, lanes] * tiles[2 * parity + h]
                     )
-        copies.append(pltpu.make_async_copy(made.at[pair], out.at[:, pair], sent.at[pair]))
-        copies[-1].start()
+            if chip % 2 == 1:
+                columns = pl.ds((chip - 1) * LANES, 2 * LANES)
+                copies.append(
+                    pltpu.make_async_copy(
+                        made.at[pair, :, :, columns],
+                        out.at[:, pair, :, columns],
+                        sent.at[pair, chip // 2],
+                    )
+                )
+                copies[-1].start()
     for copy in copies:
         copy.wait()
 
@@ -425,7 +433,7 @@
             out_shape=wide_shape,
             in_specs=[vmem()] * 4,
             out_specs=hbm(),
-            scratch_shapes=[wide_scratch, copied],
+            scratch_shapes=[wide_scratch, pltpu.SemaphoreType.DMA((PAIRS, 4))],
             compiler_params=params,
             cost_estimate=cost(10**7, 4 * nbytes),
         )(mixed_one, mixed_two, base, gain)

time: 116 us -> 117 us (level)
  no operation moved by 1% of the time
where the time goes in v8:
time: 117 us; the launch traced here: 116 us
  starting transfers between devices  43.5 us (37%)
  waiting for transfers between devices  29.3 us (25%)
  blocking collectives  26 us (22%)
  Pallas kernels  17 us (15%)
    all_to_all x1, blocking collectives, exchange(): return lax.all_to_all(blocks, 'line', 0, 0, tiled=True)  26 us
    all_to_all x3, waiting for transfers between devices, exchange(): return lax.all_to_all(blocks, 'line', 0, 0, tiled=True)  25.8 us
    ppermute x2, starting transfers between devices, halo(): lax.ppermute(rows, 'region', upward)  21.5 us
    all_to_all x3, starting transfers between devices, exchange(): return lax.all_to_all(blocks, 'line', 0, 0, tiled=True)  17.8 us
    pallas_call x1, Pallas kernels, shards(): pl.pallas_call(encode_plan_kernel, out_shape=(packed_shape, jax.ShapeDtyp...  4.42 us
    ppermute x2, starting transfers between devices, halo(): lax.ppermute(rows, 'region', downward)  4.21 us
    pallas_call x1, Pallas kernels, shards(): pl.pallas_call(free_kernel, out_shape=(wide_shape, wide_shape), in_specs=...  4.1 us
    pallas_call x2, Pallas kernels, force(): pl.pallas_call(force_kernel, out_shape=packed_shape, in_specs=[smem()] +...  3.19 us
  transfers between devices with their start and end apart: 7, of which 5 were waited for; matrix products, arithmetic and copies ran while one was open for 0% of the time, Pallas kernels for 11%

profile of v8, /device:TPU:1, one launch (start us, length us, event | category | flops | bytes accessed | tf_op | source)
XLA Modules:
  0.0 116.0 jit_solution(6679239324670660649)
XLA Ops:
  0.0 2.4 %encode.1 = f32[16,3,32,128]{3,2,1,0:T(8,128)} custom-call(f32[2,3,64,1024]{3,2,1,0:T(8,128)} %bitcast.6), custom_call_target="tpu_custom_call" | custom-call | flops 1000000 | bytes 3145728 | tf_op jit(solution)/shard_map/encode/pallas_call | solution.py:355
  2.4 10.3 %all-to-all-start.2 = ((f32[16,3,32,128]{3,2,1,0:T(8,128)}), f32[16,3,32,128]{3,2,1,0:T(8,128)S(1)}, u32[]{:S(2)}, u32[]{:S(2)}) async-start(f32[16,3,32,128]{3,2,1,0:T(8,128)} %encode.1), calls=%async_computation.2 | async-start | bytes 1572864 | tf_op jit(solution)/shard_map/all_to_all | solution.py:406
  12.7 4.4 %encode_plan.1 = (f32[16,3,32,128]{3,2,1,0:T(8,128)}, f32[3,48,128]{2,1,0:T(8,128)}, bf16[3,64,128]{2,1,0:T(8,128)(2,1)}, bf16[3,64,128]{2,1,0:T(8,128)(2,1)}, f32[3,32,128]{2,1,0:T(8,128)}, /*index=5*/s32[36]{0:T(128)}) custom-call(s32[2,192]{1,0:T(2,128)} %bitcast.4, s32[192]{0:T(256)} %partner.1, s32[192]{0:T(256)} %offset.1, f32[2,3,64,1024]{3,2,1,0:T(8,128)} %bitcast.7), custom_call_target="tpu_custom_call" | custom-call | flops 1000000 | bytes 3145728 | tf_op jit(solution)/shard_map/encode_plan/pallas_call | solution.py:365
  17.1 0.0 copy-start.1
  17.1 0.0 copy-start.4
  17.1 0.0 copy-start.2
  17.1 0.0 copy-start.3
  17.1 0.0 copy-start.5
  17.1 18.2 %all-to-all-done.2.modes = f32[16,3,32,128]{3,2,1,0:T(8,128)S(1)} async-done(((f32[16,3,32,128]{3,2,1,0:T(8,128)}), f32[16,3,32,128]{3,2,1,0:T(8,128)S(1)}, u32[]{:S(2)}, u32[]{:S(2)}) %all-to-all-start.2) | async-done | bytes 786464 | tf_op jit(solution)/shard_map/all_to_all | solution.py:406
  35.4 3.5 %all-to-all-start = ((f32[16,3,32,128]{3,2,1,0:T(8,128)}), f32[16,3,32,128]{3,2,1,0:T(8,128)S(1)}, u32[]{:S(2)}, u32[]{:S(2)}) async-start(f32[16,3,32,128]{3,2,1,0:T(8,128)} %get-tuple-element.25), calls=%async_computation | async-start | bytes 1572864 | tf_op jit(solution)/shard_map/all_to_all | solution.py:406
  38.9 0.0 copy-done.1
  38.9 0.0 copy-done.4
  38.9 0.4 rows.3.own
  39.3 2.3 %collective-permute-start.3 = (f32[3,3,32,128]{3,2,1,0:T(8,128)S(1)}, f32[3,3,32,128]{3,2,1,0:T(8,128)S(1)}, u32[]{:S(2)}, u32[]{:S(2)}) collective-permute-start(f32[3,3,32,128]{3,2,1,0:T(8,128)S(1)} %rows.3.own), channel_id=1, source_target_pairs={{0,16},{16,32},{32,48},{48,64},{64,80},{80,96},{96,112},{112,128},... | collective-permute-start | bytes 442376 | tf_op jit(solution)/shard_map/ppermute | solution.py:409
  41.6 10.8 %collective-permute-start.2 = (f32[3,3,32,128]{3,2,1,0:T(8,128)S(1)}, f32[3,3,32,128]{3,2,1,0:T(8,128)S(1)}, u32[]{:S(2)}, u32[]{:S(2)}) collective-permute-start(f32[3,3,32,128]{3,2,1,0:T(8,128)S(1)} %rows.3.own), channel_id=1, source_target_pairs={{16,0},{32,16},{48,32},{64,48},{80,64},{96,80},{112,96},{128,112},... | collective-permute-start | bytes 442376 | tf_op jit(solution)/shard_map/ppermute | solution.py:409
  52.4 2.3 %collective-permute-done.3.down = f32[3,3,32,128]{3,2,1,0:T(8,128)S(1)} collective-permute-done((f32[3,3,32,128]{3,2,1,0:T(8,128)S(1)}, f32[3,3,32,128]{3,2,1,0:T(8,128)S(1)}, u32[]{:S(2)}, u32[]{:S(2)}) %collective-permute-start.3) | collective-permute-done | bytes 147488 | tf_op jit(solution)/shard_map/ppermute | solution.py:409
  54.8 1.1 collective-permute-done.2.up
  55.9 0.0 copy-done.2
  55.9 0.0 copy-done.3
  55.9 0.0 copy-done.5
  55.9 2.0 %force.3 = f32[16,3,32,128]{3,2,1,0:T(8,128)} custom-call(s32[36]{0:T(128)S(1)} %copy-done.5, f32[3,48,128]{2,1,0:T(8,128)S(1)} %copy-done.1, bf16[3,64,128]{2,1,0:T(8,128)(2,1)S(1)} %copy-done.2, f32[3,32,128]{2,1,0:T(8,128)S(1)} %copy-done.3, f32[3,3,32,128]{3,2,1,0:T(8,128)S(1)} %rows.3.own, f32[3,3,32,128]{3,2,1,0:T(8,128)S(1)} %collective-permute-done.2.up, ...), custom_call_target="tpu_custom_call" | custom-call | flops 10000000 | bytes 1572864 | tf_op jit(solution)/shard_map/force/pallas_call | solution.py:395
  57.9 0.0 copy-start.6
  57.9 3.3 %all-to-all-done.modes = f32[16,3,32,128]{3,2,1,0:T(8,128)S(1)} async-done(((f32[16,3,32,128]{3,2,1,0:T(8,128)}), f32[16,3,32,128]{3,2,1,0:T(8,128)S(1)}, u32[]{:S(2)}, u32[]{:S(2)}) %all-to-all-start) | async-done | bytes 786464 | tf_op jit(solution)/shard_map/all_to_all | solution.py:406
  61.2 4.0 %all-to-all-start.3 = ((f32[16,3,32,128]{3,2,1,0:T(8,128)}), f32[16,3,32,128]{3,2,1,0:T(8,128)S(1)}, u32[]{:S(2)}, u32[]{:S(2)}) async-start(f32[16,3,32,128]{3,2,1,0:T(8,128)} %force.3), calls=%async_computation.3 | async-start | bytes 1572864 | tf_op jit(solution)/shard_map/all_to_all | solution.py:406
  65.2 0.4 rows.2.own
  65.6 1.9 %collective-permute-start.1 = (f32[3,3,32,128]{3,2,1,0:T(8,128)S(1)}, f32[3,3,32,128]{3,2,1,0:T(8,128)S(1)}, u32[]{:S(2)}, u32[]{:S(2)}) collective-permute-start(f32[3,3,32,128]{3,2,1,0:T(8,128)S(1)} %rows.2.own), channel_id=1, source_target_pairs={{0,16},{16,32},{32,48},{48,64},{64,80},{80,96},{96,112},{112,128},... | collective-permute-start | bytes 442376 | tf_op jit(solution)/shard_map/ppermute | solution.py:409
  67.5 10.7 %collective-permute-start = (f32[3,3,32,128]{3,2,1,0:T(8,128)S(1)}, f32[3,3,32,128]{3,2,1,0:T(8,128)S(1)}, u32[]{:S(2)}, u32[]{:S(2)}) collective-permute-start(f32[3,3,32,128]{3,2,1,0:T(8,128)S(1)} %rows.2.own), channel_id=1, source_target_pairs={{16,0},{32,16},{48,32},{64,48},{80,64},{96,80},{112,96},{128,112},... | collective-permute-start | bytes 442376 | tf_op jit(solution)/shard_map/ppermute | solution.py:409
  78.3 0.0 copy-done.6
  78.3 4.1 %free.1 = (f32[2,3,64,1024]{3,2,1,0:T(8,128)S(1)}, f32[2,3,64,1024]{3,2,1,0:T(8,128)}) custom-call(s32[2,192]{1,0:T(2,128)S(1)} %bitcast.5, f32[2,3,64,1024]{3,2,1,0:T(8,128)} %bitcast.8, f32[2,3,64,1024]{3,2,1,0:T(8,128)} %bitcast.9), custom_call_target="tpu_custom_call" | custom-call | flops 1000000000 | bytes 6291456 | tf_op jit(solution)/shard_map/free/pallas_call | solution.py:416
  82.4 0.0 collective-permute-done.1.down
  82.4 0.0 collective-permute-done.up
  82.4 1.1 force.2
  83.5 4.3 %all-to-all-done.3.mixed_two = f32[16,3,32,128]{3,2,1,0:T(8,128)S(1)} async-done(((f32[16,3,32,128]{3,2,1,0:T(8,128)}), f32[16,3,32,128]{3,2,1,0:T(8,128)S(1)}, u32[]{:S(2)}, u32[]{:S(2)}) %all-to-all-start.3) | async-done | bytes 786464 | tf_op jit(solution)/shard_map/all_to_all | solution.py:406
  87.8 0.0 copy-start
  87.8 26.0 %all_to_all.20.mixed_one = f32[16,3,32,128]{3,2,1,0:T(8,128)S(1)} all-to-all(f32[16,3,32,128]{3,2,1,0:T(8,128)S(1)} %force.2), channel_id=1, replica_groups=mesh['region'=32,'line'=16] {'line'}, dimensions={0} | all-to-all | bytes 1572864 | tf_op jit(solution)/shard_map/all_to_all | solution.py:406
  113.9 0.0 copy-done
  113.9 2.1 %update.1 = f32[2,3,64,1024]{3,2,1,0:T(8,128)} custom-call(f32[16,3,32,128]{3,2,1,0:T(8,128)S(1)} %all_to_all.20.mixed_one, f32[16,3,32,128]{3,2,1,0:T(8,128)S(1)} %all-to-all-done.3.mixed_two, f32[2,3,64,1024]{3,2,1,0:T(8,128)S(1)} %get-tuple-element.31.base, f32[2,3,64,1024]{3,2,1,0:T(8,128)S(1)} %copy-done), custom_call_target="tpu_custom_call" | custom-call | flops 10000000 | bytes 6291456 | tf_op jit(solution)/shard_map/update/pallas_call | solution.py:431
Async XLA Ops:
  2.4 33.0 %all-to-all-start.2 = ((f32[16,3,32,128]{3,2,1,0:T(8,128)}), f32[16,3,32,128]{3,2,1,0:T(8,128)S(1)}, u32[]{:S(2)}, u32[]{:S(2)}) async-start(f32[16,3,32,128]{3,2,1,0:T(8,128)} %encode.1), calls=%async_computation.2 | async-start | bytes 1572864 | tf_op jit(solution)/shard_map/all_to_all | solution.py:406
  17.1 21.8 %copy-start.1 = (f32[3,48,128]{2,1,0:T(8,128)S(1)}, f32[3,48,128]{2,1,0:T(8,128)}, u32[]{:S(2)}) copy-start(f32[3,48,128]{2,1,0:T(8,128)} %get-tuple-element.21.tables) | copy-start | bytes 221188
  17.1 21.8 %copy-start.4 = (bf16[3,64,128]{2,1,0:T(8,128)(2,1)S(1)}, bf16[3,64,128]{2,1,0:T(8,128)(2,1)}, u32[]{:S(2)}) copy-start(bf16[3,64,128]{2,1,0:T(8,128)(2,1)} %get-tuple-element.24.to_cells) | copy-start | bytes 147460
  17.1 38.8 %copy-start.2 = (bf16[3,64,128]{2,1,0:T(8,128)(2,1)S(1)}, bf16[3,64,128]{2,1,0:T(8,128)(2,1)}, u32[]{:S(2)}) copy-start(bf16[3,64,128]{2,1,0:T(8,128)(2,1)} %get-tuple-element.22.to_modes) | copy-start | bytes 147460
  17.1 38.8 %copy-start.3 = (f32[3,32,128]{2,1,0:T(8,128)S(1)}, f32[3,32,128]{2,1,0:T(8,128)}, u32[]{:S(2)}) copy-start(f32[3,32,128]{2,1,0:T(8,128)} %get-tuple-element.23.masks) | copy-start | bytes 147460
  17.1 38.7 %copy-start.5 = (s32[36]{0:T(128)S(1)}, s32[36]{0:T(128)}, u32[]{:S(2)}) copy-start(s32[36]{0:T(128)} %get-tuple-element.20.places) | copy-start | bytes 436
  35.4 25.8 %all-to-all-start = ((f32[16,3,32,128]{3,2,1,0:T(8,128)}), f32[16,3,32,128]{3,2,1,0:T(8,128)S(1)}, u32[]{:S(2)}, u32[]{:S(2)}) async-start(f32[16,3,32,128]{3,2,1,0:T(8,128)} %get-tuple-element.25), calls=%async_computation | async-start | bytes 1572864 | tf_op jit(solution)/shard_map/all_to_all | solution.py:406
  39.3 15.4 %collective-permute-start.3 = (f32[3,3,32,128]{3,2,1,0:T(8,128)S(1)}, f32[3,3,32,128]{3,2,1,0:T(8,128)S(1)}, u32[]{:S(2)}, u32[]{:S(2)}) collective-permute-start(f32[3,3,32,128]{3,2,1,0:T(8,128)S(1)} %rows.3.own), channel_id=1, source_target_pairs={{0,16},{16,32},{32,48},{48,64},{64,80},{80,96},{96,112},{112,128},... | collective-permute-start | bytes 442376 | tf_op jit(solution)/shard_map/ppermute | solution.py:409
  41.6 14.2 %collective-permute-start.2 = (f32[3,3,32,128]{3,2,1,0:T(8,128)S(1)}, f32[3,3,32,128]{3,2,1,0:T(8,128)S(1)}, u32[]{:S(2)}, u32[]{:S(2)}) collective-permute-start(f32[3,3,32,128]{3,2,1,0:T(8,128)S(1)} %rows.3.own), channel_id=1, source_target_pairs={{16,0},{32,16},{48,32},{64,48},{80,64},{96,80},{112,96},{128,112},... | collective-permute-start | bytes 442376 | tf_op jit(solution)/shard_map/ppermute | solution.py:409
  57.9 20.3 %copy-start.6 = (s32[192,2]{0,1:T(2,128)S(1)}, s32[192,2]{0,1:T(2,128)}, u32[]{:S(2)}) copy-start(s32[192,2]{0,1:T(2,128)} %param.7) | copy-start | bytes 4612
  61.2 26.6 %all-to-all-start.3 = ((f32[16,3,32,128]{3,2,1,0:T(8,128)}), f32[16,3,32,128]{3,2,1,0:T(8,128)S(1)}, u32[]{:S(2)}, u32[]{:S(2)}) async-start(f32[16,3,32,128]{3,2,1,0:T(8,128)} %force.3), calls=%async_computation.3 | async-start | bytes 1572864 | tf_op jit(solution)/shard_map/all_to_all | solution.py:406
  65.6 16.8 %collective-permute-start.1 = (f32[3,3,32,128]{3,2,1,0:T(8,128)S(1)}, f32[3,3,32,128]{3,2,1,0:T(8,128)S(1)}, u32[]{:S(2)}, u32[]{:S(2)}) collective-permute-start(f32[3,3,32,128]{3,2,1,0:T(8,128)S(1)} %rows.2.own), channel_id=1, source_target_pairs={{0,16},{16,32},{32,48},{48,64},{64,80},{80,96},{96,112},{112,128},... | collective-permute-start | bytes 442376 | tf_op jit(solution)/shard_map/ppermute | solution.py:409
  67.5 14.8 %collective-permute-start = (f32[3,3,32,128]{3,2,1,0:T(8,128)S(1)}, f32[3,3,32,128]{3,2,1,0:T(8,128)S(1)}, u32[]{:S(2)}, u32[]{:S(2)}) collective-permute-start(f32[3,3,32,128]{3,2,1,0:T(8,128)S(1)} %rows.2.own), channel_id=1, source_target_pairs={{16,0},{32,16},{48,32},{64,48},{80,64},{96,80},{112,96},{128,112},... | collective-permute-start | bytes 442376 | tf_op jit(solution)/shard_map/ppermute | solution.py:409
  87.8 26.0 %copy-start = (f32[2,3,64,1024]{3,2,1,0:T(8,128)S(1)}, f32[2,3,64,1024]{3,2,1,0:T(8,128)}, u32[]{:S(2)}) copy-start(f32[2,3,64,1024]{3,2,1,0:T(8,128)} %get-tuple-element.32.gain) | copy-start | bytes 4718596
